TPU v7x, 256 devices: a whole 4x4x8 slice. The times are simulated.
256 devices in a mesh: sample: 2 (over core), depth: 128 (over x, y, z).
Axes of the slice: x: 4, y: 4, z: 8, core: 2. Of those that a mesh axis runs over, the one named last changes fastest.
Arguments:
- volumes: bfloat16 [2, 4, 256, 32, 256], P('sample', None, 'depth'), may hold values from -6 to 6
- conv_one: bfloat16 [3, 3, 3, 4, 16], replicated, may hold values from -0.625 to 0.625
- bias_one: float32 [16], replicated, may hold values from -3 to 3
- conv_two: bfloat16 [3, 3, 3, 16, 32], replicated, may hold values from -0.3125 to 0.3125
- bias_two: float32 [32], replicated, may hold values from -3 to 3
- cotangent: bfloat16 [2, 32, 128, 16, 128], P('sample', None, 'depth'), may hold values from -0.008239746 to 0.008239746
Outputs:
- activations: bfloat16 [2, 32, 128, 16, 128], P('sample', None, 'depth')
- grad_conv_one: float32 [3, 3, 3, 4, 16], replicated
- grad_bias_one: float32 [16], replicated
- grad_conv_two: float32 [3, 3, 3, 16, 32], replicated
- grad_bias_two: float32 [32], replicated
All inputs are finite; a program needn't handle non-finite values.
Results may differ from a plain program's by a relative error of at most 0.0095.
Values may be sent and summed in bfloat16 or wider, within the bound.
No kernel may reach another device: no remote copies, remote signals or barrier semaphores. Data moves between devices by JAX's collectives and lax.ppermute only.
A program may use at most 128 MiB of HBM per device.

v0:
```python
import functools

import jax
import jax.numpy as jnp
from jax import lax
from jax.experimental import pallas as pl
from jax.experimental.pallas import tpu as pltpu
from jax.sharding import Mesh, PartitionSpec as P

BF = jnp.bfloat16
F32 = jnp.float32
ROWS = 16
LANES = 128
CELLS = ROWS * LANES
VMEM_LIMIT = 40 * 1024 * 1024


def iota(shape, dim):
    return lax.broadcasted_iota(jnp.int32, shape, dim)


def dot(a, b, ca=1, cb=0):
    return lax.dot_general(a, b, (((ca,), (cb,)), ((), ())), preferred_element_type=F32)


def flag(mask):
    return jnp.where(mask, 1.0, 0.0).astype(BF)


def smooth(z):
    return 0.3 * z + 0.7 * (jnp.maximum(z, 0.0) + jnp.log(1.0 + jnp.exp(-jnp.abs(z))))


def slope_of(z):
    return 0.65 + 0.35 * jnp.tanh(0.5 * z)


def from_left(x):
    return jnp.where(iota(x.shape, 1) == 0, 0.0, pltpu.roll(x, 1, 1))


def from_right(x):
    return jnp.where(iota(x.shape, 1) == LANES - 1, 0.0, pltpu.roll(x, LANES - 1, 1))


def tile(h):
    return slice(h * LANES, (h + 1) * LANES)


def first_kernel(vol_ref, lo_ref, hi_ref, w_ref, b_ref, patches_ref, slope_ref, pooled_ref):
    cols = iota((256, 512), 1)
    pick_cols = flag(iota((256, 512), 0) == 2 * (cols & 127) + (cols >> 7) - 1)
    rows = iota((256, 128), 0)
    src = iota((256, 128), 1)
    pick_rows = flag(((rows & 3) == (src >> 5)) & ((src & 31) == 2 * (rows >> 4) + ((rows >> 2) & 3) - 1))
    planes = [
        lo_ref[...].reshape(128, 256),
        vol_ref[:, 0].reshape(128, 256),
        vol_ref[:, 1].reshape(128, 256),
        hi_ref[...].reshape(128, 256),
    ]
    for a in range(4):
        wide = dot(planes[a], pick_cols).astype(BF)
        both = dot(pick_rows, wide).astype(BF)
        for e in range(4):
            k = (a * 4 + e) * 16
            for h in range(ROWS):
                patches_ref[k : k + 16, tile(h)] = both[h * 16 : (h + 1) * 16, tile(e)]
    base = w_ref[...]
    weights = jnp.concatenate(
        [
            base if i == 0 else pltpu.roll(base, (i >> 2) * 64 + (i & 1) * 16 + ((i >> 1) & 1) * 4, 1)
            for i in range(8)
        ],
        axis=0,
    ).astype(BF)
    bias = b_ref[...]
    for n in range(8):
        span = slice(n * 256, (n + 1) * 256)
        pre = dot(weights, patches_ref[:, span])
        total = None
        for i in range(8):
            z = pre[i * 16 : (i + 1) * 16] + bias
            slope_ref[i * 16 : (i + 1) * 16, span] = slope_of(z)
            value = smooth(z)
            total = value if total is None else total + value
        pooled_ref[:, span] = (total * 0.125).astype(BF)


def second_kernel(mid_ref, lo_ref, hi_ref, w_ref, b_ref, cot_ref, act_ref, grad_ref, gw_ref, x_ref, g_ref, t_ref, s_ref):
    zero = jnp.zeros((16, LANES), BF)
    for a, ref in enumerate((lo_ref, mid_ref, hi_ref)):
        for b in range(3):
            k = (a * 3 + b) * 16
            for h in range(ROWS):
                q = h + b - 1
                x_ref[k : k + 16, tile(h)] = ref[:, tile(q)] if 0 <= q < ROWS else zero
    x_ref[144:160, :] = jnp.ones((16, CELLS), BF)
    w = w_ref[...].astype(F32)
    weights = jnp.concatenate(
        [
            jnp.concatenate([w[(k * 3 + e) * 16 : (k * 3 + e + 1) * 16] for e in range(3)], axis=1)
            for k in range(9)
        ],
        axis=0,
    )
    weights = jnp.transpose(weights).astype(BF)
    r = iota((512, 512), 0)
    q = iota((512, 512), 1)
    swap = flag(((r >> 5) == (q & 15)) & ((r & 31) == (q >> 4)))
    cot = dot(swap, cot_ref[...].reshape(512, LANES))
    bias = b_ref[...]
    for n in range(4):
        t_ref[...] = dot(weights, x_ref[0:144, n * 512 : (n + 1) * 512])
        for j in range(4):
            h = n * 4 + j
            z = (
                from_left(t_ref[0:32, tile(j)])
                + t_ref[32:64, tile(j)]
                + from_right(t_ref[64:96, tile(j)])
                + bias
            )
            s_ref[h * 32 : (h + 1) * 32] = smooth(z).astype(BF)
            g = (cot[h * 32 : (h + 1) * 32] * slope_of(z)).astype(BF)
            grad_ref[:, tile(h)] = g
            g = g.astype(F32)
            g_ref[0:32, tile(h)] = from_right(g).astype(BF)
            g_ref[32:64, tile(h)] = g.astype(BF)
            g_ref[64:96, tile(h)] = from_left(g).astype(BF)
    g_ref[96:128, :] = jnp.zeros((32, CELLS), BF)
    act_ref[...] = dot(swap, s_ref[...], 0, 0).astype(BF).reshape(32, ROWS, LANES)
    gw_ref[...] = dot(x_ref[...], g_ref[...], 1, 1)


def third_kernel(mid_ref, lo_ref, hi_ref, w_ref, slope_ref, patches_ref, gw_ref, x_ref, t_ref, g_ref):
    for a, ref in enumerate((hi_ref, mid_ref, lo_ref)):
        x_ref[a * 32 : (a + 1) * 32, :] = ref[...]
    w = w_ref[...].astype(F32)
    weights = jnp.concatenate([w[a * 144 : (a + 1) * 144] for a in range(3)], axis=1).astype(BF)
    t_ref[...] = dot(weights, x_ref[...])
    sums = jnp.zeros((16, 1), F32)
    for h in range(ROWS):
        cols = []
        for e in range(3):
            parts = [
                t_ref[(b * 3 + e) * 16 : (b * 3 + e + 1) * 16, tile(h - b + 1)]
                for b in range(3)
                if 0 <= h - b + 1 < ROWS
            ]
            cols.append(functools.reduce(lambda x, y: x + y, parts))
        gp = (from_right(cols[0]) + cols[1] + from_left(cols[2])) * 0.125
        total = None
        for i in range(8):
            g = (gp * slope_ref[i * 16 : (i + 1) * 16, tile(h)]).astype(BF)
            g_ref[i * 16 : (i + 1) * 16, tile(h)] = g
            g = g.astype(F32)
            total = g if total is None else total + g
        sums = sums + jnp.sum(total, axis=1, keepdims=True)
    full = dot(g_ref[...], patches_ref[...], 1, 1)
    acc = full[0:16]
    for i in range(1, 8):
        shift = (i >> 2) * 64 + (i & 1) * 16 + ((i >> 1) & 1) * 4
        acc = acc + pltpu.roll(full[i * 16 : (i + 1) * 16], 256 - shift, 1)
    acc = jnp.where(iota((16, 256), 1) == 255, sums, acc)
    gw_ref[0:16] = acc[:, 0:128]
    gw_ref[16:32] = acc[:, 128:256]


def call(kernel, outs, scratch, name):
    return pl.pallas_call(
        kernel,
        out_shape=outs,
        scratch_shapes=scratch,
        compiler_params=pltpu.CompilerParams(vmem_limit_bytes=VMEM_LIMIT),
        name=name,
    )


def shape(dims, kind):
    return jax.ShapeDtypeStruct(dims, kind)


def halo(head, tail, axis):
    count = lax.axis_size(axis)
    up = [(i, i + 1) for i in range(count - 1)]
    down = [(i + 1, i) for i in range(count - 1)]
    return lax.ppermute(tail, axis, up), lax.ppermute(head, axis, down)


def direct(v, axis):
    n = lax.axis_size(axis)
    for part in [lax.ppermute(v, axis, [(i, (i + k) % n) for i in range(n)]) for k in range(1, n)]:
        v = v + part
    return v


def butterfly(v, axis):
    n = lax.axis_size(axis)
    d = 1
    while d < n:
        v = v + lax.ppermute(v, axis, [(i, i ^ d) for i in range(n)])
        d *= 2
    return v


def body(volumes, conv_one, bias_one, conv_two, bias_two, cotangent):
    depth = ("x", "y", "z")
    vol = volumes[0]
    lo, hi = halo(vol[:, 0], vol[:, 1], depth)
    base = jnp.pad(conv_one.astype(F32).transpose(4, 0, 2, 1, 3), ((0, 0), (0, 1), (0, 1), (0, 1), (0, 0))).reshape(16, 256)
    patches, slopes, pooled = call(
        first_kernel,
        (shape((256, CELLS), BF), shape((128, CELLS), F32), shape((16, CELLS), BF)),
        [],
        "first",
    )(vol, lo, hi, base, bias_one.reshape(16, 1))
    plo, phi = halo(pooled, pooled, depth)
    conv_flat = conv_two.reshape(432, 32)
    act, grad, gw_two = call(
        second_kernel,
        (shape((32, ROWS, LANES), BF), shape((32, CELLS), BF), shape((160, 128), F32)),
        [
            pltpu.VMEM((160, CELLS), BF),
            pltpu.VMEM((128, CELLS), BF),
            pltpu.VMEM((96, 512), F32),
            pltpu.VMEM((512, LANES), BF),
        ],
        "second",
    )(pooled, plo, phi, conv_flat, bias_two.reshape(32, 1), cotangent.reshape(32, ROWS, LANES))
    glo, ghi = halo(grad, grad, depth)
    gw_one = call(
        third_kernel,
        shape((32, 128), F32),
        [pltpu.VMEM((96, CELLS), BF), pltpu.VMEM((144, CELLS), F32), pltpu.VMEM((128, CELLS), BF)],
        "third",
    )(grad, glo, ghi, conv_flat, slopes, patches)
    v = jnp.concatenate([gw_one, gw_two[:152]], axis=0)
    v = direct(direct(direct(v, "core"), "x"), "y")
    v = butterfly(v, "z")
    one = jnp.concatenate([v[0:16], v[16:32]], axis=1).reshape(16, 4, 4, 4, 4)
    grad_conv_one = one[:, :3, :3, :3, :].transpose(1, 3, 2, 4, 0)
    grad_bias_one = one[:, 3, 3, 3, 3]
    grad_conv_two = v[32:176, :96].reshape(3, 3, 16, 3, 32).transpose(0, 1, 3, 2, 4)
    grad_bias_two = v[176, 32:64]
    return act.reshape(1, 32, 1, ROWS, LANES), grad_conv_one, grad_bias_one, grad_conv_two, grad_bias_two


def solution(mesh):
    devices = mesh.devices
    if devices.shape == (2, 128):
        split = (2, 4, 4, 8)
    else:
        split = (2, devices.shape[1], 1, 1)
    fine = Mesh(devices.reshape(split), ("core", "x", "y", "z"))
    cells = P("core", None, ("x", "y", "z"), None, None)
    return jax.shard_map(
        body,
        mesh=fine,
        in_specs=(cells, P(), P(), P(), P(), cells),
        out_specs=(cells, P(), P(), P(), P()),
        check_vma=False,
    )
```

profile of v0, /device:TPU:1, one launch (start us, length us, event | category | flops | bytes accessed | tf_op | source)
XLA Modules:
  0.0 94.1 jit_solution(2454650678790616482)
XLA Ops:
  0.6 0.9 copy.32
  1.5 0.0 copy-start.3
  1.6 1.3 %collective-permute-start.1 = (bf16[4,32,256]{2,1,0:T(8,128)(2,1)S(1)}, bf16[4,32,256]{2,1,0:T(8,128)(2,1)S(1)}, u32[]{:S(2)}, u32[]{:S(2)}) collective-permute-start(bf16[4,32,256]{2,1,0:T(8,128)(2,1)S(1)} %get-tuple-element.27), channel_id=1, source_target_pairs={{1,0},{2,1},{3,2},{4,3},{5,4},{6,5},{7,6},{8,7},{9,8},{10,9},{11,1... | collective-permute-start | bytes 196616 | tf_op jit(solution)/shard_map/ppermute | solution.py:187
  2.9 0.0 copy-start.4
  2.9 5.0 %collective-permute-start = (bf16[4,32,256]{2,1,0:T(8,128)(2,1)S(1)}, bf16[4,32,256]{2,1,0:T(8,128)(2,1)S(1)}, u32[]{:S(2)}, u32[]{:S(2)}) collective-permute-start(bf16[4,32,256]{2,1,0:T(8,128)(2,1)S(1)} %get-tuple-element.28), channel_id=1, source_target_pairs={{0,1},{1,2},{2,3},{3,4},{4,5},{5,6},{6,7},{7,8},{8,9},{9,10},{10,1... | collective-permute-start | bytes 196616 | tf_op jit(solution)/shard_map/ppermute | solution.py:187
  7.9 0.0 copy-done.4
  7.9 0.1 copy.24.b_ref
  8.0 0.0 copy-done.3
  8.1 0.0 copy-start
  8.1 0.1 copy.23.w_ref
  8.1 0.0 collective-permute-done.1.hi_ref
  8.1 1.1 %collective-permute-done.lo_ref = bf16[4,32,256]{2,1,0:T(8,128)(2,1)S(1)} collective-permute-done((bf16[4,32,256]{2,1,0:T(8,128)(2,1)S(1)}, bf16[4,32,256]{2,1,0:T(8,128)(2,1)S(1)}, u32[]{:S(2)}, u32[]{:S(2)}) %collective-permute-start) | collective-permute-done | bytes 65568 | tf_op jit(solution)/shard_map/ppermute | solution.py:187
  9.2 0.0 copy-done
  9.2 0.0 copy-start.1
  9.2 0.0 copy-start.2
  9.2 1.8 %first.1 = (bf16[256,2048]{1,0:T(8,128)(2,1)S(1)}, f32[128,2048]{1,0:T(8,128)S(1)}, bf16[16,2048]{1,0:T(8,128)(2,1)S(1)}) custom-call(bf16[4,2,32,256]{3,2,1,0:T(8,128)(2,1)S(1)} %bitcast.25, bf16[4,32,256]{2,1,0:T(8,128)(2,1)S(1)} %collective-permute-done.lo_ref, bf16[4,32,256]{2,1,0:T(8,128)(2,1)S(1)} %collective-permute-done.1.hi_ref, ...), custom_call_target="tpu_custom_call" | custom-call | tf_op jit(solution)/shard_map/first/pallas_call | solution.py:211
  11.1 0.0 copy-start.5
  11.1 1.3 %collective-permute-start.3 = (bf16[16,2048]{1,0:T(8,128)(2,1)S(1)}, bf16[16,2048]{1,0:T(8,128)(2,1)S(1)}, u32[]{:S(2)}, u32[]{:S(2)}) collective-permute-start(bf16[16,2048]{1,0:T(8,128)(2,1)S(1)} %get-tuple-element.11.mid_ref), channel_id=1, source_target_pairs={{1,0},{2,1},{3,2},{4,3},{5,4},{6,5},{7,6},{8,7},{9,8},{10,9},{11,1... | collective-permute-start | bytes 196616 | tf_op jit(solution)/shard_map/ppermute | solution.py:187
  12.4 4.3 %collective-permute-start.2 = (bf16[16,2048]{1,0:T(8,128)(2,1)S(1)}, bf16[16,2048]{1,0:T(8,128)(2,1)S(1)}, u32[]{:S(2)}, u32[]{:S(2)}) collective-permute-start(bf16[16,2048]{1,0:T(8,128)(2,1)S(1)} %get-tuple-element.11.mid_ref), channel_id=1, source_target_pairs={{0,1},{1,2},{2,3},{3,4},{4,5},{5,6},{6,7},{7,8},{8,9},{9,10},{10,1... | collective-permute-start | bytes 196616 | tf_op jit(solution)/shard_map/ppermute | solution.py:187
  16.7 0.0 copy-done.5
  16.7 0.1 copy.25.b_ref
  16.8 0.0 collective-permute-done.3.hi_ref
  16.8 1.2 %collective-permute-done.2.lo_ref = bf16[16,2048]{1,0:T(8,128)(2,1)S(1)} collective-permute-done((bf16[16,2048]{1,0:T(8,128)(2,1)S(1)}, bf16[16,2048]{1,0:T(8,128)(2,1)S(1)}, u32[]{:S(2)}, u32[]{:S(2)}) %collective-permute-start.2) | collective-permute-done | bytes 65568 | tf_op jit(solution)/shard_map/ppermute | solution.py:187
  18.0 0.0 copy-done.1
  18.0 0.0 copy-done.2
  18.0 1.9 %second.1 = (bf16[32,16,128]{2,1,0:T(8,128)(2,1)}, bf16[32,2048]{1,0:T(8,128)(2,1)S(1)}, f32[160,128]{1,0:T(8,128)S(1)}) custom-call(bf16[16,2048]{1,0:T(8,128)(2,1)S(1)} %get-tuple-element.11.mid_ref, bf16[16,2048]{1,0:T(8,128)(2,1)S(1)} %collective-permute-done.2.lo_ref, bf16[16,2048]{1,0:T(8,128)(2,1)S(1)} %collective-permute-done.3.hi_ref, ...), custom_call_target="tpu_custom_call" | custom-call | tf_op jit(solution)/shard_map/second/pallas_call | solution.py:219
  19.9 1.3 %collective-permute-start.5 = (bf16[32,2048]{1,0:T(8,128)(2,1)S(1)}, bf16[32,2048]{1,0:T(8,128)(2,1)S(1)}, u32[]{:S(2)}, u32[]{:S(2)}) collective-permute-start(bf16[32,2048]{1,0:T(8,128)(2,1)S(1)} %get-tuple-element.13.mid_ref), channel_id=1, source_target_pairs={{1,0},{2,1},{3,2},{4,3},{5,4},{6,5},{7,6},{8,7},{9,8},{10,9},{11,1... | collective-permute-start | bytes 393224 | tf_op jit(solution)/shard_map/ppermute | solution.py:187
  21.2 4.3 %collective-permute-start.4 = (bf16[32,2048]{1,0:T(8,128)(2,1)S(1)}, bf16[32,2048]{1,0:T(8,128)(2,1)S(1)}, u32[]{:S(2)}, u32[]{:S(2)}) collective-permute-start(bf16[32,2048]{1,0:T(8,128)(2,1)S(1)} %get-tuple-element.13.mid_ref), channel_id=1, source_target_pairs={{0,1},{1,2},{2,3},{3,4},{4,5},{5,6},{6,7},{7,8},{8,9},{9,10},{10,1... | collective-permute-start | bytes 393224 | tf_op jit(solution)/shard_map/ppermute | solution.py:187
  25.5 0.4 collective-permute-done.5.hi_ref
  25.9 1.5 %collective-permute-done.4.lo_ref = bf16[32,2048]{1,0:T(8,128)(2,1)S(1)} collective-permute-done((bf16[32,2048]{1,0:T(8,128)(2,1)S(1)}, bf16[32,2048]{1,0:T(8,128)(2,1)S(1)}, u32[]{:S(2)}, u32[]{:S(2)}) %collective-permute-start.4) | collective-permute-done | bytes 131104 | tf_op jit(solution)/shard_map/ppermute | solution.py:187
  27.4 0.9 third.1
  28.4 5.8 %collective-permute-start.6 = (f32[184,128]{1,0:T(8,128)S(1)}, f32[184,128]{1,0:T(8,128)S(1)}, u32[]{:S(2)}, u32[]{:S(2)}) collective-permute-start(f32[184,128]{1,0:T(8,128)S(1)} %pad_maximum_fusion), channel_id=1, source_target_pairs={{0,128},{128,0},{1,129},{129,1},{2,130},{130,2},{3,131},{131,3},{4... | collective-permute-start | bytes 282632 | tf_op jit(solution)/shard_map/ppermute | solution.py:192
  34.1 0.9 collective-permute-done.6
  35.1 22.5 %collective-permute-start.9 = (f32[184,128]{1,0:T(8,128)S(1)}, f32[184,128]{1,0:T(8,128)S(1)}, u32[]{:S(2)}, u32[]{:S(2)}) collective-permute-start(f32[184,128]{1,0:T(8,128)S(1)} %fusion), channel_id=1, source_target_pairs={{0,96},{32,0},{64,32},{96,64},{1,97},{33,1},{65,33},{97,65},{2,98}... | collective-permute-start | bytes 282632 | tf_op jit(solution)/shard_map/ppermute | solution.py:192
  57.5 0.2 collective-permute-start.8
  57.8 0.6 collective-permute-start.7
  58.4 2.9 %collective-permute-done.9 = f32[184,128]{1,0:T(8,128)S(1)} collective-permute-done((f32[184,128]{1,0:T(8,128)S(1)}, f32[184,128]{1,0:T(8,128)S(1)}, u32[]{:S(2)}, u32[]{:S(2)}) %collective-permute-start.9) | collective-permute-done | bytes 94240 | tf_op jit(solution)/shard_map/ppermute | solution.py:192
  61.3 1.3 %collective-permute-done.8 = f32[184,128]{1,0:T(8,128)S(1)} collective-permute-done((f32[184,128]{1,0:T(8,128)S(1)}, f32[184,128]{1,0:T(8,128)S(1)}, u32[]{:S(2)}, u32[]{:S(2)}) %collective-permute-start.8) | collective-permute-done | bytes 94240 | tf_op jit(solution)/shard_map/ppermute | solution.py:192
  62.6 2.9 %collective-permute-done.7 = f32[184,128]{1,0:T(8,128)S(1)} collective-permute-done((f32[184,128]{1,0:T(8,128)S(1)}, f32[184,128]{1,0:T(8,128)S(1)}, u32[]{:S(2)}, u32[]{:S(2)}) %collective-permute-start.7) | collective-permute-done | bytes 94240 | tf_op jit(solution)/shard_map/ppermute | solution.py:192
  65.5 0.1 collective-permute-start.12
  65.6 0.1 collective-permute-start.11
  65.7 1.4 %collective-permute-start.10 = (f32[184,128]{1,0:T(8,128)S(1)}, f32[184,128]{1,0:T(8,128)S(1)}, u32[]{:S(2)}, u32[]{:S(2)}) collective-permute-start(f32[184,128]{1,0:T(8,128)S(1)} %add_add_fusion.1), channel_id=1, source_target_pairs={{0,8},{8,16},{16,24},{24,0},{1,9},{9,17},{17,25},{25,1},{2,10},{10... | collective-permute-start | bytes 282632 | tf_op jit(solution)/shard_map/ppermute | solution.py:192
  67.1 2.0 %collective-permute-done.12 = f32[184,128]{1,0:T(8,128)S(1)} collective-permute-done((f32[184,128]{1,0:T(8,128)S(1)}, f32[184,128]{1,0:T(8,128)S(1)}, u32[]{:S(2)}, u32[]{:S(2)}) %collective-permute-start.12) | collective-permute-done | bytes 94240 | tf_op jit(solution)/shard_map/ppermute | solution.py:192
  69.0 1.6 %collective-permute-done.11 = f32[184,128]{1,0:T(8,128)S(1)} collective-permute-done((f32[184,128]{1,0:T(8,128)S(1)}, f32[184,128]{1,0:T(8,128)S(1)}, u32[]{:S(2)}, u32[]{:S(2)}) %collective-permute-start.11) | collective-permute-done | bytes 94240 | tf_op jit(solution)/shard_map/ppermute | solution.py:192
  70.6 3.1 %collective-permute-done.10 = f32[184,128]{1,0:T(8,128)S(1)} collective-permute-done((f32[184,128]{1,0:T(8,128)S(1)}, f32[184,128]{1,0:T(8,128)S(1)}, u32[]{:S(2)}, u32[]{:S(2)}) %collective-permute-start.10) | collective-permute-done | bytes 94240 | tf_op jit(solution)/shard_map/ppermute | solution.py:192
  73.8 0.1 collective-permute-start.13
  73.8 3.4 %collective-permute-done.13 = f32[184,128]{1,0:T(8,128)S(1)} collective-permute-done((f32[184,128]{1,0:T(8,128)S(1)}, f32[184,128]{1,0:T(8,128)S(1)}, u32[]{:S(2)}, u32[]{:S(2)}) %collective-permute-start.13) | collective-permute-done | bytes 94240 | tf_op jit(solution)/shard_map/ppermute | solution.py:201
  77.3 0.1 collective-permute-start.14
  77.4 6.4 %collective-permute-done.14 = f32[184,128]{1,0:T(8,128)S(1)} collective-permute-done((f32[184,128]{1,0:T(8,128)S(1)}, f32[184,128]{1,0:T(8,128)S(1)}, u32[]{:S(2)}, u32[]{:S(2)}) %collective-permute-start.14) | collective-permute-done | bytes 94240 | tf_op jit(solution)/shard_map/ppermute | solution.py:201
  83.8 0.1 collective-permute-start.15
  83.9 7.4 %collective-permute-done.15 = f32[184,128]{1,0:T(8,128)S(1)} collective-permute-done((f32[184,128]{1,0:T(8,128)S(1)}, f32[184,128]{1,0:T(8,128)S(1)}, u32[]{:S(2)}, u32[]{:S(2)}) %collective-permute-start.15) | collective-permute-done | bytes 94240 | tf_op jit(solution)/shard_map/ppermute | solution.py:201
  91.3 0.6 slice_bitcast_fusion.3
  92.0 0.1 copy.26
  92.1 0.5 slice_bitcast_fusion.4
  92.6 0.6 copy.28
  93.2 0.2 reshape.44
  93.4 0.7 copy.29
  (15 shorter events, 0.2 us)
Async XLA Ops:
  1.5 6.5 %copy-start.3 = (bf16[3,3,3,4,16]{4,3,2,1,0:T(4,128)(2,1)S(1)}, bf16[3,3,3,4,16]{4,3,2,1,0:T(4,128)(2,1)}, u32[]{:S(2)}) copy-start(bf16[3,3,3,4,16]{4,3,2,1,0:T(4,128)(2,1)} %param.7) | copy-start | bytes 10372
  1.6 6.6 %collective-permute-start.1 = (bf16[4,32,256]{2,1,0:T(8,128)(2,1)S(1)}, bf16[4,32,256]{2,1,0:T(8,128)(2,1)S(1)}, u32[]{:S(2)}, u32[]{:S(2)}) collective-permute-start(bf16[4,32,256]{2,1,0:T(8,128)(2,1)S(1)} %get-tuple-element.27), channel_id=1, source_target_pairs={{1,0},{2,1},{3,2},{4,3},{5,4},{6,5},{7,6},{8,7},{9,8},{10,9},{11,1... | collective-permute-start | bytes 196616 | tf_op jit(solution)/shard_map/ppermute | solution.py:187
  2.9 5.0 %copy-start.4 = (f32[16]{0:T(128)S(1)}, f32[16]{0:T(128)}, u32[]{:S(2)}) copy-start(f32[16]{0:T(128)} %param.8) | copy-start | bytes 196
  2.9 6.3 %collective-permute-start = (bf16[4,32,256]{2,1,0:T(8,128)(2,1)S(1)}, bf16[4,32,256]{2,1,0:T(8,128)(2,1)S(1)}, u32[]{:S(2)}, u32[]{:S(2)}) collective-permute-start(bf16[4,32,256]{2,1,0:T(8,128)(2,1)S(1)} %get-tuple-element.28), channel_id=1, source_target_pairs={{0,1},{1,2},{2,3},{3,4},{4,5},{5,6},{6,7},{7,8},{8,9},{9,10},{10,1... | collective-permute-start | bytes 196616 | tf_op jit(solution)/shard_map/ppermute | solution.py:187
  8.1 1.2 %copy-start = (bf16[1,4,2,32,256]{4,3,2,1,0:T(8,128)(2,1)S(1)}, bf16[1,4,2,32,256]{4,3,2,1,0:T(8,128)(2,1)}, u32[]{:S(2)}) copy-start(bf16[1,4,2,32,256]{4,3,2,1,0:T(8,128)(2,1)} %param.6) | copy-start | bytes 393220
  9.2 8.8 %copy-start.1 = (bf16[3,3,3,16,32]{4,3,2,1,0:T(8,128)(2,1)S(1)}, bf16[3,3,3,16,32]{4,3,2,1,0:T(8,128)(2,1)}, u32[]{:S(2)}) copy-start(bf16[3,3,3,16,32]{4,3,2,1,0:T(8,128)(2,1)} %param.9) | copy-start | bytes 82948
  9.2 8.8 %copy-start.2 = (bf16[1,32,1,16,128]{4,3,2,1,0:T(8,128)(2,1)S(1)}, bf16[1,32,1,16,128]{4,3,2,1,0:T(8,128)(2,1)}, u32[]{:S(2)}) copy-start(bf16[1,32,1,16,128]{4,3,2,1,0:T(8,128)(2,1)} %param.11) | copy-start | bytes 393220
  11.1 5.6 %copy-start.5 = (f32[32]{0:T(128)S(1)}, f32[32]{0:T(128)}, u32[]{:S(2)}) copy-start(f32[32]{0:T(128)} %param.10) | copy-start | bytes 388
  11.1 5.7 %collective-permute-start.3 = (bf16[16,2048]{1,0:T(8,128)(2,1)S(1)}, bf16[16,2048]{1,0:T(8,128)(2,1)S(1)}, u32[]{:S(2)}, u32[]{:S(2)}) collective-permute-start(bf16[16,2048]{1,0:T(8,128)(2,1)S(1)} %get-tuple-element.11.mid_ref), channel_id=1, source_target_pairs={{1,0},{2,1},{3,2},{4,3},{5,4},{6,5},{7,6},{8,7},{9,8},{10,9},{11,1... | collective-permute-start | bytes 196616 | tf_op jit(solution)/shard_map/ppermute | solution.py:187
  12.4 5.6 %collective-permute-start.2 = (bf16[16,2048]{1,0:T(8,128)(2,1)S(1)}, bf16[16,2048]{1,0:T(8,128)(2,1)S(1)}, u32[]{:S(2)}, u32[]{:S(2)}) collective-permute-start(bf16[16,2048]{1,0:T(8,128)(2,1)S(1)} %get-tuple-element.11.mid_ref), channel_id=1, source_target_pairs={{0,1},{1,2},{2,3},{3,4},{4,5},{5,6},{6,7},{7,8},{8,9},{9,10},{10,1... | collective-permute-start | bytes 196616 | tf_op jit(solution)/shard_map/ppermute | solution.py:187
  19.9 6.0 %collective-permute-start.5 = (bf16[32,2048]{1,0:T(8,128)(2,1)S(1)}, bf16[32,2048]{1,0:T(8,128)(2,1)S(1)}, u32[]{:S(2)}, u32[]{:S(2)}) collective-permute-start(bf16[32,2048]{1,0:T(8,128)(2,1)S(1)} %get-tuple-element.13.mid_ref), channel_id=1, source_target_pairs={{1,0},{2,1},{3,2},{4,3},{5,4},{6,5},{7,6},{8,7},{9,8},{10,9},{11,1... | collective-permute-start | bytes 393224 | tf_op jit(solution)/shard_map/ppermute | solution.py:187
  21.2 6.3 %collective-permute-start.4 = (bf16[32,2048]{1,0:T(8,128)(2,1)S(1)}, bf16[32,2048]{1,0:T(8,128)(2,1)S(1)}, u32[]{:S(2)}, u32[]{:S(2)}) collective-permute-start(bf16[32,2048]{1,0:T(8,128)(2,1)S(1)} %get-tuple-element.13.mid_ref), channel_id=1, source_target_pairs={{0,1},{1,2},{2,3},{3,4},{4,5},{5,6},{6,7},{7,8},{8,9},{9,10},{10,1... | collective-permute-start | bytes 393224 | tf_op jit(solution)/shard_map/ppermute | solution.py:187
  28.4 6.7 %collective-permute-start.6 = (f32[184,128]{1,0:T(8,128)S(1)}, f32[184,128]{1,0:T(8,128)S(1)}, u32[]{:S(2)}, u32[]{:S(2)}) collective-permute-start(f32[184,128]{1,0:T(8,128)S(1)} %pad_maximum_fusion), channel_id=1, source_target_pairs={{0,128},{128,0},{1,129},{129,1},{2,130},{130,2},{3,131},{131,3},{4... | collective-permute-start | bytes 282632 | tf_op jit(solution)/shard_map/ppermute | solution.py:192
  35.1 26.2 %collective-permute-start.9 = (f32[184,128]{1,0:T(8,128)S(1)}, f32[184,128]{1,0:T(8,128)S(1)}, u32[]{:S(2)}, u32[]{:S(2)}) collective-permute-start(f32[184,128]{1,0:T(8,128)S(1)} %fusion), channel_id=1, source_target_pairs={{0,96},{32,0},{64,32},{96,64},{1,97},{33,1},{65,33},{97,65},{2,98}... | collective-permute-start | bytes 282632 | tf_op jit(solution)/shard_map/ppermute | solution.py:192
  57.5 5.0 %collective-permute-start.8 = (f32[184,128]{1,0:T(8,128)S(1)}, f32[184,128]{1,0:T(8,128)S(1)}, u32[]{:S(2)}, u32[]{:S(2)}) collective-permute-start(f32[184,128]{1,0:T(8,128)S(1)} %fusion), channel_id=1, source_target_pairs={{0,64},{32,96},{64,0},{96,32},{1,65},{33,97},{65,1},{97,33},{2,66}... | collective-permute-start | bytes 282632 | tf_op jit(solution)/shard_map/ppermute | solution.py:192
  57.8 7.7 %collective-permute-start.7 = (f32[184,128]{1,0:T(8,128)S(1)}, f32[184,128]{1,0:T(8,128)S(1)}, u32[]{:S(2)}, u32[]{:S(2)}) collective-permute-start(f32[184,128]{1,0:T(8,128)S(1)} %fusion), channel_id=1, source_target_pairs={{0,32},{32,64},{64,96},{96,0},{1,33},{33,65},{65,97},{97,1},{2,34}... | collective-permute-start | bytes 282632 | tf_op jit(solution)/shard_map/ppermute | solution.py:192
  65.5 3.5 %collective-permute-start.12 = (f32[184,128]{1,0:T(8,128)S(1)}, f32[184,128]{1,0:T(8,128)S(1)}, u32[]{:S(2)}, u32[]{:S(2)}) collective-permute-start(f32[184,128]{1,0:T(8,128)S(1)} %add_add_fusion.1), channel_id=1, source_target_pairs={{0,24},{8,0},{16,8},{24,16},{1,25},{9,1},{17,9},{25,17},{2,26},{10... | collective-permute-start | bytes 282632 | tf_op jit(solution)/shard_map/ppermute | solution.py:192
  65.6 5.0 %collective-permute-start.11 = (f32[184,128]{1,0:T(8,128)S(1)}, f32[184,128]{1,0:T(8,128)S(1)}, u32[]{:S(2)}, u32[]{:S(2)}) collective-permute-start(f32[184,128]{1,0:T(8,128)S(1)} %add_add_fusion.1), channel_id=1, source_target_pairs={{0,16},{8,24},{16,0},{24,8},{1,17},{9,25},{17,1},{25,9},{2,18},{10... | collective-permute-start | bytes 282632 | tf_op jit(solution)/shard_map/ppermute | solution.py:192
  65.7 8.0 %collective-permute-start.10 = (f32[184,128]{1,0:T(8,128)S(1)}, f32[184,128]{1,0:T(8,128)S(1)}, u32[]{:S(2)}, u32[]{:S(2)}) collective-permute-start(f32[184,128]{1,0:T(8,128)S(1)} %add_add_fusion.1), channel_id=1, source_target_pairs={{0,8},{8,16},{16,24},{24,0},{1,9},{9,17},{17,25},{25,1},{2,10},{10... | collective-permute-start | bytes 282632 | tf_op jit(solution)/shard_map/ppermute | solution.py:192
  73.8 3.5 %collective-permute-start.13 = (f32[184,128]{1,0:T(8,128)S(1)}, f32[184,128]{1,0:T(8,128)S(1)}, u32[]{:S(2)}, u32[]{:S(2)}) collective-permute-start(f32[184,128]{1,0:T(8,128)S(1)} %add_add_fusion), channel_id=1, source_target_pairs={{0,1},{1,0},{2,3},{3,2},{4,5},{5,4},{6,7},{7,6},{8,9},{9,8},{10,11... | collective-permute-start | bytes 282632 | tf_op jit(solution)/shard_map/ppermute | solution.py:201
  77.3 6.5 %collective-permute-start.14 = (f32[184,128]{1,0:T(8,128)S(1)}, f32[184,128]{1,0:T(8,128)S(1)}, u32[]{:S(2)}, u32[]{:S(2)}) collective-permute-start(f32[184,128]{1,0:T(8,128)S(1)} %add.39), channel_id=1, source_target_pairs={{0,2},{1,3},{2,0},{3,1},{4,6},{5,7},{6,4},{7,5},{8,10},{9,11},{10,... | collective-permute-start | bytes 282632 | tf_op jit(solution)/shard_map/ppermute | solution.py:201
  83.8 7.5 %collective-permute-start.15 = (f32[184,128]{1,0:T(8,128)S(1)}, f32[184,128]{1,0:T(8,128)S(1)}, u32[]{:S(2)}, u32[]{:S(2)}) collective-permute-start(f32[184,128]{1,0:T(8,128)S(1)} %add.40), channel_id=1, source_target_pairs={{0,4},{1,5},{2,6},{3,7},{4,0},{5,1},{6,2},{7,3},{8,12},{9,13},{10,... | collective-permute-start | bytes 282632 | tf_op jit(solution)/shard_map/ppermute | solution.py:201
where the time goes:
time: 95 us; the launch traced here: 94.1 us
  starting transfers between devices  48.4 us (51%)
  waiting for transfers between devices  36.2 us (38%)
  Pallas kernels  4.61 us (5%)
  local copies, waits for them, and re-layouts  3.92 us (4%)
    ppermute x7, starting transfers between devices, direct(): lax.ppermute(v, axis, [(i, (i + k) % n) for i in range(n)])  30.6 us
    ppermute x6, starting transfers between devices, halo(): return (lax.ppermute(tail, axis, up), lax.ppermute(head, axis, down))  17.5 us
    ppermute x3, waiting for transfers between devices, butterfly(): v = v + lax.ppermute(v, axis, [(i, i ^ d) for i in range(n)])  17.3 us
    ppermute x7, waiting for transfers between devices, direct(): lax.ppermute(v, axis, [(i, (i + k) % n) for i in range(n)])  14.7 us
    ppermute x6, waiting for transfers between devices, halo(): return (lax.ppermute(tail, axis, up), lax.ppermute(head, axis, down))  4.2 us
    unnamed x15, local copies, waits for them, and re-layouts  2.28 us
  transfers between devices with their start and end apart: 16, of which 14 were waited for; matrix products, arithmetic and copies ran while one was open for 0% of the time, Pallas kernels for 0%

commit v1 on v0

--- a/solution.py
+++ b/solution.py
@@ -47,7 +47,30 @@
     return slice(h * LANES, (h + 1) * LANES)
 
 
-def first_kernel(vol_ref, lo_ref, hi_ref, w_ref, b_ref, patches_ref, slope_ref, pooled_ref):
+def place(where_ref, even_ref, odd_ref, lo_ref, hi_ref):
+    @pl.when(where_ref[0] == 1)
+    def _():
+        lo_ref[...] = even_ref[...]
+        hi_ref[...] = odd_ref[...]
+
+    @pl.when(where_ref[0] == 0)
+    def _():
+        lo_ref[...] = odd_ref[...]
+        hi_ref[...] = even_ref[...]
+
+    @pl.when(where_ref[1] == 1)
+    def _():
+        lo_ref[...] = jnp.zeros_like(lo_ref)
+
+    @pl.when(where_ref[2] == 1)
+    def _():
+        hi_ref[...] = jnp.zeros_like(hi_ref)
+
+
+def first_kernel(
+    where_ref, vol_ref, even_ref, odd_ref, w_ref, b_ref, patches_ref, slope_ref, pooled_ref, lo_ref, hi_ref
+):
+    place(where_ref, even_ref, odd_ref, lo_ref, hi_ref)
     cols = iota((256, 512), 1)
     pick_cols = flag(iota((256, 512), 0) == 2 * (cols & 127) + (cols >> 7) - 1)
     rows = iota((256, 128), 0)
@@ -87,7 +110,10 @@
         pooled_ref[:, span] = (total * 0.125).astype(BF)
 
 
-def second_kernel(mid_ref, lo_ref, hi_ref, w_ref, b_ref, cot_ref, act_ref, grad_ref, gw_ref, x_ref, g_ref, t_ref, s_ref):
+def second_kernel(
+    where_ref, mid_ref, even_ref, odd_ref, w_ref, b_ref, cot_ref, act_ref, grad_ref, gw_ref, x_ref, g_ref, t_ref, s_ref, lo_ref, hi_ref
+):
+    place(where_ref, even_ref, odd_ref, lo_ref, hi_ref)
     zero = jnp.zeros((16, LANES), BF)
     for a, ref in enumerate((lo_ref, mid_ref, hi_ref)):
         for b in range(3):
@@ -132,9 +158,9 @@
     gw_ref[...] = dot(x_ref[...], g_ref[...], 1, 1)
 
 
-def third_kernel(mid_ref, lo_ref, hi_ref, w_ref, slope_ref, patches_ref, gw_ref, x_ref, t_ref, g_ref):
-    for a, ref in enumerate((hi_ref, mid_ref, lo_ref)):
-        x_ref[a * 32 : (a + 1) * 32, :] = ref[...]
+def third_kernel(where_ref, mid_ref, even_ref, odd_ref, w_ref, slope_ref, patches_ref, gw_ref, x_ref, t_ref, g_ref):
+    x_ref[32:64, :] = mid_ref[...]
+    place(where_ref, even_ref, odd_ref, x_ref.at[64:96], x_ref.at[0:32])
     w = w_ref[...].astype(F32)
     weights = jnp.concatenate([w[a * 144 : (a + 1) * 144] for a in range(3)], axis=1).astype(BF)
     t_ref[...] = dot(weights, x_ref[...])
@@ -166,10 +192,28 @@
     gw_ref[16:32] = acc[:, 128:256]
 
 
-def call(kernel, outs, scratch, name):
+def last_kernel(mine_ref, other_ref, one_ref, bias_one_ref, two_ref, bias_two_ref):
+    v = mine_ref[...] + other_ref[...]
+    turned = jnp.transpose(jnp.concatenate([v[0:16], v[16:32]], axis=1))
+    for a in range(3):
+        for b in range(3):
+            k = a * 3 + b
+            for e in range(3):
+                row = a * 64 + e * 16 + b * 4
+                one_ref[k * 3 + e] = turned[row : row + 4]
+                two_ref[k * 3 + e] = v[32 + k * 16 : 48 + k * 16, e * 32 : (e + 1) * 32]
+    bias_one_ref[...] = turned[255:256]
+    bias_two_ref[...] = v[176:177, 32:64]
+
+
+def call(kernel, outs, scratch, name, where=True):
+    count = {"first": 6, "second": 7, "third": 7, "last": 2}[name]
+    vmem = pl.BlockSpec(memory_space=pltpu.VMEM)
+    specs = [pl.BlockSpec(memory_space=pltpu.SMEM) if where and i == 0 else vmem for i in range(count)]
     return pl.pallas_call(
         kernel,
         out_shape=outs,
+        in_specs=specs,
         scratch_shapes=scratch,
         compiler_params=pltpu.CompilerParams(vmem_limit_bytes=VMEM_LIMIT),
         name=name,
@@ -180,41 +224,30 @@
     return jax.ShapeDtypeStruct(dims, kind)
 
 
-def halo(head, tail, axis):
-    count = lax.axis_size(axis)
-    up = [(i, i + 1) for i in range(count - 1)]
-    down = [(i + 1, i) for i in range(count - 1)]
-    return lax.ppermute(tail, axis, up), lax.ppermute(head, axis, down)
-
-
-def direct(v, axis):
+def pairs(even, odd, axis):
     n = lax.axis_size(axis)
-    for part in [lax.ppermute(v, axis, [(i, (i + k) % n) for i in range(n)]) for k in range(1, n)]:
-        v = v + part
-    return v
-
-
-def butterfly(v, axis):
-    n = lax.axis_size(axis)
-    d = 1
-    while d < n:
-        v = v + lax.ppermute(v, axis, [(i, i ^ d) for i in range(n)])
-        d *= 2
-    return v
+    first = lax.ppermute(even, axis, [(i, i ^ 1) for i in range(n)])
+    second = lax.ppermute(odd, axis, [(i, (((i + 1) ^ 1) - 1) % n) for i in range(n)])
+    return first, second
 
 
 def body(volumes, conv_one, bias_one, conv_two, bias_two, cotangent):
     depth = ("x", "y", "z")
     vol = volumes[0]
-    lo, hi = halo(vol[:, 0], vol[:, 1], depth)
+    place_at = lax.axis_index(depth)
+    odd = place_at % 2
+    where = jnp.stack([odd, place_at == 0, place_at == lax.axis_size(depth) - 1]).astype(jnp.int32)
+    head, tail = vol[:, 0], vol[:, 1]
+    even_part, odd_part = pairs(jnp.where(odd == 1, head, tail), jnp.where(odd == 1, tail, head), depth)
     base = jnp.pad(conv_one.astype(F32).transpose(4, 0, 2, 1, 3), ((0, 0), (0, 1), (0, 1), (0, 1), (0, 0))).reshape(16, 256)
+    plane = pltpu.VMEM((4, 32, 256), BF)
     patches, slopes, pooled = call(
         first_kernel,
         (shape((256, CELLS), BF), shape((128, CELLS), F32), shape((16, CELLS), BF)),
-        [],
+        [plane, plane],
         "first",
-    )(vol, lo, hi, base, bias_one.reshape(16, 1))
-    plo, phi = halo(pooled, pooled, depth)
+    )(where, vol, even_part, odd_part, base, bias_one.reshape(16, 1))
+    even_part, odd_part = pairs(pooled, pooled, depth)
     conv_flat = conv_two.reshape(432, 32)
     act, grad, gw_two = call(
         second_kernel,
@@ -224,25 +257,42 @@
             pltpu.VMEM((128, CELLS), BF),
             pltpu.VMEM((96, 512), F32),
             pltpu.VMEM((512, LANES), BF),
+            pltpu.VMEM((16, CELLS), BF),
+            pltpu.VMEM((16, CELLS), BF),
         ],
         "second",
-    )(pooled, plo, phi, conv_flat, bias_two.reshape(32, 1), cotangent.reshape(32, ROWS, LANES))
-    glo, ghi = halo(grad, grad, depth)
+    )(where, pooled, even_part, odd_part, conv_flat, bias_two.reshape(32, 1), cotangent.reshape(32, ROWS, LANES))
+    even_part, odd_part = pairs(grad, grad, depth)
     gw_one = call(
         third_kernel,
         shape((32, 128), F32),
         [pltpu.VMEM((96, CELLS), BF), pltpu.VMEM((144, CELLS), F32), pltpu.VMEM((128, CELLS), BF)],
         "third",
-    )(grad, glo, ghi, conv_flat, slopes, patches)
+    )(where, grad, even_part, odd_part, conv_flat, slopes, patches)
     v = jnp.concatenate([gw_one, gw_two[:152]], axis=0)
-    v = direct(direct(direct(v, "core"), "x"), "y")
-    v = butterfly(v, "z")
-    one = jnp.concatenate([v[0:16], v[16:32]], axis=1).reshape(16, 4, 4, 4, 4)
-    grad_conv_one = one[:, :3, :3, :3, :].transpose(1, 3, 2, 4, 0)
-    grad_bias_one = one[:, 3, 3, 3, 3]
-    grad_conv_two = v[32:176, :96].reshape(3, 3, 16, 3, 32).transpose(0, 1, 3, 2, 4)
-    grad_bias_two = v[176, 32:64]
-    return act.reshape(1, 32, 1, ROWS, LANES), grad_conv_one, grad_bias_one, grad_conv_two, grad_bias_two
+    n = {axis: lax.axis_size(axis) for axis in ("z", "y", "x", "core")}
+    steps = [
+        (axis, [(i, i ^ 2 if d == 4 and size == 8 else i ^ (d - 1)) for i in range(size)])
+        for axis, size in n.items()
+        for d in (2, 4, 8)
+        if d <= size
+    ]
+    for axis, perm in steps[:-1]:
+        v = v + lax.ppermute(v, axis, perm)
+    one, sum_one, two, sum_two = call(
+        last_kernel,
+        (shape((27, 4, 16), F32), shape((1, 16), F32), shape((27, 16, 32), F32), shape((1, 32), F32)),
+        [],
+        "last",
+        where=False,
+    )(v, lax.ppermute(v, *steps[-1]))
+    return (
+        act.reshape(1, 32, 1, ROWS, LANES),
+        one.reshape(3, 3, 3, 4, 16),
+        sum_one.reshape(16),
+        two.reshape(3, 3, 3, 16, 32),
+        sum_two.reshape(32),
+    )
 
 
 def solution(mesh):
@@ -250,7 +300,7 @@
     if devices.shape == (2, 128):
         split = (2, 4, 4, 8)
     else:
-        split = (2, devices.shape[1], 1, 1)
+        split = (2, 1, 1, devices.shape[1])
     fine = Mesh(devices.reshape(split), ("core", "x", "y", "z"))
     cells = P("core", None, ("x", "y", "z"), None, None)
     return jax.shard_map(

time: 95 us -> 84.8 us (0.89)
  starting transfers between devices: 48.4 us -> 33.6 us
  waiting for transfers between devices: 36.2 us -> 41 us
  Pallas kernels: 4.61 us -> 7.2 us
  local copies, waits for them, and re-layouts: 3.92 us -> 1.86 us
    ppermute x16 -> x14, starting transfers between devices: 48.4 us -> 33.6 us  [the longest x3 21.8 us: pairs(): lax.ppermute(odd, axis, [(i, ((i + 1 ^ 1) - 1) % n) for i in range(n)])]
    ppermute x16 -> x14, waiting for transfers between devices: 36.2 us -> 41 us  [the longest x7 30.5 us: body(): v = v + lax.ppermute(v, axis, perm)]
    squeeze x3 -> x0, local copies, waits for them, and re-layouts: 1.11 us -> none  [the longest x1 0.58 us: body(): grad_bias_two = v[176, 32:64]]
    unnamed x15 -> x13, local copies, waits for them, and re-layouts: 2.28 us -> 1.6 us
  transfers between devices with their start and end apart: 16 -> 14, of which waited for: 14 -> 13; matrix products, arithmetic and copies ran while one was open for 0% -> 0% of each run, Pallas kernels for 0% -> 0%
where the time goes in v1:
time: 84.8 us; the launch traced here: 84.7 us
  waiting for transfers between devices  41 us (48%)
  starting transfers between devices  33.6 us (40%)
  Pallas kernels  7.2 us (8%)
  local copies, waits for them, and re-layouts  1.86 us (2%)
    ppermute x7, waiting for transfers between devices, body(): v = v + lax.ppermute(v, axis, perm)  30.5 us
    ppermute x3, starting transfers between devices, pairs(): lax.ppermute(odd, axis, [(i, ((i + 1 ^ 1) - 1) % n) for i in range(n)])  21.8 us
    ppermute x1, starting transfers between devices, body(): lax.ppermute(v, *steps[-1])  11.1 us
    ppermute x3, waiting for transfers between devices, pairs(): lax.ppermute(odd, axis, [(i, ((i + 1 ^ 1) - 1) % n) for i in range(n)])  7.8 us
    pallas_call x1, Pallas kernels, body(): call(second_kernel, (shape((32, ROWS, LANES), BF), shape((32, CELLS), BF)...  2.45 us
    pallas_call x1, Pallas kernels, body(): call(first_kernel, (shape((256, CELLS), BF), shape((128, CELLS), F32), sh...  2.42 us
    ppermute x3, waiting for transfers between devices, pairs(): first = lax.ppermute(even, axis, [(i, i ^ 1) for i in range(n)])  1.77 us
  transfers between devices with their start and end apart: 14, of which 13 were waited for; matrix products, arithmetic and copies ran while one was open for 0% of the time, Pallas kernels for 0%

profile of v1, /device:TPU:1, one launch (start us, length us, event | category | flops | bytes accessed | tf_op | source)
XLA Modules:
  0.0 84.7 jit_solution(5951496242696511437)
XLA Ops:
  0.6 0.9 %copy.26 = bf16[1,4,2,32,256]{4,3,1,2,0:T(8,128)(2,1)S(1)} copy(bf16[1,4,2,32,256]{4,3,2,1,0:T(8,128)(2,1)} %param.6) | data formatting | bytes 262144 | tf_op args[0]
  1.6 0.0 copy-start.3
  1.6 11.1 %collective-permute-start.1 = (bf16[4,32,256]{2,1,0:T(8,128)(2,1)S(1)}, bf16[4,32,256]{2,1,0:T(8,128)(2,1)S(1)}, u32[]{:S(2)}, u32[]{:S(2)}) collective-permute-start(bf16[4,32,256]{2,1,0:T(8,128)(2,1)S(1)} %get-tuple-element.35), channel_id=1, source_target_pairs={{0,127},{1,2},{2,1},{3,4},{4,3},{5,6},{6,5},{7,8},{8,7},{9,10},{10... | collective-permute-start | bytes 196616 | tf_op jit(solution)/shard_map/ppermute | solution.py:230
  12.7 0.0 collective-permute-start
  12.7 0.0 copy-start.4
  12.7 0.7 copy-done.4
  13.4 0.1 copy.21.b_ref
  13.5 0.0 copy-done.3
  13.5 0.0 copy-start
  13.6 0.1 copy.20.w_ref
  13.6 0.1 pad_add_fusion.where_ref
  13.7 0.7 collective-permute-done.1.odd_ref
  14.4 1.5 %collective-permute-done.even_ref = bf16[4,32,256]{2,1,0:T(8,128)(2,1)S(1)} collective-permute-done((bf16[4,32,256]{2,1,0:T(8,128)(2,1)S(1)}, bf16[4,32,256]{2,1,0:T(8,128)(2,1)S(1)}, u32[]{:S(2)}, u32[]{:S(2)}) %collective-permute-start) | collective-permute-done | bytes 65568 | tf_op jit(solution)/shard_map/ppermute | solution.py:229
  15.9 0.0 copy-done
  15.9 0.0 copy-start.1
  15.9 0.0 copy-start.2
  15.9 2.4 %first.1 = (bf16[256,2048]{1,0:T(8,128)(2,1)S(1)}, f32[128,2048]{1,0:T(8,128)S(1)}, bf16[16,2048]{1,0:T(8,128)(2,1)S(1)}) custom-call(s32[3]{0:T(128)S(1)} %pad_add_fusion.where_ref, bf16[4,2,32,256]{3,2,1,0:T(8,128)(2,1)S(1)} %bitcast.24, bf16[4,32,256]{2,1,0:T(8,128)(2,1)S(1)} %collective-permute-done.even_ref, ...), custom_call_target="tpu_custom_call" | custom-call | tf_op jit(solution)/shard_map/first/pallas_call | solution.py:244
  18.3 0.0 copy-start.5
  18.3 5.5 %collective-permute-start.3 = (bf16[16,2048]{1,0:T(8,128)(2,1)S(1)}, bf16[16,2048]{1,0:T(8,128)(2,1)S(1)}, u32[]{:S(2)}, u32[]{:S(2)}) collective-permute-start(bf16[16,2048]{1,0:T(8,128)(2,1)S(1)} %get-tuple-element.15.mid_ref), channel_id=1, source_target_pairs={{0,127},{1,2},{2,1},{3,4},{4,3},{5,6},{6,5},{7,8},{8,7},{9,10},{10... | collective-permute-start | bytes 196616 | tf_op jit(solution)/shard_map/ppermute | solution.py:230
  23.8 0.0 collective-permute-start.2
  23.8 0.0 copy-done.5
  23.8 0.1 copy.22.b_ref
  23.9 3.0 %collective-permute-done.3.odd_ref = bf16[16,2048]{1,0:T(8,128)(2,1)S(1)} collective-permute-done((bf16[16,2048]{1,0:T(8,128)(2,1)S(1)}, bf16[16,2048]{1,0:T(8,128)(2,1)S(1)}, u32[]{:S(2)}, u32[]{:S(2)}) %collective-permute-start.3) | collective-permute-done | bytes 65568 | tf_op jit(solution)/shard_map/ppermute | solution.py:230
  26.9 0.3 collective-permute-done.2.even_ref
  27.2 0.0 copy-done.1
  27.2 0.0 copy-done.2
  27.2 2.4 %second.1 = (bf16[32,16,128]{2,1,0:T(8,128)(2,1)}, bf16[32,2048]{1,0:T(8,128)(2,1)S(1)}, f32[160,128]{1,0:T(8,128)S(1)}) custom-call(s32[3]{0:T(128)S(1)} %pad_add_fusion.where_ref, bf16[16,2048]{1,0:T(8,128)(2,1)S(1)} %get-tuple-element.15.mid_ref, bf16[16,2048]{1,0:T(8,128)(2,1)S(1)} %collective-permute-done.2.even_ref, ...), custom_call_target="tpu_custom_call" | custom-call | tf_op jit(solution)/shard_map/second/pallas_call | solution.py:252
  29.7 5.1 %collective-permute-start.5 = (bf16[32,2048]{1,0:T(8,128)(2,1)S(1)}, bf16[32,2048]{1,0:T(8,128)(2,1)S(1)}, u32[]{:S(2)}, u32[]{:S(2)}) collective-permute-start(bf16[32,2048]{1,0:T(8,128)(2,1)S(1)} %get-tuple-element.17.mid_ref), channel_id=1, source_target_pairs={{0,127},{1,2},{2,1},{3,4},{4,3},{5,6},{6,5},{7,8},{8,7},{9,10},{10... | collective-permute-start | bytes 393224 | tf_op jit(solution)/shard_map/ppermute | solution.py:230
  34.8 0.0 collective-permute-start.4
  34.8 4.1 %collective-permute-done.5.odd_ref = bf16[32,2048]{1,0:T(8,128)(2,1)S(1)} collective-permute-done((bf16[32,2048]{1,0:T(8,128)(2,1)S(1)}, bf16[32,2048]{1,0:T(8,128)(2,1)S(1)}, u32[]{:S(2)}, u32[]{:S(2)}) %collective-permute-start.5) | collective-permute-done | bytes 131104 | tf_op jit(solution)/shard_map/ppermute | solution.py:230
  38.9 0.0 collective-permute-done.4.even_ref
  38.9 1.5 %third.1 = f32[32,128]{1,0:T(8,128)S(1)} custom-call(s32[3]{0:T(128)S(1)} %pad_add_fusion.where_ref, bf16[32,2048]{1,0:T(8,128)(2,1)S(1)} %get-tuple-element.17.mid_ref, bf16[32,2048]{1,0:T(8,128)(2,1)S(1)} %collective-permute-done.4.even_ref, bf16[32,2048]{1,0:T(8,128)(2,1)S(1)} %collective-permute-done.5.odd_ref, bf16[432,32]{1,0:T(8,128)(2,1)S(1)} %bitcast.26, ...), custom_call_target="tpu_custom_call" | custom-call | tf_op jit(solution)/shard_map/third/pallas_call | solution.py:266
  40.5 0.1 collective-permute-start.6
  40.6 3.4 %collective-permute-done.6 = f32[184,128]{1,0:T(8,128)S(1)} collective-permute-done((f32[184,128]{1,0:T(8,128)S(1)}, f32[184,128]{1,0:T(8,128)S(1)}, u32[]{:S(2)}, u32[]{:S(2)}) %collective-permute-start.6) | collective-permute-done | bytes 94240 | tf_op jit(solution)/shard_map/ppermute | solution.py:281
  44.0 0.1 collective-permute-start.7
  44.1 5.1 %collective-permute-done.7 = f32[184,128]{1,0:T(8,128)S(1)} collective-permute-done((f32[184,128]{1,0:T(8,128)S(1)}, f32[184,128]{1,0:T(8,128)S(1)}, u32[]{:S(2)}, u32[]{:S(2)}) %collective-permute-start.7) | collective-permute-done | bytes 94240 | tf_op jit(solution)/shard_map/ppermute | solution.py:281
  49.3 0.1 collective-permute-start.8
  49.4 5.6 %collective-permute-done.8 = f32[184,128]{1,0:T(8,128)S(1)} collective-permute-done((f32[184,128]{1,0:T(8,128)S(1)}, f32[184,128]{1,0:T(8,128)S(1)}, u32[]{:S(2)}, u32[]{:S(2)}) %collective-permute-start.8) | collective-permute-done | bytes 94240 | tf_op jit(solution)/shard_map/ppermute | solution.py:281
  55.0 0.1 collective-permute-start.9
  55.1 3.4 %collective-permute-done.9 = f32[184,128]{1,0:T(8,128)S(1)} collective-permute-done((f32[184,128]{1,0:T(8,128)S(1)}, f32[184,128]{1,0:T(8,128)S(1)}, u32[]{:S(2)}, u32[]{:S(2)}) %collective-permute-start.9) | collective-permute-done | bytes 94240 | tf_op jit(solution)/shard_map/ppermute | solution.py:281
  58.5 0.1 collective-permute-start.10
  58.6 4.6 %collective-permute-done.10 = f32[184,128]{1,0:T(8,128)S(1)} collective-permute-done((f32[184,128]{1,0:T(8,128)S(1)}, f32[184,128]{1,0:T(8,128)S(1)}, u32[]{:S(2)}, u32[]{:S(2)}) %collective-permute-start.10) | collective-permute-done | bytes 94240 | tf_op jit(solution)/shard_map/ppermute | solution.py:281
  63.3 0.1 collective-permute-start.11
  63.4 3.4 %collective-permute-done.11 = f32[184,128]{1,0:T(8,128)S(1)} collective-permute-done((f32[184,128]{1,0:T(8,128)S(1)}, f32[184,128]{1,0:T(8,128)S(1)}, u32[]{:S(2)}, u32[]{:S(2)}) %collective-permute-start.11) | collective-permute-done | bytes 94240 | tf_op jit(solution)/shard_map/ppermute | solution.py:281
  66.8 0.1 collective-permute-start.12
  66.9 4.9 %collective-permute-done.12 = f32[184,128]{1,0:T(8,128)S(1)} collective-permute-done((f32[184,128]{1,0:T(8,128)S(1)}, f32[184,128]{1,0:T(8,128)S(1)}, u32[]{:S(2)}, u32[]{:S(2)}) %collective-permute-start.12) | collective-permute-done | bytes 94240 | tf_op jit(solution)/shard_map/ppermute | solution.py:281
  71.8 11.1 %collective-permute-start.13 = (f32[184,128]{1,0:T(8,128)S(1)}, f32[184,128]{1,0:T(8,128)S(1)}, u32[]{:S(2)}, u32[]{:S(2)}) collective-permute-start(f32[184,128]{1,0:T(8,128)S(1)} %add.42.mine_ref), channel_id=1, source_target_pairs={{0,128},{128,0},{1,129},{129,1},{2,130},{130,2},{3,131},{131,3},{4... | collective-permute-start | bytes 282632 | tf_op jit(solution)/shard_map/ppermute | solution.py:288
  82.9 0.9 %collective-permute-done.13.other_ref = f32[184,128]{1,0:T(8,128)S(1)} collective-permute-done((f32[184,128]{1,0:T(8,128)S(1)}, f32[184,128]{1,0:T(8,128)S(1)}, u32[]{:S(2)}, u32[]{:S(2)}) %collective-permute-start.13) | collective-permute-done | bytes 94240 | tf_op jit(solution)/shard_map/ppermute | solution.py:288
  83.9 0.8 last.1
  (12 shorter events, 0.2 us)
Async XLA Ops:
  1.6 11.9 %copy-start.3 = (bf16[3,3,3,4,16]{4,3,2,1,0:T(4,128)(2,1)S(1)}, bf16[3,3,3,4,16]{4,3,2,1,0:T(4,128)(2,1)}, u32[]{:S(2)}) copy-start(bf16[3,3,3,4,16]{4,3,2,1,0:T(4,128)(2,1)} %param.7) | copy-start | bytes 10372
  1.6 12.8 %collective-permute-start.1 = (bf16[4,32,256]{2,1,0:T(8,128)(2,1)S(1)}, bf16[4,32,256]{2,1,0:T(8,128)(2,1)S(1)}, u32[]{:S(2)}, u32[]{:S(2)}) collective-permute-start(bf16[4,32,256]{2,1,0:T(8,128)(2,1)S(1)} %get-tuple-element.35), channel_id=1, source_target_pairs={{0,127},{1,2},{2,1},{3,4},{4,3},{5,6},{6,5},{7,8},{8,7},{9,10},{10... | collective-permute-start | bytes 196616 | tf_op jit(solution)/shard_map/ppermute | solution.py:230
  12.7 3.1 %collective-permute-start = (bf16[4,32,256]{2,1,0:T(8,128)(2,1)S(1)}, bf16[4,32,256]{2,1,0:T(8,128)(2,1)S(1)}, u32[]{:S(2)}, u32[]{:S(2)}) collective-permute-start(bf16[4,32,256]{2,1,0:T(8,128)(2,1)S(1)} %get-tuple-element.36), channel_id=1, source_target_pairs={{0,1},{1,0},{2,3},{3,2},{4,5},{5,4},{6,7},{7,6},{8,9},{9,8},{10,11... | collective-permute-start | bytes 196616 | tf_op jit(solution)/shard_map/ppermute | solution.py:229
  12.7 0.7 copy-start.4
  13.5 2.3 %copy-start = (bf16[1,4,2,32,256]{4,3,2,1,0:T(8,128)(2,1)S(1)}, bf16[1,4,2,32,256]{4,3,2,1,0:T(8,128)(2,1)}, u32[]{:S(2)}) copy-start(bf16[1,4,2,32,256]{4,3,2,1,0:T(8,128)(2,1)} %param.6) | copy-start | bytes 393220
  15.9 11.4 %copy-start.1 = (bf16[3,3,3,16,32]{4,3,2,1,0:T(8,128)(2,1)S(1)}, bf16[3,3,3,16,32]{4,3,2,1,0:T(8,128)(2,1)}, u32[]{:S(2)}) copy-start(bf16[3,3,3,16,32]{4,3,2,1,0:T(8,128)(2,1)} %param.9) | copy-start | bytes 82948
  15.9 11.4 %copy-start.2 = (bf16[1,32,1,16,128]{4,3,2,1,0:T(8,128)(2,1)S(1)}, bf16[1,32,1,16,128]{4,3,2,1,0:T(8,128)(2,1)}, u32[]{:S(2)}) copy-start(bf16[1,32,1,16,128]{4,3,2,1,0:T(8,128)(2,1)} %param.11) | copy-start | bytes 393220
  18.3 5.6 %copy-start.5 = (f32[32]{0:T(128)S(1)}, f32[32]{0:T(128)}, u32[]{:S(2)}) copy-start(f32[32]{0:T(128)} %param.10) | copy-start | bytes 388
  18.3 8.6 %collective-permute-start.3 = (bf16[16,2048]{1,0:T(8,128)(2,1)S(1)}, bf16[16,2048]{1,0:T(8,128)(2,1)S(1)}, u32[]{:S(2)}, u32[]{:S(2)}) collective-permute-start(bf16[16,2048]{1,0:T(8,128)(2,1)S(1)} %get-tuple-element.15.mid_ref), channel_id=1, source_target_pairs={{0,127},{1,2},{2,1},{3,4},{4,3},{5,6},{6,5},{7,8},{8,7},{9,10},{10... | collective-permute-start | bytes 196616 | tf_op jit(solution)/shard_map/ppermute | solution.py:230
  23.8 3.4 %collective-permute-start.2 = (bf16[16,2048]{1,0:T(8,128)(2,1)S(1)}, bf16[16,2048]{1,0:T(8,128)(2,1)S(1)}, u32[]{:S(2)}, u32[]{:S(2)}) collective-permute-start(bf16[16,2048]{1,0:T(8,128)(2,1)S(1)} %get-tuple-element.15.mid_ref), channel_id=1, source_target_pairs={{0,1},{1,0},{2,3},{3,2},{4,5},{5,4},{6,7},{7,6},{8,9},{9,8},{10,11... | collective-permute-start | bytes 196616 | tf_op jit(solution)/shard_map/ppermute | solution.py:229
  29.7 9.2 %collective-permute-start.5 = (bf16[32,2048]{1,0:T(8,128)(2,1)S(1)}, bf16[32,2048]{1,0:T(8,128)(2,1)S(1)}, u32[]{:S(2)}, u32[]{:S(2)}) collective-permute-start(bf16[32,2048]{1,0:T(8,128)(2,1)S(1)} %get-tuple-element.17.mid_ref), channel_id=1, source_target_pairs={{0,127},{1,2},{2,1},{3,4},{4,3},{5,6},{6,5},{7,8},{8,7},{9,10},{10... | collective-permute-start | bytes 393224 | tf_op jit(solution)/shard_map/ppermute | solution.py:230
  34.8 4.1 %collective-permute-start.4 = (bf16[32,2048]{1,0:T(8,128)(2,1)S(1)}, bf16[32,2048]{1,0:T(8,128)(2,1)S(1)}, u32[]{:S(2)}, u32[]{:S(2)}) collective-permute-start(bf16[32,2048]{1,0:T(8,128)(2,1)S(1)} %get-tuple-element.17.mid_ref), channel_id=1, source_target_pairs={{0,1},{1,0},{2,3},{3,2},{4,5},{5,4},{6,7},{7,6},{8,9},{9,8},{10,11... | collective-permute-start | bytes 393224 | tf_op jit(solution)/shard_map/ppermute | solution.py:229
  40.5 3.5 %collective-permute-start.6 = (f32[184,128]{1,0:T(8,128)S(1)}, f32[184,128]{1,0:T(8,128)S(1)}, u32[]{:S(2)}, u32[]{:S(2)}) collective-permute-start(f32[184,128]{1,0:T(8,128)S(1)} %pad_maximum_fusion), channel_id=1, source_target_pairs={{0,1},{1,0},{2,3},{3,2},{4,5},{5,4},{6,7},{7,6},{8,9},{9,8},{10,11... | collective-permute-start | bytes 282632 | tf_op jit(solution)/shard_map/ppermute | solution.py:281
  44.0 5.2 %collective-permute-start.7 = (f32[184,128]{1,0:T(8,128)S(1)}, f32[184,128]{1,0:T(8,128)S(1)}, u32[]{:S(2)}, u32[]{:S(2)}) collective-permute-start(f32[184,128]{1,0:T(8,128)S(1)} %fusion), channel_id=1, source_target_pairs={{0,2},{1,3},{2,0},{3,1},{4,6},{5,7},{6,4},{7,5},{8,10},{9,11},{10,... | collective-permute-start | bytes 282632 | tf_op jit(solution)/shard_map/ppermute | solution.py:281
  49.3 5.7 %collective-permute-start.8 = (f32[184,128]{1,0:T(8,128)S(1)}, f32[184,128]{1,0:T(8,128)S(1)}, u32[]{:S(2)}, u32[]{:S(2)}) collective-permute-start(f32[184,128]{1,0:T(8,128)S(1)} %add.37), channel_id=1, source_target_pairs={{0,7},{1,6},{2,5},{3,4},{4,3},{5,2},{6,1},{7,0},{8,15},{9,14},{10,... | collective-permute-start | bytes 282632 | tf_op jit(solution)/shard_map/ppermute | solution.py:281
  55.0 3.5 %collective-permute-start.9 = (f32[184,128]{1,0:T(8,128)S(1)}, f32[184,128]{1,0:T(8,128)S(1)}, u32[]{:S(2)}, u32[]{:S(2)}) collective-permute-start(f32[184,128]{1,0:T(8,128)S(1)} %add.38), channel_id=1, source_target_pairs={{0,8},{8,0},{16,24},{24,16},{1,9},{9,1},{17,25},{25,17},{2,10},{10... | collective-permute-start | bytes 282632 | tf_op jit(solution)/shard_map/ppermute | solution.py:281
  58.5 4.7 %collective-permute-start.10 = (f32[184,128]{1,0:T(8,128)S(1)}, f32[184,128]{1,0:T(8,128)S(1)}, u32[]{:S(2)}, u32[]{:S(2)}) collective-permute-start(f32[184,128]{1,0:T(8,128)S(1)} %add.39), channel_id=1, source_target_pairs={{0,24},{8,16},{16,8},{24,0},{1,25},{9,17},{17,9},{25,1},{2,26},{10... | collective-permute-start | bytes 282632 | tf_op jit(solution)/shard_map/ppermute | solution.py:281
  63.3 3.5 %collective-permute-start.11 = (f32[184,128]{1,0:T(8,128)S(1)}, f32[184,128]{1,0:T(8,128)S(1)}, u32[]{:S(2)}, u32[]{:S(2)}) collective-permute-start(f32[184,128]{1,0:T(8,128)S(1)} %add.40), channel_id=1, source_target_pairs={{0,32},{32,0},{64,96},{96,64},{1,33},{33,1},{65,97},{97,65},{2,34}... | collective-permute-start | bytes 282632 | tf_op jit(solution)/shard_map/ppermute | solution.py:281
  66.8 5.0 %collective-permute-start.12 = (f32[184,128]{1,0:T(8,128)S(1)}, f32[184,128]{1,0:T(8,128)S(1)}, u32[]{:S(2)}, u32[]{:S(2)}) collective-permute-start(f32[184,128]{1,0:T(8,128)S(1)} %add.41), channel_id=1, source_target_pairs={{0,96},{32,64},{64,32},{96,0},{1,97},{33,65},{65,33},{97,1},{2,98}... | collective-permute-start | bytes 282632 | tf_op jit(solution)/shard_map/ppermute | solution.py:281
  71.8 12.1 %collective-permute-start.13 = (f32[184,128]{1,0:T(8,128)S(1)}, f32[184,128]{1,0:T(8,128)S(1)}, u32[]{:S(2)}, u32[]{:S(2)}) collective-permute-start(f32[184,128]{1,0:T(8,128)S(1)} %add.42.mine_ref), channel_id=1, source_target_pairs={{0,128},{128,0},{1,129},{129,1},{2,130},{130,2},{3,131},{131,3},{4... | collective-permute-start | bytes 282632 | tf_op jit(solution)/shard_map/ppermute | solution.py:288

commit v2 on v1

--- a/solution.py
+++ b/solution.py
@@ -47,30 +47,37 @@
     return slice(h * LANES, (h + 1) * LANES)
 
 
-def place(where_ref, even_ref, odd_ref, lo_ref, hi_ref):
-    @pl.when(where_ref[0] == 1)
+def spot():
+    at = (lax.axis_index("x") * lax.axis_size("y") + lax.axis_index("y")) * lax.axis_size("z") + lax.axis_index("z")
+    return at, lax.axis_size("x") * lax.axis_size("y") * lax.axis_size("z")
+
+
+def place(even_ref, odd_ref, lo_ref, hi_ref):
+    at, count = spot()
+
+    @pl.when(lax.rem(at, 2) == 1)
     def _():
         lo_ref[...] = even_ref[...]
         hi_ref[...] = odd_ref[...]
 
-    @pl.when(where_ref[0] == 0)
+    @pl.when(lax.rem(at, 2) == 0)
     def _():
         lo_ref[...] = odd_ref[...]
         hi_ref[...] = even_ref[...]
 
-    @pl.when(where_ref[1] == 1)
+    @pl.when(at == 0)
     def _():
         lo_ref[...] = jnp.zeros_like(lo_ref)
 
-    @pl.when(where_ref[2] == 1)
+    @pl.when(at == count - 1)
     def _():
         hi_ref[...] = jnp.zeros_like(hi_ref)
 
 
 def first_kernel(
-    where_ref, vol_ref, even_ref, odd_ref, w_ref, b_ref, patches_ref, slope_ref, pooled_ref, lo_ref, hi_ref
+    vol_ref, even_ref, odd_ref, w_ref, b_ref, patches_ref, slope_ref, pooled_ref, lo_ref, hi_ref
 ):
-    place(where_ref, even_ref, odd_ref, lo_ref, hi_ref)
+    place(even_ref, odd_ref, lo_ref, hi_ref)
     cols = iota((256, 512), 1)
     pick_cols = flag(iota((256, 512), 0) == 2 * (cols & 127) + (cols >> 7) - 1)
     rows = iota((256, 128), 0)
@@ -111,9 +118,9 @@
 
 
 def second_kernel(
-    where_ref, mid_ref, even_ref, odd_ref, w_ref, b_ref, cot_ref, act_ref, grad_ref, gw_ref, x_ref, g_ref, t_ref, s_ref, lo_ref, hi_ref
+    mid_ref, even_ref, odd_ref, w_ref, b_ref, cot_ref, act_ref, grad_ref, gw_ref, x_ref, g_ref, t_ref, s_ref, lo_ref, hi_ref
 ):
-    place(where_ref, even_ref, odd_ref, lo_ref, hi_ref)
+    place(even_ref, odd_ref, lo_ref, hi_ref)
     zero = jnp.zeros((16, LANES), BF)
     for a, ref in enumerate((lo_ref, mid_ref, hi_ref)):
         for b in range(3):
@@ -158,9 +165,9 @@
     gw_ref[...] = dot(x_ref[...], g_ref[...], 1, 1)
 
 
-def third_kernel(where_ref, mid_ref, even_ref, odd_ref, w_ref, slope_ref, patches_ref, gw_ref, x_ref, t_ref, g_ref):
+def third_kernel(mid_ref, even_ref, odd_ref, w_ref, slope_ref, patches_ref, gw_two_ref, gw_ref, x_ref, t_ref, g_ref):
     x_ref[32:64, :] = mid_ref[...]
-    place(where_ref, even_ref, odd_ref, x_ref.at[64:96], x_ref.at[0:32])
+    place(even_ref, odd_ref, x_ref.at[64:96], x_ref.at[0:32])
     w = w_ref[...].astype(F32)
     weights = jnp.concatenate([w[a * 144 : (a + 1) * 144] for a in range(3)], axis=1).astype(BF)
     t_ref[...] = dot(weights, x_ref[...])
@@ -188,32 +195,32 @@
         shift = (i >> 2) * 64 + (i & 1) * 16 + ((i >> 1) & 1) * 4
         acc = acc + pltpu.roll(full[i * 16 : (i + 1) * 16], 256 - shift, 1)
     acc = jnp.where(iota((16, 256), 1) == 255, sums, acc)
-    gw_ref[0:16] = acc[:, 0:128]
-    gw_ref[16:32] = acc[:, 128:256]
+    gw_ref[...] = gw_two_ref[...]
+    for i in range(8):
+        gw_ref[i * 16 : (i + 1) * 16, 96:128] = acc[:, i * 32 : (i + 1) * 32]
 
 
 def last_kernel(mine_ref, other_ref, one_ref, bias_one_ref, two_ref, bias_two_ref):
-    v = mine_ref[...] + other_ref[...]
-    turned = jnp.transpose(jnp.concatenate([v[0:16], v[16:32]], axis=1))
+    mine = mine_ref[...]
+    other = other_ref[...]
+    low = lax.axis_index("core") == 0
+    v = jnp.concatenate([jnp.where(low, mine, other), jnp.where(low, other, mine)], axis=0)
+    turned = jnp.transpose(jnp.concatenate([v[i * 16 : (i + 1) * 16, 96:128] for i in range(8)], axis=1))
     for a in range(3):
         for b in range(3):
             k = a * 3 + b
             for e in range(3):
                 row = a * 64 + e * 16 + b * 4
                 one_ref[k * 3 + e] = turned[row : row + 4]
-                two_ref[k * 3 + e] = v[32 + k * 16 : 48 + k * 16, e * 32 : (e + 1) * 32]
+                two_ref[k * 3 + e] = v[k * 16 : (k + 1) * 16, e * 32 : (e + 1) * 32]
     bias_one_ref[...] = turned[255:256]
-    bias_two_ref[...] = v[176:177, 32:64]
-
-
-def call(kernel, outs, scratch, name, where=True):
-    count = {"first": 6, "second": 7, "third": 7, "last": 2}[name]
-    vmem = pl.BlockSpec(memory_space=pltpu.VMEM)
-    specs = [pl.BlockSpec(memory_space=pltpu.SMEM) if where and i == 0 else vmem for i in range(count)]
+    bias_two_ref[...] = v[144:145, 32:64]
+
+
+def call(kernel, outs, scratch, name):
     return pl.pallas_call(
         kernel,
         out_shape=outs,
-        in_specs=specs,
         scratch_shapes=scratch,
         compiler_params=pltpu.CompilerParams(vmem_limit_bytes=VMEM_LIMIT),
         name=name,
@@ -236,7 +243,6 @@
     vol = volumes[0]
     place_at = lax.axis_index(depth)
     odd = place_at % 2
-    where = jnp.stack([odd, place_at == 0, place_at == lax.axis_size(depth) - 1]).astype(jnp.int32)
     head, tail = vol[:, 0], vol[:, 1]
     even_part, odd_part = pairs(jnp.where(odd == 1, head, tail), jnp.where(odd == 1, tail, head), depth)
     base = jnp.pad(conv_one.astype(F32).transpose(4, 0, 2, 1, 3), ((0, 0), (0, 1), (0, 1), (0, 1), (0, 0))).reshape(16, 256)
@@ -246,7 +252,7 @@
         (shape((256, CELLS), BF), shape((128, CELLS), F32), shape((16, CELLS), BF)),
         [plane, plane],
         "first",
-    )(where, vol, even_part, odd_part, base, bias_one.reshape(16, 1))
+    )(vol, even_part, odd_part, base, bias_one.reshape(16, 1))
     even_part, odd_part = pairs(pooled, pooled, depth)
     conv_flat = conv_two.reshape(432, 32)
     act, grad, gw_two = call(
@@ -261,31 +267,32 @@
             pltpu.VMEM((16, CELLS), BF),
         ],
         "second",
-    )(where, pooled, even_part, odd_part, conv_flat, bias_two.reshape(32, 1), cotangent.reshape(32, ROWS, LANES))
+    )(pooled, even_part, odd_part, conv_flat, bias_two.reshape(32, 1), cotangent.reshape(32, ROWS, LANES))
     even_part, odd_part = pairs(grad, grad, depth)
-    gw_one = call(
+    v = call(
         third_kernel,
-        shape((32, 128), F32),
+        shape((160, 128), F32),
         [pltpu.VMEM((96, CELLS), BF), pltpu.VMEM((144, CELLS), F32), pltpu.VMEM((128, CELLS), BF)],
         "third",
-    )(where, grad, even_part, odd_part, conv_flat, slopes, patches)
-    v = jnp.concatenate([gw_one, gw_two[:152]], axis=0)
-    n = {axis: lax.axis_size(axis) for axis in ("z", "y", "x", "core")}
+    )(grad, even_part, odd_part, conv_flat, slopes, patches, gw_two)
+    low = lax.axis_index("core") == 0
+    swap = [(0, 1), (1, 0)]
+    v = jnp.where(low, v[:80], v[80:]) + lax.ppermute(jnp.where(low, v[80:], v[:80]), "core", swap)
+    n = {axis: lax.axis_size(axis) for axis in ("z", "y", "x")}
     steps = [
         (axis, [(i, i ^ 2 if d == 4 and size == 8 else i ^ (d - 1)) for i in range(size)])
         for axis, size in n.items()
         for d in (2, 4, 8)
         if d <= size
     ]
-    for axis, perm in steps[:-1]:
+    for axis, perm in steps:
         v = v + lax.ppermute(v, axis, perm)
     one, sum_one, two, sum_two = call(
         last_kernel,
         (shape((27, 4, 16), F32), shape((1, 16), F32), shape((27, 16, 32), F32), shape((1, 32), F32)),
         [],
         "last",
-        where=False,
-    )(v, lax.ppermute(v, *steps[-1]))
+    )(v, lax.ppermute(v, "core", swap))
     return (
         act.reshape(1, 32, 1, ROWS, LANES),
         one.reshape(3, 3, 3, 4, 16),

time: 84.8 us -> 78.9 us (0.930)
  waiting for transfers between devices: 41 us -> 36.1 us
  Pallas kernels: 7.2 us -> 5.65 us
    ppermute x7, waiting for transfers between devices: 30.5 us -> 24.7 us  [body(): v = v + lax.ppermute(v, axis, perm)]
    ppermute x1 -> x2, starting transfers between devices: 11.1 us -> 12.2 us  [the longest x1 7.95 us: body(): lax.ppermute(v, 'core', swap)]
    ppermute x1 -> x2, waiting for transfers between devices: 0.94 us -> 1.74 us  [the longest x1 0.87 us: body(): lax.ppermute(jnp.where(low, v[80:], v[:80]), 'core', swap)]
  transfers between devices with their start and end apart: 14 -> 15, of which waited for: 13 -> 14; matrix products, arithmetic and copies ran while one was open for 0% -> 0% of each run, Pallas kernels for 0% -> 0%
where the time goes in v2:
time: 78.9 us; the launch traced here: 78.8 us
  waiting for transfers between devices  36.1 us (46%)
  starting transfers between devices  34.3 us (43%)
  Pallas kernels  5.65 us (7%)
  local copies, waits for them, and re-layouts  1.85 us (2%)
    ppermute x7, waiting for transfers between devices, body(): v = v + lax.ppermute(v, axis, perm)  24.7 us
    ppermute x3, starting transfers between devices, pairs(): lax.ppermute(odd, axis, [(i, ((i + 1 ^ 1) - 1) % n) for i in range(n)])  21.9 us
    ppermute x1, starting transfers between devices, body(): lax.ppermute(v, 'core', swap)  7.95 us
    ppermute x3, waiting for transfers between devices, pairs(): lax.ppermute(odd, axis, [(i, ((i + 1 ^ 1) - 1) % n) for i in range(n)])  7.83 us
    ppermute x1, starting transfers between devices, body(): lax.ppermute(jnp.where(low, v[80:], v[:80]), 'core', swap)  4.22 us
    pallas_call x1, Pallas kernels, body(): call(second_kernel, (shape((32, ROWS, LANES), BF), shape((32, CELLS), BF)...  1.89 us
    pallas_call x1, Pallas kernels, body(): call(first_kernel, (shape((256, CELLS), BF), shape((128, CELLS), F32), sh...  1.84 us
    ppermute x3, waiting for transfers between devices, pairs(): first = lax.ppermute(even, axis, [(i, i ^ 1) for i in range(n)])  1.81 us
  transfers between devices with their start and end apart: 15, of which 14 were waited for; matrix products, arithmetic and copies ran while one was open for 0% of the time, Pallas kernels for 0%

profile of v2, /device:TPU:1, one launch (start us, length us, event | category | flops | bytes accessed | tf_op | source)
XLA Modules:
  0.0 78.8 jit_solution(11924256613731390487)
XLA Ops:
  0.6 0.9 %copy.26 = bf16[1,4,2,32,256]{4,3,1,2,0:T(8,128)(2,1)S(1)} copy(bf16[1,4,2,32,256]{4,3,2,1,0:T(8,128)(2,1)} %param.6) | data formatting | bytes 262144 | tf_op args[0]
  1.6 0.0 copy-start.3
  1.6 11.1 %collective-permute-start.1 = (bf16[4,32,256]{2,1,0:T(8,128)(2,1)S(1)}, bf16[4,32,256]{2,1,0:T(8,128)(2,1)S(1)}, u32[]{:S(2)}, u32[]{:S(2)}) collective-permute-start(bf16[4,32,256]{2,1,0:T(8,128)(2,1)S(1)} %get-tuple-element.35), channel_id=1, source_target_pairs={{0,127},{1,2},{2,1},{3,4},{4,3},{5,6},{6,5},{7,8},{8,7},{9,10},{10... | collective-permute-start | bytes 196616 | tf_op jit(solution)/shard_map/ppermute | solution.py:237
  12.7 0.0 copy-start.4
  12.7 0.0 collective-permute-start
  12.7 0.7 copy-done.4
  13.4 0.1 copy.21.b_ref
  13.5 0.0 copy-done.3
  13.5 0.0 copy-start
  13.6 0.1 copy.20.w_ref
  13.6 0.8 collective-permute-done.1.odd_ref
  14.4 1.5 %collective-permute-done.even_ref = bf16[4,32,256]{2,1,0:T(8,128)(2,1)S(1)} collective-permute-done((bf16[4,32,256]{2,1,0:T(8,128)(2,1)S(1)}, bf16[4,32,256]{2,1,0:T(8,128)(2,1)S(1)}, u32[]{:S(2)}, u32[]{:S(2)}) %collective-permute-start) | collective-permute-done | bytes 65568 | tf_op jit(solution)/shard_map/ppermute | solution.py:236
  15.9 0.0 copy-done
  15.9 0.0 copy-start.1
  15.9 0.0 copy-start.2
  15.9 1.8 %first.1 = (bf16[256,2048]{1,0:T(8,128)(2,1)S(1)}, f32[128,2048]{1,0:T(8,128)S(1)}, bf16[16,2048]{1,0:T(8,128)(2,1)S(1)}) custom-call(bf16[4,2,32,256]{3,2,1,0:T(8,128)(2,1)S(1)} %bitcast.21, bf16[4,32,256]{2,1,0:T(8,128)(2,1)S(1)} %collective-permute-done.even_ref, bf16[4,32,256]{2,1,0:T(8,128)(2,1)S(1)} %collective-permute-done.1.odd_ref, ...), custom_call_target="tpu_custom_call" | custom-call | tf_op jit(solution)/shard_map/first/pallas_call | solution.py:250
  17.7 0.0 copy-start.5
  17.7 5.6 %collective-permute-start.3 = (bf16[16,2048]{1,0:T(8,128)(2,1)S(1)}, bf16[16,2048]{1,0:T(8,128)(2,1)S(1)}, u32[]{:S(2)}, u32[]{:S(2)}) collective-permute-start(bf16[16,2048]{1,0:T(8,128)(2,1)S(1)} %get-tuple-element.15.mid_ref), channel_id=1, source_target_pairs={{0,127},{1,2},{2,1},{3,4},{4,3},{5,6},{6,5},{7,8},{8,7},{9,10},{10... | collective-permute-start | bytes 196616 | tf_op jit(solution)/shard_map/ppermute | solution.py:237
  23.3 0.0 collective-permute-start.2
  23.3 0.0 copy-done.5
  23.3 0.1 copy.22.b_ref
  23.4 3.0 %collective-permute-done.3.odd_ref = bf16[16,2048]{1,0:T(8,128)(2,1)S(1)} collective-permute-done((bf16[16,2048]{1,0:T(8,128)(2,1)S(1)}, bf16[16,2048]{1,0:T(8,128)(2,1)S(1)}, u32[]{:S(2)}, u32[]{:S(2)}) %collective-permute-start.3) | collective-permute-done | bytes 65568 | tf_op jit(solution)/shard_map/ppermute | solution.py:237
  26.4 0.3 collective-permute-done.2.even_ref
  26.7 0.0 copy-done.1
  26.7 0.0 copy-done.2
  26.7 1.9 %second.1 = (bf16[32,16,128]{2,1,0:T(8,128)(2,1)}, bf16[32,2048]{1,0:T(8,128)(2,1)S(1)}, f32[160,128]{1,0:T(8,128)S(1)}) custom-call(bf16[16,2048]{1,0:T(8,128)(2,1)S(1)} %get-tuple-element.15.mid_ref, bf16[16,2048]{1,0:T(8,128)(2,1)S(1)} %collective-permute-done.2.even_ref, bf16[16,2048]{1,0:T(8,128)(2,1)S(1)} %collective-permute-done.3.odd_ref, ...), custom_call_target="tpu_custom_call" | custom-call | tf_op jit(solution)/shard_map/second/pallas_call | solution.py:258
  28.6 5.2 %collective-permute-start.5 = (bf16[32,2048]{1,0:T(8,128)(2,1)S(1)}, bf16[32,2048]{1,0:T(8,128)(2,1)S(1)}, u32[]{:S(2)}, u32[]{:S(2)}) collective-permute-start(bf16[32,2048]{1,0:T(8,128)(2,1)S(1)} %get-tuple-element.17.mid_ref), channel_id=1, source_target_pairs={{0,127},{1,2},{2,1},{3,4},{4,3},{5,6},{6,5},{7,8},{8,7},{9,10},{10... | collective-permute-start | bytes 393224 | tf_op jit(solution)/shard_map/ppermute | solution.py:237
  33.8 0.0 collective-permute-start.4
  33.8 4.1 %collective-permute-done.5.odd_ref = bf16[32,2048]{1,0:T(8,128)(2,1)S(1)} collective-permute-done((bf16[32,2048]{1,0:T(8,128)(2,1)S(1)}, bf16[32,2048]{1,0:T(8,128)(2,1)S(1)}, u32[]{:S(2)}, u32[]{:S(2)}) %collective-permute-start.5) | collective-permute-done | bytes 131104 | tf_op jit(solution)/shard_map/ppermute | solution.py:237
  37.8 0.0 collective-permute-done.4.even_ref
  37.8 1.0 %third.1 = f32[160,128]{1,0:T(8,128)S(1)} custom-call(bf16[32,2048]{1,0:T(8,128)(2,1)S(1)} %get-tuple-element.17.mid_ref, bf16[32,2048]{1,0:T(8,128)(2,1)S(1)} %collective-permute-done.4.even_ref, bf16[32,2048]{1,0:T(8,128)(2,1)S(1)} %collective-permute-done.5.odd_ref, bf16[432,32]{1,0:T(8,128)(2,1)S(1)} %bitcast.23, ...), custom_call_target="tpu_custom_call" | custom-call | tf_op jit(solution)/shard_map/third/pallas_call | solution.py:272
  38.9 4.2 %collective-permute-start.6 = (f32[80,128]{1,0:T(8,128)S(1)}, f32[80,128]{1,0:T(8,128)S(1)}, u32[]{:S(2)}, u32[]{:S(2)}) collective-permute-start(f32[80,128]{1,0:T(8,128)S(1)} %slice_select_fusion), channel_id=1, source_target_pairs={{0,128},{128,0},{1,129},{129,1},{2,130},{130,2},{3,131},{131,3},{4... | collective-permute-start | bytes 122888 | tf_op jit(solution)/shard_map/ppermute | solution.py:280
  43.1 0.9 %collective-permute-done.6 = f32[80,128]{1,0:T(8,128)S(1)} collective-permute-done((f32[80,128]{1,0:T(8,128)S(1)}, f32[80,128]{1,0:T(8,128)S(1)}, u32[]{:S(2)}, u32[]{:S(2)}) %collective-permute-start.6) | collective-permute-done | bytes 40992 | tf_op jit(solution)/shard_map/ppermute | solution.py:280
  44.0 0.1 collective-permute-start.7
  44.1 2.8 %collective-permute-done.7 = f32[80,128]{1,0:T(8,128)S(1)} collective-permute-done((f32[80,128]{1,0:T(8,128)S(1)}, f32[80,128]{1,0:T(8,128)S(1)}, u32[]{:S(2)}, u32[]{:S(2)}) %collective-permute-start.7) | collective-permute-done | bytes 40992 | tf_op jit(solution)/shard_map/ppermute | solution.py:289
  46.9 0.0 collective-permute-start.8
  46.9 3.9 %collective-permute-done.8 = f32[80,128]{1,0:T(8,128)S(1)} collective-permute-done((f32[80,128]{1,0:T(8,128)S(1)}, f32[80,128]{1,0:T(8,128)S(1)}, u32[]{:S(2)}, u32[]{:S(2)}) %collective-permute-start.8) | collective-permute-done | bytes 40992 | tf_op jit(solution)/shard_map/ppermute | solution.py:289
  50.8 0.0 collective-permute-start.9
  50.9 4.1 %collective-permute-done.9 = f32[80,128]{1,0:T(8,128)S(1)} collective-permute-done((f32[80,128]{1,0:T(8,128)S(1)}, f32[80,128]{1,0:T(8,128)S(1)}, u32[]{:S(2)}, u32[]{:S(2)}) %collective-permute-start.9) | collective-permute-done | bytes 40992 | tf_op jit(solution)/shard_map/ppermute | solution.py:289
  54.9 0.0 collective-permute-start.10
  54.9 3.1 %collective-permute-done.10 = f32[80,128]{1,0:T(8,128)S(1)} collective-permute-done((f32[80,128]{1,0:T(8,128)S(1)}, f32[80,128]{1,0:T(8,128)S(1)}, u32[]{:S(2)}, u32[]{:S(2)}) %collective-permute-start.10) | collective-permute-done | bytes 40992 | tf_op jit(solution)/shard_map/ppermute | solution.py:289
  58.1 0.0 collective-permute-start.11
  58.1 4.1 %collective-permute-done.11 = f32[80,128]{1,0:T(8,128)S(1)} collective-permute-done((f32[80,128]{1,0:T(8,128)S(1)}, f32[80,128]{1,0:T(8,128)S(1)}, u32[]{:S(2)}, u32[]{:S(2)}) %collective-permute-start.11) | collective-permute-done | bytes 40992 | tf_op jit(solution)/shard_map/ppermute | solution.py:289
  62.1 0.0 collective-permute-start.12
  62.2 2.8 %collective-permute-done.12 = f32[80,128]{1,0:T(8,128)S(1)} collective-permute-done((f32[80,128]{1,0:T(8,128)S(1)}, f32[80,128]{1,0:T(8,128)S(1)}, u32[]{:S(2)}, u32[]{:S(2)}) %collective-permute-start.12) | collective-permute-done | bytes 40992 | tf_op jit(solution)/shard_map/ppermute | solution.py:289
  65.0 0.2 collective-permute-start.13
  65.2 3.9 %collective-permute-done.13 = f32[80,128]{1,0:T(8,128)S(1)} collective-permute-done((f32[80,128]{1,0:T(8,128)S(1)}, f32[80,128]{1,0:T(8,128)S(1)}, u32[]{:S(2)}, u32[]{:S(2)}) %collective-permute-start.13) | collective-permute-done | bytes 40992 | tf_op jit(solution)/shard_map/ppermute | solution.py:289
  69.1 8.0 %collective-permute-start.14 = (f32[80,128]{1,0:T(8,128)S(1)}, f32[80,128]{1,0:T(8,128)S(1)}, u32[]{:S(2)}, u32[]{:S(2)}) collective-permute-start(f32[80,128]{1,0:T(8,128)S(1)} %add.46.mine_ref), channel_id=1, source_target_pairs={{0,128},{128,0},{1,129},{129,1},{2,130},{130,2},{3,131},{131,3},{4... | collective-permute-start | bytes 122888 | tf_op jit(solution)/shard_map/ppermute | solution.py:295
  77.0 0.9 %collective-permute-done.14.other_ref = f32[80,128]{1,0:T(8,128)S(1)} collective-permute-done((f32[80,128]{1,0:T(8,128)S(1)}, f32[80,128]{1,0:T(8,128)S(1)}, u32[]{:S(2)}, u32[]{:S(2)}) %collective-permute-start.14) | collective-permute-done | bytes 40992 | tf_op jit(solution)/shard_map/ppermute | solution.py:295
  77.9 0.9 %last.1 = (f32[27,4,16]{2,1,0:T(4,128)}, f32[1,16]{1,0:T(1,128)}, f32[27,16,32]{2,1,0:T(8,128)}, f32[1,32]{1,0:T(1,128)}) custom-call(f32[80,128]{1,0:T(8,128)S(1)} %add.46.mine_ref, f32[80,128]{1,0:T(8,128)S(1)} %collective-permute-done.14.other_ref), custom_call_target="tpu_custom_call" | custom-call | tf_op jit(solution)/shard_map/last/pallas_call | solution.py:290
  (12 shorter events, 0.1 us)
Async XLA Ops:
  1.6 11.9 %copy-start.3 = (bf16[3,3,3,4,16]{4,3,2,1,0:T(4,128)(2,1)S(1)}, bf16[3,3,3,4,16]{4,3,2,1,0:T(4,128)(2,1)}, u32[]{:S(2)}) copy-start(bf16[3,3,3,4,16]{4,3,2,1,0:T(4,128)(2,1)} %param.7) | copy-start | bytes 10372
  1.6 12.8 %collective-permute-start.1 = (bf16[4,32,256]{2,1,0:T(8,128)(2,1)S(1)}, bf16[4,32,256]{2,1,0:T(8,128)(2,1)S(1)}, u32[]{:S(2)}, u32[]{:S(2)}) collective-permute-start(bf16[4,32,256]{2,1,0:T(8,128)(2,1)S(1)} %get-tuple-element.35), channel_id=1, source_target_pairs={{0,127},{1,2},{2,1},{3,4},{4,3},{5,6},{6,5},{7,8},{8,7},{9,10},{10... | collective-permute-start | bytes 196616 | tf_op jit(solution)/shard_map/ppermute | solution.py:237
  12.7 0.7 copy-start.4
  12.7 3.1 %collective-permute-start = (bf16[4,32,256]{2,1,0:T(8,128)(2,1)S(1)}, bf16[4,32,256]{2,1,0:T(8,128)(2,1)S(1)}, u32[]{:S(2)}, u32[]{:S(2)}) collective-permute-start(bf16[4,32,256]{2,1,0:T(8,128)(2,1)S(1)} %get-tuple-element.36), channel_id=1, source_target_pairs={{0,1},{1,0},{2,3},{3,2},{4,5},{5,4},{6,7},{7,6},{8,9},{9,8},{10,11... | collective-permute-start | bytes 196616 | tf_op jit(solution)/shard_map/ppermute | solution.py:236
  13.5 2.3 %copy-start = (bf16[1,4,2,32,256]{4,3,2,1,0:T(8,128)(2,1)S(1)}, bf16[1,4,2,32,256]{4,3,2,1,0:T(8,128)(2,1)}, u32[]{:S(2)}) copy-start(bf16[1,4,2,32,256]{4,3,2,1,0:T(8,128)(2,1)} %param.6) | copy-start | bytes 393220
  15.9 10.8 %copy-start.1 = (bf16[3,3,3,16,32]{4,3,2,1,0:T(8,128)(2,1)S(1)}, bf16[3,3,3,16,32]{4,3,2,1,0:T(8,128)(2,1)}, u32[]{:S(2)}) copy-start(bf16[3,3,3,16,32]{4,3,2,1,0:T(8,128)(2,1)} %param.9) | copy-start | bytes 82948
  15.9 10.8 %copy-start.2 = (bf16[1,32,1,16,128]{4,3,2,1,0:T(8,128)(2,1)S(1)}, bf16[1,32,1,16,128]{4,3,2,1,0:T(8,128)(2,1)}, u32[]{:S(2)}) copy-start(bf16[1,32,1,16,128]{4,3,2,1,0:T(8,128)(2,1)} %param.11) | copy-start | bytes 393220
  17.7 5.6 %copy-start.5 = (f32[32]{0:T(128)S(1)}, f32[32]{0:T(128)}, u32[]{:S(2)}) copy-start(f32[32]{0:T(128)} %param.10) | copy-start | bytes 388
  17.7 8.6 %collective-permute-start.3 = (bf16[16,2048]{1,0:T(8,128)(2,1)S(1)}, bf16[16,2048]{1,0:T(8,128)(2,1)S(1)}, u32[]{:S(2)}, u32[]{:S(2)}) collective-permute-start(bf16[16,2048]{1,0:T(8,128)(2,1)S(1)} %get-tuple-element.15.mid_ref), channel_id=1, source_target_pairs={{0,127},{1,2},{2,1},{3,4},{4,3},{5,6},{6,5},{7,8},{8,7},{9,10},{10... | collective-permute-start | bytes 196616 | tf_op jit(solution)/shard_map/ppermute | solution.py:237
  23.3 3.4 %collective-permute-start.2 = (bf16[16,2048]{1,0:T(8,128)(2,1)S(1)}, bf16[16,2048]{1,0:T(8,128)(2,1)S(1)}, u32[]{:S(2)}, u32[]{:S(2)}) collective-permute-start(bf16[16,2048]{1,0:T(8,128)(2,1)S(1)} %get-tuple-element.15.mid_ref), channel_id=1, source_target_pairs={{0,1},{1,0},{2,3},{3,2},{4,5},{5,4},{6,7},{7,6},{8,9},{9,8},{10,11... | collective-permute-start | bytes 196616 | tf_op jit(solution)/shard_map/ppermute | solution.py:236
  28.6 9.2 %collective-permute-start.5 = (bf16[32,2048]{1,0:T(8,128)(2,1)S(1)}, bf16[32,2048]{1,0:T(8,128)(2,1)S(1)}, u32[]{:S(2)}, u32[]{:S(2)}) collective-permute-start(bf16[32,2048]{1,0:T(8,128)(2,1)S(1)} %get-tuple-element.17.mid_ref), channel_id=1, source_target_pairs={{0,127},{1,2},{2,1},{3,4},{4,3},{5,6},{6,5},{7,8},{8,7},{9,10},{10... | collective-permute-start | bytes 393224 | tf_op jit(solution)/shard_map/ppermute | solution.py:237
  33.8 4.1 %collective-permute-start.4 = (bf16[32,2048]{1,0:T(8,128)(2,1)S(1)}, bf16[32,2048]{1,0:T(8,128)(2,1)S(1)}, u32[]{:S(2)}, u32[]{:S(2)}) collective-permute-start(bf16[32,2048]{1,0:T(8,128)(2,1)S(1)} %get-tuple-element.17.mid_ref), channel_id=1, source_target_pairs={{0,1},{1,0},{2,3},{3,2},{4,5},{5,4},{6,7},{7,6},{8,9},{9,8},{10,11... | collective-permute-start | bytes 393224 | tf_op jit(solution)/shard_map/ppermute | solution.py:236
  38.9 5.1 %collective-permute-start.6 = (f32[80,128]{1,0:T(8,128)S(1)}, f32[80,128]{1,0:T(8,128)S(1)}, u32[]{:S(2)}, u32[]{:S(2)}) collective-permute-start(f32[80,128]{1,0:T(8,128)S(1)} %slice_select_fusion), channel_id=1, source_target_pairs={{0,128},{128,0},{1,129},{129,1},{2,130},{130,2},{3,131},{131,3},{4... | collective-permute-start | bytes 122888 | tf_op jit(solution)/shard_map/ppermute | solution.py:280
  44.0 2.9 %collective-permute-start.7 = (f32[80,128]{1,0:T(8,128)S(1)}, f32[80,128]{1,0:T(8,128)S(1)}, u32[]{:S(2)}, u32[]{:S(2)}) collective-permute-start(f32[80,128]{1,0:T(8,128)S(1)} %select_add_fusion), channel_id=1, source_target_pairs={{0,1},{1,0},{2,3},{3,2},{4,5},{5,4},{6,7},{7,6},{8,9},{9,8},{10,11... | collective-permute-start | bytes 122888 | tf_op jit(solution)/shard_map/ppermute | solution.py:289
  46.9 3.9 %collective-permute-start.8 = (f32[80,128]{1,0:T(8,128)S(1)}, f32[80,128]{1,0:T(8,128)S(1)}, u32[]{:S(2)}, u32[]{:S(2)}) collective-permute-start(f32[80,128]{1,0:T(8,128)S(1)} %add.40), channel_id=1, source_target_pairs={{0,2},{1,3},{2,0},{3,1},{4,6},{5,7},{6,4},{7,5},{8,10},{9,11},{10,... | collective-permute-start | bytes 122888 | tf_op jit(solution)/shard_map/ppermute | solution.py:289
  50.8 4.1 %collective-permute-start.9 = (f32[80,128]{1,0:T(8,128)S(1)}, f32[80,128]{1,0:T(8,128)S(1)}, u32[]{:S(2)}, u32[]{:S(2)}) collective-permute-start(f32[80,128]{1,0:T(8,128)S(1)} %add.41), channel_id=1, source_target_pairs={{0,7},{1,6},{2,5},{3,4},{4,3},{5,2},{6,1},{7,0},{8,15},{9,14},{10,... | collective-permute-start | bytes 122888 | tf_op jit(solution)/shard_map/ppermute | solution.py:289
  54.9 3.1 %collective-permute-start.10 = (f32[80,128]{1,0:T(8,128)S(1)}, f32[80,128]{1,0:T(8,128)S(1)}, u32[]{:S(2)}, u32[]{:S(2)}) collective-permute-start(f32[80,128]{1,0:T(8,128)S(1)} %add.42), channel_id=1, source_target_pairs={{0,8},{8,0},{16,24},{24,16},{1,9},{9,1},{17,25},{25,17},{2,10},{10... | collective-permute-start | bytes 122888 | tf_op jit(solution)/shard_map/ppermute | solution.py:289
  58.1 4.1 %collective-permute-start.11 = (f32[80,128]{1,0:T(8,128)S(1)}, f32[80,128]{1,0:T(8,128)S(1)}, u32[]{:S(2)}, u32[]{:S(2)}) collective-permute-start(f32[80,128]{1,0:T(8,128)S(1)} %add.43), channel_id=1, source_target_pairs={{0,24},{8,16},{16,8},{24,0},{1,25},{9,17},{17,9},{25,1},{2,26},{10... | collective-permute-start | bytes 122888 | tf_op jit(solution)/shard_map/ppermute | solution.py:289
  62.1 2.9 %collective-permute-start.12 = (f32[80,128]{1,0:T(8,128)S(1)}, f32[80,128]{1,0:T(8,128)S(1)}, u32[]{:S(2)}, u32[]{:S(2)}) collective-permute-start(f32[80,128]{1,0:T(8,128)S(1)} %add.44), channel_id=1, source_target_pairs={{0,32},{32,0},{64,96},{96,64},{1,33},{33,1},{65,97},{97,65},{2,34}... | collective-permute-start | bytes 122888 | tf_op jit(solution)/shard_map/ppermute | solution.py:289
  65.0 4.1 %collective-permute-start.13 = (f32[80,128]{1,0:T(8,128)S(1)}, f32[80,128]{1,0:T(8,128)S(1)}, u32[]{:S(2)}, u32[]{:S(2)}) collective-permute-start(f32[80,128]{1,0:T(8,128)S(1)} %add.45), channel_id=1, source_target_pairs={{0,96},{32,64},{64,32},{96,0},{1,97},{33,65},{65,33},{97,1},{2,98}... | collective-permute-start | bytes 122888 | tf_op jit(solution)/shard_map/ppermute | solution.py:289
  69.1 8.8 %collective-permute-start.14 = (f32[80,128]{1,0:T(8,128)S(1)}, f32[80,128]{1,0:T(8,128)S(1)}, u32[]{:S(2)}, u32[]{:S(2)}) collective-permute-start(f32[80,128]{1,0:T(8,128)S(1)} %add.46.mine_ref), channel_id=1, source_target_pairs={{0,128},{128,0},{1,129},{129,1},{2,130},{130,2},{3,131},{131,3},{4... | collective-permute-start | bytes 122888 | tf_op jit(solution)/shard_map/ppermute | solution.py:295

commit v3 on v2

--- a/solution.py
+++ b/solution.py
@@ -12,6 +12,7 @@
 ROWS = 16
 LANES = 128
 CELLS = ROWS * LANES
+GROUPS = ((1, 32), (8, 96), (24, 2), (7,))
 VMEM_LIMIT = 40 * 1024 * 1024
 
 
@@ -52,42 +53,65 @@
     return at, lax.axis_size("x") * lax.axis_size("y") * lax.axis_size("z")
 
 
-def place(even_ref, odd_ref, lo_ref, hi_ref):
+def place(even_ref, odd_ref, lo_ref, hi_ref, step=1):
     at, count = spot()
-
-    @pl.when(lax.rem(at, 2) == 1)
+    upper = lax.rem(at // step, 2) == 1
+
+    @pl.when(upper)
     def _():
         lo_ref[...] = even_ref[...]
         hi_ref[...] = odd_ref[...]
 
-    @pl.when(lax.rem(at, 2) == 0)
+    @pl.when(jnp.logical_not(upper))
     def _():
         lo_ref[...] = odd_ref[...]
         hi_ref[...] = even_ref[...]
 
-    @pl.when(at == 0)
+    @pl.when(at < step)
     def _():
         lo_ref[...] = jnp.zeros_like(lo_ref)
 
-    @pl.when(at == count - 1)
+    @pl.when(at >= count - step)
     def _():
         hi_ref[...] = jnp.zeros_like(hi_ref)
+
+
+def pack_kernel(vol_ref, cot_ref, even_ref, odd_ref):
+    cot = cot_ref[...].reshape(512, LANES)
+    even_ref[0:512] = cot
+    odd_ref[0:512] = cot
+    at, _ = spot()
+    upper = lax.rem(at, 2) == 1
+
+    def put(even, odd):
+        for ref, d in ((even_ref, even), (odd_ref, odd)):
+            plane = vol_ref[:, d].reshape(128, 256)
+            ref[512:640] = plane[:, 0:128]
+            ref[640:768] = plane[:, 128:256]
+
+    @pl.when(upper)
+    def _():
+        put(0, 1)
+
+    @pl.when(jnp.logical_not(upper))
+    def _():
+        put(1, 0)
 
 
 def first_kernel(
     vol_ref, even_ref, odd_ref, w_ref, b_ref, patches_ref, slope_ref, pooled_ref, lo_ref, hi_ref
 ):
-    place(even_ref, odd_ref, lo_ref, hi_ref)
+    place(even_ref.at[512:768], odd_ref.at[512:768], lo_ref, hi_ref)
     cols = iota((256, 512), 1)
     pick_cols = flag(iota((256, 512), 0) == 2 * (cols & 127) + (cols >> 7) - 1)
     rows = iota((256, 128), 0)
     src = iota((256, 128), 1)
     pick_rows = flag(((rows & 3) == (src >> 5)) & ((src & 31) == 2 * (rows >> 4) + ((rows >> 2) & 3) - 1))
     planes = [
-        lo_ref[...].reshape(128, 256),
+        jnp.concatenate([lo_ref[0:128], lo_ref[128:256]], axis=1),
         vol_ref[:, 0].reshape(128, 256),
         vol_ref[:, 1].reshape(128, 256),
-        hi_ref[...].reshape(128, 256),
+        jnp.concatenate([hi_ref[0:128], hi_ref[128:256]], axis=1),
     ]
     for a in range(4):
         wide = dot(planes[a], pick_cols).astype(BF)
@@ -118,17 +142,20 @@
 
 
 def second_kernel(
-    mid_ref, even_ref, odd_ref, w_ref, b_ref, cot_ref, act_ref, grad_ref, gw_ref, x_ref, g_ref, t_ref, s_ref, lo_ref, hi_ref
+    mid_ref, near_even_ref, near_odd_ref, far_even_ref, far_odd_ref, w_ref, b_ref, cot_ref, cot_even_ref, cot_odd_ref,
+    slope_ref, patches_ref, act_ref, gw_ref, p_ref, x_ref, g_ref, t_ref, s_ref, cot_lo_ref, cot_hi_ref, u_ref, up_ref, one_ref
 ):
-    place(even_ref, odd_ref, lo_ref, hi_ref)
+    place(near_even_ref, near_odd_ref, p_ref.at[16:32], p_ref.at[48:64])
+    place(far_even_ref, far_odd_ref, p_ref.at[0:16], p_ref.at[64:80], 2)
+    p_ref[32:48, :] = mid_ref[...]
+    place(cot_even_ref.at[0:512], cot_odd_ref.at[0:512], cot_lo_ref, cot_hi_ref)
     zero = jnp.zeros((16, LANES), BF)
-    for a, ref in enumerate((lo_ref, mid_ref, hi_ref)):
+    for a in range(5):
         for b in range(3):
             k = (a * 3 + b) * 16
             for h in range(ROWS):
                 q = h + b - 1
-                x_ref[k : k + 16, tile(h)] = ref[:, tile(q)] if 0 <= q < ROWS else zero
-    x_ref[144:160, :] = jnp.ones((16, CELLS), BF)
+                x_ref[k : k + 16, tile(h)] = p_ref[a * 16 : (a + 1) * 16, tile(q)] if 0 <= q < ROWS else zero
     w = w_ref[...].astype(F32)
     weights = jnp.concatenate(
         [
@@ -141,42 +168,40 @@
     r = iota((512, 512), 0)
     q = iota((512, 512), 1)
     swap = flag(((r >> 5) == (q & 15)) & ((r & 31) == (q >> 4)))
-    cot = dot(swap, cot_ref[...].reshape(512, LANES))
+    cots = jnp.concatenate([c[...].reshape(512, LANES) for c in (cot_lo_ref, cot_ref, cot_hi_ref)], axis=1)
+    cots = dot(swap, cots)
     bias = b_ref[...]
-    for n in range(4):
-        t_ref[...] = dot(weights, x_ref[0:144, n * 512 : (n + 1) * 512])
-        for j in range(4):
-            h = n * 4 + j
-            z = (
-                from_left(t_ref[0:32, tile(j)])
-                + t_ref[32:64, tile(j)]
-                + from_right(t_ref[64:96, tile(j)])
-                + bias
-            )
-            s_ref[h * 32 : (h + 1) * 32] = smooth(z).astype(BF)
-            g = (cot[h * 32 : (h + 1) * 32] * slope_of(z)).astype(BF)
-            grad_ref[:, tile(h)] = g
-            g = g.astype(F32)
-            g_ref[0:32, tile(h)] = from_right(g).astype(BF)
-            g_ref[32:64, tile(h)] = g.astype(BF)
-            g_ref[64:96, tile(h)] = from_left(g).astype(BF)
+    for d in range(3):
+        for n in range(4):
+            t_ref[...] = dot(weights, x_ref[d * 48 : d * 48 + 144, n * 512 : (n + 1) * 512])
+            for j in range(4):
+                h = n * 4 + j
+                z = (
+                    from_left(t_ref[0:32, tile(j)])
+                    + t_ref[32:64, tile(j)]
+                    + from_right(t_ref[64:96, tile(j)])
+                    + bias
+                )
+                g = (cots[h * 32 : (h + 1) * 32, tile(d)] * slope_of(z)).astype(BF)
+                up_ref[(2 - d) * 32 : (3 - d) * 32, tile(h)] = g
+                if d == 1:
+                    s_ref[h * 32 : (h + 1) * 32] = smooth(z).astype(BF)
+                    g = g.astype(F32)
+                    g_ref[0:32, tile(h)] = from_right(g).astype(BF)
+                    g_ref[32:64, tile(h)] = g.astype(BF)
+                    g_ref[64:96, tile(h)] = from_left(g).astype(BF)
     g_ref[96:128, :] = jnp.zeros((32, CELLS), BF)
     act_ref[...] = dot(swap, s_ref[...], 0, 0).astype(BF).reshape(32, ROWS, LANES)
-    gw_ref[...] = dot(x_ref[...], g_ref[...], 1, 1)
-
-
-def third_kernel(mid_ref, even_ref, odd_ref, w_ref, slope_ref, patches_ref, gw_two_ref, gw_ref, x_ref, t_ref, g_ref):
-    x_ref[32:64, :] = mid_ref[...]
-    place(even_ref, odd_ref, x_ref.at[64:96], x_ref.at[0:32])
-    w = w_ref[...].astype(F32)
+    gw_ref[0:144] = dot(x_ref[48:192], g_ref[...], 1, 1)
+    gw_ref[144:160] = dot(jnp.ones((16, CELLS), BF), g_ref[...], 1, 1)
     weights = jnp.concatenate([w[a * 144 : (a + 1) * 144] for a in range(3)], axis=1).astype(BF)
-    t_ref[...] = dot(weights, x_ref[...])
+    u_ref[...] = dot(weights, up_ref[...])
     sums = jnp.zeros((16, 1), F32)
     for h in range(ROWS):
         cols = []
         for e in range(3):
             parts = [
-                t_ref[(b * 3 + e) * 16 : (b * 3 + e + 1) * 16, tile(h - b + 1)]
+                u_ref[(b * 3 + e) * 16 : (b * 3 + e + 1) * 16, tile(h - b + 1)]
                 for b in range(3)
                 if 0 <= h - b + 1 < ROWS
             ]
@@ -185,17 +210,16 @@
         total = None
         for i in range(8):
             g = (gp * slope_ref[i * 16 : (i + 1) * 16, tile(h)]).astype(BF)
-            g_ref[i * 16 : (i + 1) * 16, tile(h)] = g
+            one_ref[i * 16 : (i + 1) * 16, tile(h)] = g
             g = g.astype(F32)
             total = g if total is None else total + g
         sums = sums + jnp.sum(total, axis=1, keepdims=True)
-    full = dot(g_ref[...], patches_ref[...], 1, 1)
+    full = dot(one_ref[...], patches_ref[...], 1, 1)
     acc = full[0:16]
     for i in range(1, 8):
         shift = (i >> 2) * 64 + (i & 1) * 16 + ((i >> 1) & 1) * 4
         acc = acc + pltpu.roll(full[i * 16 : (i + 1) * 16], 256 - shift, 1)
     acc = jnp.where(iota((16, 256), 1) == 255, sums, acc)
-    gw_ref[...] = gw_two_ref[...]
     for i in range(8):
         gw_ref[i * 16 : (i + 1) * 16, 96:128] = acc[:, i * 32 : (i + 1) * 32]
 
@@ -231,62 +255,63 @@
     return jax.ShapeDtypeStruct(dims, kind)
 
 
-def pairs(even, odd, axis):
+def pairs(even, odd, axis, step=1):
     n = lax.axis_size(axis)
-    first = lax.ppermute(even, axis, [(i, i ^ 1) for i in range(n)])
-    second = lax.ppermute(odd, axis, [(i, (((i + 1) ^ 1) - 1) % n) for i in range(n)])
+    first = lax.ppermute(even, axis, [(i, i ^ step) for i in range(n)])
+    second = lax.ppermute(odd, axis, [(i, (((i + step) ^ step) - step) % n) for i in range(n)])
     return first, second
+
+
+def group_sum(v, axis, masks):
+    n = lax.axis_size(axis)
+    places = [0]
+    for m in masks:
+        places = places + [p ^ m for p in places]
+    parts = [v if p == 0 else lax.ppermute(v, axis, [(i, i ^ p) for i in range(n)]) for p in places]
+    while len(parts) > 1:
+        half = len(parts) // 2
+        parts = [parts[i] + parts[i + half] for i in range(half)]
+    return parts[0]
 
 
 def body(volumes, conv_one, bias_one, conv_two, bias_two, cotangent):
     depth = ("x", "y", "z")
     vol = volumes[0]
-    place_at = lax.axis_index(depth)
-    odd = place_at % 2
-    head, tail = vol[:, 0], vol[:, 1]
-    even_part, odd_part = pairs(jnp.where(odd == 1, head, tail), jnp.where(odd == 1, tail, head), depth)
+    cot = cotangent.reshape(32, ROWS, LANES)
+    packed = shape((768, LANES), BF)
+    even_part, odd_part = pairs(*call(pack_kernel, (packed, packed), [], "pack")(vol, cot), depth)
     base = jnp.pad(conv_one.astype(F32).transpose(4, 0, 2, 1, 3), ((0, 0), (0, 1), (0, 1), (0, 1), (0, 0))).reshape(16, 256)
-    plane = pltpu.VMEM((4, 32, 256), BF)
+    plane = pltpu.VMEM((256, LANES), BF)
     patches, slopes, pooled = call(
         first_kernel,
         (shape((256, CELLS), BF), shape((128, CELLS), F32), shape((16, CELLS), BF)),
         [plane, plane],
         "first",
     )(vol, even_part, odd_part, base, bias_one.reshape(16, 1))
-    even_part, odd_part = pairs(pooled, pooled, depth)
-    conv_flat = conv_two.reshape(432, 32)
-    act, grad, gw_two = call(
+    near = pairs(pooled, pooled, depth)
+    far = pairs(pooled, pooled, depth, 2)
+    act, v = call(
         second_kernel,
-        (shape((32, ROWS, LANES), BF), shape((32, CELLS), BF), shape((160, 128), F32)),
+        (shape((32, ROWS, LANES), BF), shape((160, 128), F32)),
         [
-            pltpu.VMEM((160, CELLS), BF),
+            pltpu.VMEM((80, CELLS), BF),
+            pltpu.VMEM((240, CELLS), BF),
             pltpu.VMEM((128, CELLS), BF),
             pltpu.VMEM((96, 512), F32),
             pltpu.VMEM((512, LANES), BF),
-            pltpu.VMEM((16, CELLS), BF),
-            pltpu.VMEM((16, CELLS), BF),
+            pltpu.VMEM((512, LANES), BF),
+            pltpu.VMEM((512, LANES), BF),
+            pltpu.VMEM((144, CELLS), F32),
+            pltpu.VMEM((96, CELLS), BF),
+            pltpu.VMEM((128, CELLS), BF),
         ],
         "second",
-    )(pooled, even_part, odd_part, conv_flat, bias_two.reshape(32, 1), cotangent.reshape(32, ROWS, LANES))
-    even_part, odd_part = pairs(grad, grad, depth)
-    v = call(
-        third_kernel,
-        shape((160, 128), F32),
-        [pltpu.VMEM((96, CELLS), BF), pltpu.VMEM((144, CELLS), F32), pltpu.VMEM((128, CELLS), BF)],
-        "third",
-    )(grad, even_part, odd_part, conv_flat, slopes, patches, gw_two)
+    )(pooled, *near, *far, conv_two.reshape(432, 32), bias_two.reshape(32, 1), cot, even_part, odd_part, slopes, patches)
     low = lax.axis_index("core") == 0
     swap = [(0, 1), (1, 0)]
     v = jnp.where(low, v[:80], v[80:]) + lax.ppermute(jnp.where(low, v[80:], v[:80]), "core", swap)
-    n = {axis: lax.axis_size(axis) for axis in ("z", "y", "x")}
-    steps = [
-        (axis, [(i, i ^ 2 if d == 4 and size == 8 else i ^ (d - 1)) for i in range(size)])
-        for axis, size in n.items()
-        for d in (2, 4, 8)
-        if d <= size
-    ]
-    for axis, perm in steps:
-        v = v + lax.ppermute(v, axis, perm)
+    for masks in GROUPS if lax.axis_size(depth) == 128 else ((1, 2), (7,)):
+        v = group_sum(v, depth, masks)
     one, sum_one, two, sum_two = call(
         last_kernel,
         (shape((27, 4, 16), F32), shape((1, 16), F32), shape((27, 16, 32), F32), shape((1, 32), F32)),

time: 78.9 us -> 72.4 us (0.918)
  waiting for transfers between devices: 36.1 us -> 18.9 us
  starting transfers between devices: 34.3 us -> 43.3 us
  local copies, waits for them, and re-layouts: 1.85 us -> 3.4 us
    ppermute x13 -> x16, waiting for transfers between devices: 34.4 us -> 17.1 us  [the longest x3 8.7 us: pairs(): lax.ppermute(odd, axis, [(i, ((i + step ^ step) - step) % n) for i in ran...]
    ppermute x13 -> x16, starting transfers between devices: 22.2 us -> 34.4 us  [the longest x3 17.1 us: pairs(): lax.ppermute(odd, axis, [(i, ((i + step ^ step) - step) % n) for i in ran...]
    ppermute x1, starting transfers between devices: 7.95 us -> 5.51 us  [body(): lax.ppermute(v, 'core', swap)]
    unnamed x13 -> x16, local copies, waits for them, and re-layouts: 1.59 us -> 3.14 us
    ppermute x1, starting transfers between devices: 4.22 us -> 3.39 us  [body(): lax.ppermute(jnp.where(low, v[80:], v[:80]), 'core', swap)]
  transfers between devices with their start and end apart: 15 -> 18, of which waited for: 14 -> 13; matrix products, arithmetic and copies ran while one was open for 0% -> 0% of each run, Pallas kernels for 0% -> 0%
where the time goes in v3:
time: 72.4 us; the launch traced here: 72.1 us
  starting transfers between devices  43.3 us (60%)
  waiting for transfers between devices  18.9 us (26%)
  Pallas kernels  5.7 us (8%)
  local copies, waits for them, and re-layouts  3.4 us (5%)
  between operations  0.77 us (1%)
    ppermute x3, starting transfers between devices, pairs(): lax.ppermute(odd, axis, [(i, ((i + step ^ step) - step) % n) for i in ran...  17.1 us
    ppermute x10, starting transfers between devices, group_sum(): lax.ppermute(v, axis, [(i, i ^ p) for i in range(n)])  14.7 us
    ppermute x3, waiting for transfers between devices, pairs(): lax.ppermute(odd, axis, [(i, ((i + step ^ step) - step) % n) for i in ran...  8.7 us
    ppermute x10, waiting for transfers between devices, group_sum(): lax.ppermute(v, axis, [(i, i ^ p) for i in range(n)])  6.1 us
    ppermute x1, starting transfers between devices, body(): lax.ppermute(v, 'core', swap)  5.51 us
    ppermute x1, starting transfers between devices, body(): lax.ppermute(jnp.where(low, v[80:], v[:80]), 'core', swap)  3.39 us
    unnamed x16, local copies, waits for them, and re-layouts  3.14 us
    pallas_call x1, Pallas kernels, body(): call(second_kernel, (shape((32, ROWS, LANES), BF), shape((160, 128), F32)...  2.87 us
  transfers between devices with their start and end apart: 18, of which 13 were waited for; matrix products, arithmetic and copies ran while one was open for 0% of the time, Pallas kernels for 0%

profile of v3, /device:TPU:1, one launch (start us, length us, event | category | flops | bytes accessed | tf_op | source)
XLA Modules:
  0.0 72.1 jit_solution(1068676428815024585)
XLA Ops:
  0.6 0.0 copy-start
  0.6 0.9 %copy-done = bf16[1,32,1,16,128]{4,3,2,1,0:T(8,128)(2,1)S(1)} copy-done((bf16[1,32,1,16,128]{4,3,2,1,0:T(8,128)(2,1)S(1)}, bf16[1,32,1,16,128]{4,3,2,1,0:T(8,128)(2,1)}, u32[]{:S(2)}) %copy-start) | copy-done | bytes 131096
  1.5 0.0 copy-start.2
  1.5 0.9 %copy-done.2 = bf16[1,4,2,32,256]{4,3,2,1,0:T(8,128)(2,1)S(1)} copy-done((bf16[1,4,2,32,256]{4,3,2,1,0:T(8,128)(2,1)S(1)}, bf16[1,4,2,32,256]{4,3,2,1,0:T(8,128)(2,1)}, u32[]{:S(2)}) %copy-start.2) | copy-done | bytes 131096
  2.4 0.0 copy-start.5
  2.4 0.1 pack.1
  2.5 2.6 %collective-permute-start = (bf16[768,128]{1,0:T(8,128)(2,1)S(1)}, bf16[768,128]{1,0:T(8,128)(2,1)S(1)}, u32[]{:S(2)}, u32[]{:S(2)}) collective-permute-start(bf16[768,128]{1,0:T(8,128)(2,1)S(1)} %get-tuple-element.16), channel_id=1, source_target_pairs={{0,1},{1,0},{2,3},{3,2},{4,5},{5,4},{6,7},{7,6},{8,9},{9,8},{10,11... | collective-permute-start | bytes 589832 | tf_op jit(solution)/shard_map/ppermute | solution.py:260
  5.1 9.3 %collective-permute-start.1 = (bf16[768,128]{1,0:T(8,128)(2,1)S(1)}, bf16[768,128]{1,0:T(8,128)(2,1)S(1)}, u32[]{:S(2)}, u32[]{:S(2)}) collective-permute-start(bf16[768,128]{1,0:T(8,128)(2,1)S(1)} %get-tuple-element.17), channel_id=1, source_target_pairs={{0,127},{1,2},{2,1},{3,4},{4,3},{5,6},{6,5},{7,8},{8,7},{9,10},{10... | collective-permute-start | bytes 589832 | tf_op jit(solution)/shard_map/ppermute | solution.py:261
  14.4 0.0 copy-done.5
  14.4 0.0 copy-start.3
  14.5 0.1 copy.16.w_ref
  14.5 0.0 copy-start.6
  14.5 0.7 copy-done.6
  15.2 0.1 copy.17.b_ref
  15.3 0.0 copy-start.1
  15.3 0.0 collective-permute-done.even_ref.cot_even_ref
  15.3 3.4 %collective-permute-done.1.odd_ref.cot_odd_ref = bf16[768,128]{1,0:T(8,128)(2,1)S(1)} collective-permute-done((bf16[768,128]{1,0:T(8,128)(2,1)S(1)}, bf16[768,128]{1,0:T(8,128)(2,1)S(1)}, u32[]{:S(2)}, u32[]{:S(2)}) %collective-permute-start.1) | collective-permute-done | bytes 196640 | tf_op jit(solution)/shard_map/ppermute | solution.py:261
  18.7 0.0 copy-done.3
  18.7 0.0 copy-start.4
  18.7 1.9 %first.1 = (bf16[256,2048]{1,0:T(8,128)(2,1)S(1)}, f32[128,2048]{1,0:T(8,128)S(1)}, bf16[16,2048]{1,0:T(8,128)(2,1)S(1)}) custom-call(bf16[4,2,32,256]{3,2,1,0:T(8,128)(2,1)S(1)} %bitcast.17, bf16[768,128]{1,0:T(8,128)(2,1)S(1)} %collective-permute-done.even_ref.cot_even_ref, bf16[768,128]{1,0:T(8,128)(2,1)S(1)} %collective-permute-done.1.odd_ref.cot_odd_ref, ...), custom_call_target="tpu_custom_call" | custom-call | tf_op jit(solution)/shard_map/first/pallas_call | solution.py:285
  20.6 0.1 collective-permute-start.2
  20.7 6.7 %collective-permute-start.3 = (bf16[16,2048]{1,0:T(8,128)(2,1)S(1)}, bf16[16,2048]{1,0:T(8,128)(2,1)S(1)}, u32[]{:S(2)}, u32[]{:S(2)}) collective-permute-start(bf16[16,2048]{1,0:T(8,128)(2,1)S(1)} %get-tuple-element.18.mid_ref), channel_id=1, source_target_pairs={{0,127},{1,2},{2,1},{3,4},{4,3},{5,6},{6,5},{7,8},{8,7},{9,10},{10... | collective-permute-start | bytes 196616 | tf_op jit(solution)/shard_map/ppermute | solution.py:261
  27.3 0.0 collective-permute-start.4
  27.3 1.1 %collective-permute-start.5 = (bf16[16,2048]{1,0:T(8,128)(2,1)S(1)}, bf16[16,2048]{1,0:T(8,128)(2,1)S(1)}, u32[]{:S(2)}, u32[]{:S(2)}) collective-permute-start(bf16[16,2048]{1,0:T(8,128)(2,1)S(1)} %get-tuple-element.18.mid_ref), channel_id=1, source_target_pairs={{0,126},{1,127},{2,4},{3,5},{4,2},{5,3},{6,8},{7,9},{8,6},{9,7},{1... | collective-permute-start | bytes 196616 | tf_op jit(solution)/shard_map/ppermute | solution.py:261
  28.4 0.0 copy-start.7
  28.4 0.7 copy-done.7
  29.1 0.1 copy.18.b_ref
  29.1 0.0 collective-permute-done.2.near_even_ref
  29.1 0.1 collective-permute-done.3.near_odd_ref
  29.3 2.3 %collective-permute-done.4.far_even_ref = bf16[16,2048]{1,0:T(8,128)(2,1)S(1)} collective-permute-done((bf16[16,2048]{1,0:T(8,128)(2,1)S(1)}, bf16[16,2048]{1,0:T(8,128)(2,1)S(1)}, u32[]{:S(2)}, u32[]{:S(2)}) %collective-permute-start.4) | collective-permute-done | bytes 65568 | tf_op jit(solution)/shard_map/ppermute | solution.py:260
  31.6 5.1 %collective-permute-done.5.far_odd_ref = bf16[16,2048]{1,0:T(8,128)(2,1)S(1)} collective-permute-done((bf16[16,2048]{1,0:T(8,128)(2,1)S(1)}, bf16[16,2048]{1,0:T(8,128)(2,1)S(1)}, u32[]{:S(2)}, u32[]{:S(2)}) %collective-permute-start.5) | collective-permute-done | bytes 65568 | tf_op jit(solution)/shard_map/ppermute | solution.py:261
  36.8 0.0 copy-done.1
  36.8 0.0 copy-done.4
  36.8 2.9 %second.1 = (bf16[32,16,128]{2,1,0:T(8,128)(2,1)}, f32[160,128]{1,0:T(8,128)S(1)}) custom-call(bf16[16,2048]{1,0:T(8,128)(2,1)S(1)} %get-tuple-element.18.mid_ref, bf16[16,2048]{1,0:T(8,128)(2,1)S(1)} %collective-permute-done.2.near_even_ref, bf16[16,2048]{1,0:T(8,128)(2,1)S(1)} %collective-permute-done.3.near_odd_ref, ...), custom_call_target="tpu_custom_call" | custom-call | tf_op jit(solution)/shard_map/second/pallas_call | solution.py:293
  39.7 3.4 %collective-permute-start.6 = (f32[80,128]{1,0:T(8,128)S(1)}, f32[80,128]{1,0:T(8,128)S(1)}, u32[]{:S(2)}, u32[]{:S(2)}) collective-permute-start(f32[80,128]{1,0:T(8,128)S(1)} %slice_select_fusion), channel_id=1, source_target_pairs={{0,128},{128,0},{1,129},{129,1},{2,130},{130,2},{3,131},{131,3},{4... | collective-permute-start | bytes 122888 | tf_op jit(solution)/shard_map/ppermute | solution.py:312
  43.1 0.9 %collective-permute-done.6 = f32[80,128]{1,0:T(8,128)S(1)} collective-permute-done((f32[80,128]{1,0:T(8,128)S(1)}, f32[80,128]{1,0:T(8,128)S(1)}, u32[]{:S(2)}, u32[]{:S(2)}) %collective-permute-start.6) | collective-permute-done | bytes 40992 | tf_op jit(solution)/shard_map/ppermute | solution.py:312
  43.9 0.1 collective-permute-start.7
  44.0 0.1 collective-permute-start.8
  44.1 2.5 %collective-permute-start.9 = (f32[80,128]{1,0:T(8,128)S(1)}, f32[80,128]{1,0:T(8,128)S(1)}, u32[]{:S(2)}, u32[]{:S(2)}) collective-permute-start(f32[80,128]{1,0:T(8,128)S(1)} %select_add_fusion), channel_id=1, source_target_pairs={{0,33},{1,32},{2,35},{3,34},{4,37},{5,36},{6,39},{7,38},{8,41},{9,... | collective-permute-start | bytes 122888 | tf_op jit(solution)/shard_map/ppermute | solution.py:270
  46.7 0.2 collective-permute-done.7
  46.9 0.1 collective-permute-done.8
  47.0 1.5 %collective-permute-done.9 = f32[80,128]{1,0:T(8,128)S(1)} collective-permute-done((f32[80,128]{1,0:T(8,128)S(1)}, f32[80,128]{1,0:T(8,128)S(1)}, u32[]{:S(2)}, u32[]{:S(2)}) %collective-permute-start.9) | collective-permute-done | bytes 40992 | tf_op jit(solution)/shard_map/ppermute | solution.py:270
  48.5 0.1 collective-permute-start.10
  48.6 0.1 collective-permute-start.11
  48.7 3.7 %collective-permute-start.12 = (f32[80,128]{1,0:T(8,128)S(1)}, f32[80,128]{1,0:T(8,128)S(1)}, u32[]{:S(2)}, u32[]{:S(2)}) collective-permute-start(f32[80,128]{1,0:T(8,128)S(1)} %add_add_fusion.2), channel_id=1, source_target_pairs={{0,104},{1,105},{2,106},{3,107},{4,108},{5,109},{6,110},{7,111},{8... | collective-permute-start | bytes 122888 | tf_op jit(solution)/shard_map/ppermute | solution.py:270
  52.5 0.2 collective-permute-done.10
  52.7 0.0 collective-permute-done.11
  52.7 1.3 %collective-permute-done.12 = f32[80,128]{1,0:T(8,128)S(1)} collective-permute-done((f32[80,128]{1,0:T(8,128)S(1)}, f32[80,128]{1,0:T(8,128)S(1)}, u32[]{:S(2)}, u32[]{:S(2)}) %collective-permute-start.12) | collective-permute-done | bytes 40992 | tf_op jit(solution)/shard_map/ppermute | solution.py:270
  54.0 0.1 collective-permute-start.13
  54.1 0.1 collective-permute-start.14
  54.2 4.6 %collective-permute-start.15 = (f32[80,128]{1,0:T(8,128)S(1)}, f32[80,128]{1,0:T(8,128)S(1)}, u32[]{:S(2)}, u32[]{:S(2)}) collective-permute-start(f32[80,128]{1,0:T(8,128)S(1)} %add_add_fusion.1), channel_id=1, source_target_pairs={{0,26},{1,27},{2,24},{3,25},{4,30},{5,31},{6,28},{7,29},{8,18},{9,... | collective-permute-start | bytes 122888 | tf_op jit(solution)/shard_map/ppermute | solution.py:270
  58.8 0.0 collective-permute-done.13
  58.8 0.0 collective-permute-done.14
  58.8 1.4 %collective-permute-done.15 = f32[80,128]{1,0:T(8,128)S(1)} collective-permute-done((f32[80,128]{1,0:T(8,128)S(1)}, f32[80,128]{1,0:T(8,128)S(1)}, u32[]{:S(2)}, u32[]{:S(2)}) %collective-permute-start.15) | collective-permute-done | bytes 40992 | tf_op jit(solution)/shard_map/ppermute | solution.py:270
  60.2 3.2 %collective-permute-start.16 = (f32[80,128]{1,0:T(8,128)S(1)}, f32[80,128]{1,0:T(8,128)S(1)}, u32[]{:S(2)}, u32[]{:S(2)}) collective-permute-start(f32[80,128]{1,0:T(8,128)S(1)} %add_add_fusion), channel_id=1, source_target_pairs={{0,7},{1,6},{2,5},{3,4},{4,3},{5,2},{6,1},{7,0},{8,15},{9,14},{10,... | collective-permute-start | bytes 122888 | tf_op jit(solution)/shard_map/ppermute | solution.py:270
  63.4 1.4 %collective-permute-done.16 = f32[80,128]{1,0:T(8,128)S(1)} collective-permute-done((f32[80,128]{1,0:T(8,128)S(1)}, f32[80,128]{1,0:T(8,128)S(1)}, u32[]{:S(2)}, u32[]{:S(2)}) %collective-permute-start.16) | collective-permute-done | bytes 40992 | tf_op jit(solution)/shard_map/ppermute | solution.py:270
  64.8 5.5 %collective-permute-start.17 = (f32[80,128]{1,0:T(8,128)S(1)}, f32[80,128]{1,0:T(8,128)S(1)}, u32[]{:S(2)}, u32[]{:S(2)}) collective-permute-start(f32[80,128]{1,0:T(8,128)S(1)} %add.45.mine_ref), channel_id=1, source_target_pairs={{0,128},{128,0},{1,129},{129,1},{2,130},{130,2},{3,131},{131,3},{4... | collective-permute-start | bytes 122888 | tf_op jit(solution)/shard_map/ppermute | solution.py:320
  70.3 0.9 %collective-permute-done.17.other_ref = f32[80,128]{1,0:T(8,128)S(1)} collective-permute-done((f32[80,128]{1,0:T(8,128)S(1)}, f32[80,128]{1,0:T(8,128)S(1)}, u32[]{:S(2)}, u32[]{:S(2)}) %collective-permute-start.17) | collective-permute-done | bytes 40992 | tf_op jit(solution)/shard_map/ppermute | solution.py:320
  71.2 0.9 %last.1 = (f32[27,4,16]{2,1,0:T(4,128)}, f32[1,16]{1,0:T(1,128)}, f32[27,16,32]{2,1,0:T(8,128)}, f32[1,32]{1,0:T(1,128)}) custom-call(f32[80,128]{1,0:T(8,128)S(1)} %add.45.mine_ref, f32[80,128]{1,0:T(8,128)S(1)} %collective-permute-done.17.other_ref), custom_call_target="tpu_custom_call" | custom-call | tf_op jit(solution)/shard_map/last/pallas_call | solution.py:315
  (8 shorter events, 0.1 us)
Async XLA Ops:
  0.6 0.9 %copy-start = (bf16[1,32,1,16,128]{4,3,2,1,0:T(8,128)(2,1)S(1)}, bf16[1,32,1,16,128]{4,3,2,1,0:T(8,128)(2,1)}, u32[]{:S(2)}) copy-start(bf16[1,32,1,16,128]{4,3,2,1,0:T(8,128)(2,1)} %param.11) | copy-start | bytes 393220
  1.5 0.9 %copy-start.2 = (bf16[1,4,2,32,256]{4,3,2,1,0:T(8,128)(2,1)S(1)}, bf16[1,4,2,32,256]{4,3,2,1,0:T(8,128)(2,1)}, u32[]{:S(2)}) copy-start(bf16[1,4,2,32,256]{4,3,2,1,0:T(8,128)(2,1)} %param.6) | copy-start | bytes 393220
  2.4 11.9 %copy-start.5 = (bf16[3,3,3,4,16]{4,3,2,1,0:T(4,128)(2,1)S(1)}, bf16[3,3,3,4,16]{4,3,2,1,0:T(4,128)(2,1)}, u32[]{:S(2)}) copy-start(bf16[3,3,3,4,16]{4,3,2,1,0:T(4,128)(2,1)} %param.7) | copy-start | bytes 10372
  2.5 12.8 %collective-permute-start = (bf16[768,128]{1,0:T(8,128)(2,1)S(1)}, bf16[768,128]{1,0:T(8,128)(2,1)S(1)}, u32[]{:S(2)}, u32[]{:S(2)}) collective-permute-start(bf16[768,128]{1,0:T(8,128)(2,1)S(1)} %get-tuple-element.16), channel_id=1, source_target_pairs={{0,1},{1,0},{2,3},{3,2},{4,5},{5,4},{6,7},{7,6},{8,9},{9,8},{10,11... | collective-permute-start | bytes 589832 | tf_op jit(solution)/shard_map/ppermute | solution.py:260
  5.1 13.6 %collective-permute-start.1 = (bf16[768,128]{1,0:T(8,128)(2,1)S(1)}, bf16[768,128]{1,0:T(8,128)(2,1)S(1)}, u32[]{:S(2)}, u32[]{:S(2)}) collective-permute-start(bf16[768,128]{1,0:T(8,128)(2,1)S(1)} %get-tuple-element.17), channel_id=1, source_target_pairs={{0,127},{1,2},{2,1},{3,4},{4,3},{5,6},{6,5},{7,8},{8,7},{9,10},{10... | collective-permute-start | bytes 589832 | tf_op jit(solution)/shard_map/ppermute | solution.py:261
  14.4 4.2 %copy-start.3 = (bf16[1,4,2,32,256]{4,3,2,1,0:T(8,128)(2,1)S(1)}, bf16[1,4,2,32,256]{4,3,2,1,0:T(8,128)(2,1)}, u32[]{:S(2)}) copy-start(bf16[1,4,2,32,256]{4,3,2,1,0:T(8,128)(2,1)} %param.6) | copy-start | bytes 393220
  14.5 0.7 copy-start.6
  15.3 21.5 %copy-start.1 = (bf16[1,32,1,16,128]{4,3,2,1,0:T(8,128)(2,1)S(1)}, bf16[1,32,1,16,128]{4,3,2,1,0:T(8,128)(2,1)}, u32[]{:S(2)}) copy-start(bf16[1,32,1,16,128]{4,3,2,1,0:T(8,128)(2,1)} %param.11) | copy-start | bytes 393220
  18.7 18.1 %copy-start.4 = (bf16[3,3,3,16,32]{4,3,2,1,0:T(8,128)(2,1)S(1)}, bf16[3,3,3,16,32]{4,3,2,1,0:T(8,128)(2,1)}, u32[]{:S(2)}) copy-start(bf16[3,3,3,16,32]{4,3,2,1,0:T(8,128)(2,1)} %param.9) | copy-start | bytes 82948
  20.6 8.6 %collective-permute-start.2 = (bf16[16,2048]{1,0:T(8,128)(2,1)S(1)}, bf16[16,2048]{1,0:T(8,128)(2,1)S(1)}, u32[]{:S(2)}, u32[]{:S(2)}) collective-permute-start(bf16[16,2048]{1,0:T(8,128)(2,1)S(1)} %get-tuple-element.18.mid_ref), channel_id=1, source_target_pairs={{0,1},{1,0},{2,3},{3,2},{4,5},{5,4},{6,7},{7,6},{8,9},{9,8},{10,11... | collective-permute-start | bytes 196616 | tf_op jit(solution)/shard_map/ppermute | solution.py:260
  20.7 8.6 %collective-permute-start.3 = (bf16[16,2048]{1,0:T(8,128)(2,1)S(1)}, bf16[16,2048]{1,0:T(8,128)(2,1)S(1)}, u32[]{:S(2)}, u32[]{:S(2)}) collective-permute-start(bf16[16,2048]{1,0:T(8,128)(2,1)S(1)} %get-tuple-element.18.mid_ref), channel_id=1, source_target_pairs={{0,127},{1,2},{2,1},{3,4},{4,3},{5,6},{6,5},{7,8},{8,7},{9,10},{10... | collective-permute-start | bytes 196616 | tf_op jit(solution)/shard_map/ppermute | solution.py:261
  27.3 4.3 %collective-permute-start.4 = (bf16[16,2048]{1,0:T(8,128)(2,1)S(1)}, bf16[16,2048]{1,0:T(8,128)(2,1)S(1)}, u32[]{:S(2)}, u32[]{:S(2)}) collective-permute-start(bf16[16,2048]{1,0:T(8,128)(2,1)S(1)} %get-tuple-element.18.mid_ref), channel_id=1, source_target_pairs={{0,2},{1,3},{2,0},{3,1},{4,6},{5,7},{6,4},{7,5},{8,10},{9,11},{10,... | collective-permute-start | bytes 196616 | tf_op jit(solution)/shard_map/ppermute | solution.py:260
  27.3 9.4 %collective-permute-start.5 = (bf16[16,2048]{1,0:T(8,128)(2,1)S(1)}, bf16[16,2048]{1,0:T(8,128)(2,1)S(1)}, u32[]{:S(2)}, u32[]{:S(2)}) collective-permute-start(bf16[16,2048]{1,0:T(8,128)(2,1)S(1)} %get-tuple-element.18.mid_ref), channel_id=1, source_target_pairs={{0,126},{1,127},{2,4},{3,5},{4,2},{5,3},{6,8},{7,9},{8,6},{9,7},{1... | collective-permute-start | bytes 196616 | tf_op jit(solution)/shard_map/ppermute | solution.py:261
  28.4 0.7 copy-start.7
  39.7 4.3 %collective-permute-start.6 = (f32[80,128]{1,0:T(8,128)S(1)}, f32[80,128]{1,0:T(8,128)S(1)}, u32[]{:S(2)}, u32[]{:S(2)}) collective-permute-start(f32[80,128]{1,0:T(8,128)S(1)} %slice_select_fusion), channel_id=1, source_target_pairs={{0,128},{128,0},{1,129},{129,1},{2,130},{130,2},{3,131},{131,3},{4... | collective-permute-start | bytes 122888 | tf_op jit(solution)/shard_map/ppermute | solution.py:312
  43.9 2.9 %collective-permute-start.7 = (f32[80,128]{1,0:T(8,128)S(1)}, f32[80,128]{1,0:T(8,128)S(1)}, u32[]{:S(2)}, u32[]{:S(2)}) collective-permute-start(f32[80,128]{1,0:T(8,128)S(1)} %select_add_fusion), channel_id=1, source_target_pairs={{0,32},{1,33},{2,34},{3,35},{4,36},{5,37},{6,38},{7,39},{8,40},{9,... | collective-permute-start | bytes 122888 | tf_op jit(solution)/shard_map/ppermute | solution.py:270
  44.0 2.9 %collective-permute-start.8 = (f32[80,128]{1,0:T(8,128)S(1)}, f32[80,128]{1,0:T(8,128)S(1)}, u32[]{:S(2)}, u32[]{:S(2)}) collective-permute-start(f32[80,128]{1,0:T(8,128)S(1)} %select_add_fusion), channel_id=1, source_target_pairs={{0,1},{1,0},{2,3},{3,2},{4,5},{5,4},{6,7},{7,6},{8,9},{9,8},{10,11... | collective-permute-start | bytes 122888 | tf_op jit(solution)/shard_map/ppermute | solution.py:270
  44.1 4.4 %collective-permute-start.9 = (f32[80,128]{1,0:T(8,128)S(1)}, f32[80,128]{1,0:T(8,128)S(1)}, u32[]{:S(2)}, u32[]{:S(2)}) collective-permute-start(f32[80,128]{1,0:T(8,128)S(1)} %select_add_fusion), channel_id=1, source_target_pairs={{0,33},{1,32},{2,35},{3,34},{4,37},{5,36},{6,39},{7,38},{8,41},{9,... | collective-permute-start | bytes 122888 | tf_op jit(solution)/shard_map/ppermute | solution.py:270
  48.5 4.2 %collective-permute-start.10 = (f32[80,128]{1,0:T(8,128)S(1)}, f32[80,128]{1,0:T(8,128)S(1)}, u32[]{:S(2)}, u32[]{:S(2)}) collective-permute-start(f32[80,128]{1,0:T(8,128)S(1)} %add_add_fusion.2), channel_id=1, source_target_pairs={{0,96},{1,97},{2,98},{3,99},{4,100},{5,101},{6,102},{7,103},{8,104... | collective-permute-start | bytes 122888 | tf_op jit(solution)/shard_map/ppermute | solution.py:270
  48.6 4.1 %collective-permute-start.11 = (f32[80,128]{1,0:T(8,128)S(1)}, f32[80,128]{1,0:T(8,128)S(1)}, u32[]{:S(2)}, u32[]{:S(2)}) collective-permute-start(f32[80,128]{1,0:T(8,128)S(1)} %add_add_fusion.2), channel_id=1, source_target_pairs={{0,8},{1,9},{2,10},{3,11},{4,12},{5,13},{6,14},{7,15},{8,0},{9,1},... | collective-permute-start | bytes 122888 | tf_op jit(solution)/shard_map/ppermute | solution.py:270
  48.7 5.2 %collective-permute-start.12 = (f32[80,128]{1,0:T(8,128)S(1)}, f32[80,128]{1,0:T(8,128)S(1)}, u32[]{:S(2)}, u32[]{:S(2)}) collective-permute-start(f32[80,128]{1,0:T(8,128)S(1)} %add_add_fusion.2), channel_id=1, source_target_pairs={{0,104},{1,105},{2,106},{3,107},{4,108},{5,109},{6,110},{7,111},{8... | collective-permute-start | bytes 122888 | tf_op jit(solution)/shard_map/ppermute | solution.py:270
  54.0 4.8 %collective-permute-start.13 = (f32[80,128]{1,0:T(8,128)S(1)}, f32[80,128]{1,0:T(8,128)S(1)}, u32[]{:S(2)}, u32[]{:S(2)}) collective-permute-start(f32[80,128]{1,0:T(8,128)S(1)} %add_add_fusion.1), channel_id=1, source_target_pairs={{0,2},{1,3},{2,0},{3,1},{4,6},{5,7},{6,4},{7,5},{8,10},{9,11},{10,... | collective-permute-start | bytes 122888 | tf_op jit(solution)/shard_map/ppermute | solution.py:270
  54.1 4.8 %collective-permute-start.14 = (f32[80,128]{1,0:T(8,128)S(1)}, f32[80,128]{1,0:T(8,128)S(1)}, u32[]{:S(2)}, u32[]{:S(2)}) collective-permute-start(f32[80,128]{1,0:T(8,128)S(1)} %add_add_fusion.1), channel_id=1, source_target_pairs={{0,24},{1,25},{2,26},{3,27},{4,28},{5,29},{6,30},{7,31},{8,16},{9,... | collective-permute-start | bytes 122888 | tf_op jit(solution)/shard_map/ppermute | solution.py:270
  54.2 6.0 %collective-permute-start.15 = (f32[80,128]{1,0:T(8,128)S(1)}, f32[80,128]{1,0:T(8,128)S(1)}, u32[]{:S(2)}, u32[]{:S(2)}) collective-permute-start(f32[80,128]{1,0:T(8,128)S(1)} %add_add_fusion.1), channel_id=1, source_target_pairs={{0,26},{1,27},{2,24},{3,25},{4,30},{5,31},{6,28},{7,29},{8,18},{9,... | collective-permute-start | bytes 122888 | tf_op jit(solution)/shard_map/ppermute | solution.py:270
  60.2 4.6 %collective-permute-start.16 = (f32[80,128]{1,0:T(8,128)S(1)}, f32[80,128]{1,0:T(8,128)S(1)}, u32[]{:S(2)}, u32[]{:S(2)}) collective-permute-start(f32[80,128]{1,0:T(8,128)S(1)} %add_add_fusion), channel_id=1, source_target_pairs={{0,7},{1,6},{2,5},{3,4},{4,3},{5,2},{6,1},{7,0},{8,15},{9,14},{10,... | collective-permute-start | bytes 122888 | tf_op jit(solution)/shard_map/ppermute | solution.py:270
  64.8 6.4 %collective-permute-start.17 = (f32[80,128]{1,0:T(8,128)S(1)}, f32[80,128]{1,0:T(8,128)S(1)}, u32[]{:S(2)}, u32[]{:S(2)}) collective-permute-start(f32[80,128]{1,0:T(8,128)S(1)} %add.45.mine_ref), channel_id=1, source_target_pairs={{0,128},{128,0},{1,129},{129,1},{2,130},{130,2},{3,131},{131,3},{4... | collective-permute-start | bytes 122888 | tf_op jit(solution)/shard_map/ppermute | solution.py:320

commit v4 on v3

--- a/solution.py
+++ b/solution.py
@@ -258,7 +258,10 @@
 def pairs(even, odd, axis, step=1):
     n = lax.axis_size(axis)
     first = lax.ppermute(even, axis, [(i, i ^ step) for i in range(n)])
-    second = lax.ppermute(odd, axis, [(i, (((i + step) ^ step) - step) % n) for i in range(n)])
+    to = [(((i + step) ^ step) - step) % n for i in range(n)]
+    if step == 2:
+        to[0], to[1], to[n - 2], to[n - 1] = 1, 0, n - 1, n - 2
+    second = lax.ppermute(odd, axis, list(enumerate(to)))
     return first, second
 
 

time: 72.4 us -> 70.5 us (0.974)
  starting transfers between devices: 43.3 us -> 42.2 us
  waiting for transfers between devices: 18.9 us -> 17.9 us
    ppermute x3, waiting for transfers between devices: 8.7 us -> 4.65 us  [pairs(): second = lax.ppermute(odd, axis, list(enumerate(to)))]
    ppermute x10, waiting for transfers between devices: 6.1 us -> 9.18 us  [group_sum(): lax.ppermute(v, axis, [(i, i ^ p) for i in range(n)])]
    ppermute x3, starting transfers between devices: 17.1 us -> 16 us  [pairs(): second = lax.ppermute(odd, axis, list(enumerate(to)))]
where the time goes in v4:
time: 70.5 us; the launch traced here: 70 us
  starting transfers between devices  42.2 us (60%)
  waiting for transfers between devices  17.9 us (25%)
  Pallas kernels  5.73 us (8%)
  local copies, waits for them, and re-layouts  3.39 us (5%)
  between operations  0.73 us (1%)
    ppermute x3, starting transfers between devices, pairs(): second = lax.ppermute(odd, axis, list(enumerate(to)))  16 us
    ppermute x10, starting transfers between devices, group_sum(): lax.ppermute(v, axis, [(i, i ^ p) for i in range(n)])  14.7 us
    ppermute x10, waiting for transfers between devices, group_sum(): lax.ppermute(v, axis, [(i, i ^ p) for i in range(n)])  9.18 us
    ppermute x1, starting transfers between devices, body(): lax.ppermute(v, 'core', swap)  5.68 us
    ppermute x3, waiting for transfers between devices, pairs(): second = lax.ppermute(odd, axis, list(enumerate(to)))  4.65 us
    unnamed x16, local copies, waits for them, and re-layouts  3.14 us
    ppermute x1, starting transfers between devices, body(): lax.ppermute(jnp.where(low, v[80:], v[:80]), 'core', swap)  3.13 us
    pallas_call x1, Pallas kernels, body(): call(second_kernel, (shape((32, ROWS, LANES), BF), shape((160, 128), F32)...  2.9 us
  transfers between devices with their start and end apart: 18, of which 13 were waited for; matrix products, arithmetic and copies ran while one was open for 0% of the time, Pallas kernels for 0%

profile of v4, /device:TPU:1, one launch (start us, length us, event | category | flops | bytes accessed | tf_op | source)
XLA Modules:
  0.0 70.0 jit_solution(2814537513184225464)
XLA Ops:
  0.6 0.0 copy-start
  0.6 0.9 %copy-done = bf16[1,32,1,16,128]{4,3,2,1,0:T(8,128)(2,1)S(1)} copy-done((bf16[1,32,1,16,128]{4,3,2,1,0:T(8,128)(2,1)S(1)}, bf16[1,32,1,16,128]{4,3,2,1,0:T(8,128)(2,1)}, u32[]{:S(2)}) %copy-start) | copy-done | bytes 131096
  1.5 0.0 copy-start.2
  1.5 0.9 %copy-done.2 = bf16[1,4,2,32,256]{4,3,2,1,0:T(8,128)(2,1)S(1)} copy-done((bf16[1,4,2,32,256]{4,3,2,1,0:T(8,128)(2,1)S(1)}, bf16[1,4,2,32,256]{4,3,2,1,0:T(8,128)(2,1)}, u32[]{:S(2)}) %copy-start.2) | copy-done | bytes 131096
  2.4 0.0 copy-start.5
  2.4 0.1 pack.1
  2.5 2.6 %collective-permute-start = (bf16[768,128]{1,0:T(8,128)(2,1)S(1)}, bf16[768,128]{1,0:T(8,128)(2,1)S(1)}, u32[]{:S(2)}, u32[]{:S(2)}) collective-permute-start(bf16[768,128]{1,0:T(8,128)(2,1)S(1)} %get-tuple-element.16), channel_id=1, source_target_pairs={{0,1},{1,0},{2,3},{3,2},{4,5},{5,4},{6,7},{7,6},{8,9},{9,8},{10,11... | collective-permute-start | bytes 589832 | tf_op jit(solution)/shard_map/ppermute | solution.py:260
  5.1 9.3 %collective-permute-start.1 = (bf16[768,128]{1,0:T(8,128)(2,1)S(1)}, bf16[768,128]{1,0:T(8,128)(2,1)S(1)}, u32[]{:S(2)}, u32[]{:S(2)}) collective-permute-start(bf16[768,128]{1,0:T(8,128)(2,1)S(1)} %get-tuple-element.17), channel_id=1, source_target_pairs={{0,127},{1,2},{2,1},{3,4},{4,3},{5,6},{6,5},{7,8},{8,7},{9,10},{10... | collective-permute-start | bytes 589832 | tf_op jit(solution)/shard_map/ppermute | solution.py:264
  14.4 0.0 copy-done.5
  14.4 0.0 copy-start.3
  14.5 0.1 copy.16.w_ref
  14.5 0.0 copy-start.6
  14.5 0.7 copy-done.6
  15.2 0.1 copy.17.b_ref
  15.3 0.0 copy-start.1
  15.3 0.0 collective-permute-done.even_ref.cot_even_ref
  15.3 3.4 %collective-permute-done.1.odd_ref.cot_odd_ref = bf16[768,128]{1,0:T(8,128)(2,1)S(1)} collective-permute-done((bf16[768,128]{1,0:T(8,128)(2,1)S(1)}, bf16[768,128]{1,0:T(8,128)(2,1)S(1)}, u32[]{:S(2)}, u32[]{:S(2)}) %collective-permute-start.1) | collective-permute-done | bytes 196640 | tf_op jit(solution)/shard_map/ppermute | solution.py:264
  18.7 0.0 copy-done.3
  18.7 0.0 copy-start.4
  18.7 1.9 %first.1 = (bf16[256,2048]{1,0:T(8,128)(2,1)S(1)}, f32[128,2048]{1,0:T(8,128)S(1)}, bf16[16,2048]{1,0:T(8,128)(2,1)S(1)}) custom-call(bf16[4,2,32,256]{3,2,1,0:T(8,128)(2,1)S(1)} %bitcast.17, bf16[768,128]{1,0:T(8,128)(2,1)S(1)} %collective-permute-done.even_ref.cot_even_ref, bf16[768,128]{1,0:T(8,128)(2,1)S(1)} %collective-permute-done.1.odd_ref.cot_odd_ref, ...), custom_call_target="tpu_custom_call" | custom-call | tf_op jit(solution)/shard_map/first/pallas_call | solution.py:288
  20.6 0.1 collective-permute-start.2
  20.7 6.7 %collective-permute-start.3 = (bf16[16,2048]{1,0:T(8,128)(2,1)S(1)}, bf16[16,2048]{1,0:T(8,128)(2,1)S(1)}, u32[]{:S(2)}, u32[]{:S(2)}) collective-permute-start(bf16[16,2048]{1,0:T(8,128)(2,1)S(1)} %get-tuple-element.18.mid_ref), channel_id=1, source_target_pairs={{0,127},{1,2},{2,1},{3,4},{4,3},{5,6},{6,5},{7,8},{8,7},{9,10},{10... | collective-permute-start | bytes 196616 | tf_op jit(solution)/shard_map/ppermute | solution.py:264
  27.3 0.0 collective-permute-start.4
  27.3 0.0 collective-permute-start.5
  27.3 0.0 copy-start.7
  27.3 0.7 copy-done.7
  28.0 0.1 copy.18.b_ref
  28.1 0.0 collective-permute-done.2.near_even_ref
  28.1 1.2 %collective-permute-done.3.near_odd_ref = bf16[16,2048]{1,0:T(8,128)(2,1)S(1)} collective-permute-done((bf16[16,2048]{1,0:T(8,128)(2,1)S(1)}, bf16[16,2048]{1,0:T(8,128)(2,1)S(1)}, u32[]{:S(2)}, u32[]{:S(2)}) %collective-permute-start.3) | collective-permute-done | bytes 65568 | tf_op jit(solution)/shard_map/ppermute | solution.py:264
  29.3 2.3 %collective-permute-done.4.far_even_ref = bf16[16,2048]{1,0:T(8,128)(2,1)S(1)} collective-permute-done((bf16[16,2048]{1,0:T(8,128)(2,1)S(1)}, bf16[16,2048]{1,0:T(8,128)(2,1)S(1)}, u32[]{:S(2)}, u32[]{:S(2)}) %collective-permute-start.4) | collective-permute-done | bytes 65568 | tf_op jit(solution)/shard_map/ppermute | solution.py:260
  31.6 0.0 collective-permute-done.5.far_odd_ref
  31.6 0.0 copy-done.1
  31.6 0.0 copy-done.4
  31.6 2.9 %second.1 = (bf16[32,16,128]{2,1,0:T(8,128)(2,1)}, f32[160,128]{1,0:T(8,128)S(1)}) custom-call(bf16[16,2048]{1,0:T(8,128)(2,1)S(1)} %get-tuple-element.18.mid_ref, bf16[16,2048]{1,0:T(8,128)(2,1)S(1)} %collective-permute-done.2.near_even_ref, bf16[16,2048]{1,0:T(8,128)(2,1)S(1)} %collective-permute-done.3.near_odd_ref, ...), custom_call_target="tpu_custom_call" | custom-call | tf_op jit(solution)/shard_map/second/pallas_call | solution.py:296
  34.5 3.1 %collective-permute-start.6 = (f32[80,128]{1,0:T(8,128)S(1)}, f32[80,128]{1,0:T(8,128)S(1)}, u32[]{:S(2)}, u32[]{:S(2)}) collective-permute-start(f32[80,128]{1,0:T(8,128)S(1)} %slice_select_fusion), channel_id=1, source_target_pairs={{0,128},{128,0},{1,129},{129,1},{2,130},{130,2},{3,131},{131,3},{4... | collective-permute-start | bytes 122888 | tf_op jit(solution)/shard_map/ppermute | solution.py:315
  37.7 0.9 %collective-permute-done.6 = f32[80,128]{1,0:T(8,128)S(1)} collective-permute-done((f32[80,128]{1,0:T(8,128)S(1)}, f32[80,128]{1,0:T(8,128)S(1)}, u32[]{:S(2)}, u32[]{:S(2)}) %collective-permute-start.6) | collective-permute-done | bytes 40992 | tf_op jit(solution)/shard_map/ppermute | solution.py:315
  38.5 2.0 %collective-permute-start.7 = (f32[80,128]{1,0:T(8,128)S(1)}, f32[80,128]{1,0:T(8,128)S(1)}, u32[]{:S(2)}, u32[]{:S(2)}) collective-permute-start(f32[80,128]{1,0:T(8,128)S(1)} %select_add_fusion), channel_id=1, source_target_pairs={{0,32},{1,33},{2,34},{3,35},{4,36},{5,37},{6,38},{7,39},{8,40},{9,... | collective-permute-start | bytes 122888 | tf_op jit(solution)/shard_map/ppermute | solution.py:273
  40.6 0.0 collective-permute-start.8
  40.6 1.3 %collective-permute-start.9 = (f32[80,128]{1,0:T(8,128)S(1)}, f32[80,128]{1,0:T(8,128)S(1)}, u32[]{:S(2)}, u32[]{:S(2)}) collective-permute-start(f32[80,128]{1,0:T(8,128)S(1)} %select_add_fusion), channel_id=1, source_target_pairs={{0,33},{1,32},{2,35},{3,34},{4,37},{5,36},{6,39},{7,38},{8,41},{9,... | collective-permute-start | bytes 122888 | tf_op jit(solution)/shard_map/ppermute | solution.py:273
  41.8 0.1 collective-permute-done.7
  42.0 1.5 %collective-permute-done.8 = f32[80,128]{1,0:T(8,128)S(1)} collective-permute-done((f32[80,128]{1,0:T(8,128)S(1)}, f32[80,128]{1,0:T(8,128)S(1)}, u32[]{:S(2)}, u32[]{:S(2)}) %collective-permute-start.8) | collective-permute-done | bytes 40992 | tf_op jit(solution)/shard_map/ppermute | solution.py:273
  43.4 1.1 %collective-permute-done.9 = f32[80,128]{1,0:T(8,128)S(1)} collective-permute-done((f32[80,128]{1,0:T(8,128)S(1)}, f32[80,128]{1,0:T(8,128)S(1)}, u32[]{:S(2)}, u32[]{:S(2)}) %collective-permute-start.9) | collective-permute-done | bytes 40992 | tf_op jit(solution)/shard_map/ppermute | solution.py:273
  44.5 2.2 %collective-permute-start.10 = (f32[80,128]{1,0:T(8,128)S(1)}, f32[80,128]{1,0:T(8,128)S(1)}, u32[]{:S(2)}, u32[]{:S(2)}) collective-permute-start(f32[80,128]{1,0:T(8,128)S(1)} %add_add_fusion.2), channel_id=1, source_target_pairs={{0,96},{1,97},{2,98},{3,99},{4,100},{5,101},{6,102},{7,103},{8,104... | collective-permute-start | bytes 122888 | tf_op jit(solution)/shard_map/ppermute | solution.py:273
  46.7 0.0 collective-permute-start.11
  46.7 1.7 %collective-permute-start.12 = (f32[80,128]{1,0:T(8,128)S(1)}, f32[80,128]{1,0:T(8,128)S(1)}, u32[]{:S(2)}, u32[]{:S(2)}) collective-permute-start(f32[80,128]{1,0:T(8,128)S(1)} %add_add_fusion.2), channel_id=1, source_target_pairs={{0,104},{1,105},{2,106},{3,107},{4,108},{5,109},{6,110},{7,111},{8... | collective-permute-start | bytes 122888 | tf_op jit(solution)/shard_map/ppermute | solution.py:273
  48.4 0.2 collective-permute-done.10
  48.6 0.9 %collective-permute-done.11 = f32[80,128]{1,0:T(8,128)S(1)} collective-permute-done((f32[80,128]{1,0:T(8,128)S(1)}, f32[80,128]{1,0:T(8,128)S(1)}, u32[]{:S(2)}, u32[]{:S(2)}) %collective-permute-start.11) | collective-permute-done | bytes 40992 | tf_op jit(solution)/shard_map/ppermute | solution.py:273
  49.6 2.1 %collective-permute-done.12 = f32[80,128]{1,0:T(8,128)S(1)} collective-permute-done((f32[80,128]{1,0:T(8,128)S(1)}, f32[80,128]{1,0:T(8,128)S(1)}, u32[]{:S(2)}, u32[]{:S(2)}) %collective-permute-start.12) | collective-permute-done | bytes 40992 | tf_op jit(solution)/shard_map/ppermute | solution.py:273
  51.7 0.8 %collective-permute-start.13 = (f32[80,128]{1,0:T(8,128)S(1)}, f32[80,128]{1,0:T(8,128)S(1)}, u32[]{:S(2)}, u32[]{:S(2)}) collective-permute-start(f32[80,128]{1,0:T(8,128)S(1)} %add_add_fusion.1), channel_id=1, source_target_pairs={{0,2},{1,3},{2,0},{3,1},{4,6},{5,7},{6,4},{7,5},{8,10},{9,11},{10,... | collective-permute-start | bytes 122888 | tf_op jit(solution)/shard_map/ppermute | solution.py:273
  52.5 0.0 collective-permute-start.14
  52.5 4.1 %collective-permute-start.15 = (f32[80,128]{1,0:T(8,128)S(1)}, f32[80,128]{1,0:T(8,128)S(1)}, u32[]{:S(2)}, u32[]{:S(2)}) collective-permute-start(f32[80,128]{1,0:T(8,128)S(1)} %add_add_fusion.1), channel_id=1, source_target_pairs={{0,26},{1,27},{2,24},{3,25},{4,30},{5,31},{6,28},{7,29},{8,18},{9,... | collective-permute-start | bytes 122888 | tf_op jit(solution)/shard_map/ppermute | solution.py:273
  56.5 0.0 collective-permute-done.13
  56.5 0.0 collective-permute-done.14
  56.5 1.8 %collective-permute-done.15 = f32[80,128]{1,0:T(8,128)S(1)} collective-permute-done((f32[80,128]{1,0:T(8,128)S(1)}, f32[80,128]{1,0:T(8,128)S(1)}, u32[]{:S(2)}, u32[]{:S(2)}) %collective-permute-start.15) | collective-permute-done | bytes 40992 | tf_op jit(solution)/shard_map/ppermute | solution.py:273
  58.3 2.6 %collective-permute-start.16 = (f32[80,128]{1,0:T(8,128)S(1)}, f32[80,128]{1,0:T(8,128)S(1)}, u32[]{:S(2)}, u32[]{:S(2)}) collective-permute-start(f32[80,128]{1,0:T(8,128)S(1)} %add_add_fusion), channel_id=1, source_target_pairs={{0,7},{1,6},{2,5},{3,4},{4,3},{5,2},{6,1},{7,0},{8,15},{9,14},{10,... | collective-permute-start | bytes 122888 | tf_op jit(solution)/shard_map/ppermute | solution.py:273
  61.0 1.5 %collective-permute-done.16 = f32[80,128]{1,0:T(8,128)S(1)} collective-permute-done((f32[80,128]{1,0:T(8,128)S(1)}, f32[80,128]{1,0:T(8,128)S(1)}, u32[]{:S(2)}, u32[]{:S(2)}) %collective-permute-start.16) | collective-permute-done | bytes 40992 | tf_op jit(solution)/shard_map/ppermute | solution.py:273
  62.5 5.7 %collective-permute-start.17 = (f32[80,128]{1,0:T(8,128)S(1)}, f32[80,128]{1,0:T(8,128)S(1)}, u32[]{:S(2)}, u32[]{:S(2)}) collective-permute-start(f32[80,128]{1,0:T(8,128)S(1)} %add.45.mine_ref), channel_id=1, source_target_pairs={{0,128},{128,0},{1,129},{129,1},{2,130},{130,2},{3,131},{131,3},{4... | collective-permute-start | bytes 122888 | tf_op jit(solution)/shard_map/ppermute | solution.py:323
  68.2 0.9 %collective-permute-done.17.other_ref = f32[80,128]{1,0:T(8,128)S(1)} collective-permute-done((f32[80,128]{1,0:T(8,128)S(1)}, f32[80,128]{1,0:T(8,128)S(1)}, u32[]{:S(2)}, u32[]{:S(2)}) %collective-permute-start.17) | collective-permute-done | bytes 40992 | tf_op jit(solution)/shard_map/ppermute | solution.py:323
  69.1 0.9 %last.1 = (f32[27,4,16]{2,1,0:T(4,128)}, f32[1,16]{1,0:T(1,128)}, f32[27,16,32]{2,1,0:T(8,128)}, f32[1,32]{1,0:T(1,128)}) custom-call(f32[80,128]{1,0:T(8,128)S(1)} %add.45.mine_ref, f32[80,128]{1,0:T(8,128)S(1)} %collective-permute-done.17.other_ref), custom_call_target="tpu_custom_call" | custom-call | tf_op jit(solution)/shard_map/last/pallas_call | solution.py:318
  (8 shorter events, 0.1 us)
Async XLA Ops:
  0.6 0.9 %copy-start = (bf16[1,32,1,16,128]{4,3,2,1,0:T(8,128)(2,1)S(1)}, bf16[1,32,1,16,128]{4,3,2,1,0:T(8,128)(2,1)}, u32[]{:S(2)}) copy-start(bf16[1,32,1,16,128]{4,3,2,1,0:T(8,128)(2,1)} %param.11) | copy-start | bytes 393220
  1.5 0.9 %copy-start.2 = (bf16[1,4,2,32,256]{4,3,2,1,0:T(8,128)(2,1)S(1)}, bf16[1,4,2,32,256]{4,3,2,1,0:T(8,128)(2,1)}, u32[]{:S(2)}) copy-start(bf16[1,4,2,32,256]{4,3,2,1,0:T(8,128)(2,1)} %param.6) | copy-start | bytes 393220
  2.4 11.9 %copy-start.5 = (bf16[3,3,3,4,16]{4,3,2,1,0:T(4,128)(2,1)S(1)}, bf16[3,3,3,4,16]{4,3,2,1,0:T(4,128)(2,1)}, u32[]{:S(2)}) copy-start(bf16[3,3,3,4,16]{4,3,2,1,0:T(4,128)(2,1)} %param.7) | copy-start | bytes 10372
  2.5 12.8 %collective-permute-start = (bf16[768,128]{1,0:T(8,128)(2,1)S(1)}, bf16[768,128]{1,0:T(8,128)(2,1)S(1)}, u32[]{:S(2)}, u32[]{:S(2)}) collective-permute-start(bf16[768,128]{1,0:T(8,128)(2,1)S(1)} %get-tuple-element.16), channel_id=1, source_target_pairs={{0,1},{1,0},{2,3},{3,2},{4,5},{5,4},{6,7},{7,6},{8,9},{9,8},{10,11... | collective-permute-start | bytes 589832 | tf_op jit(solution)/shard_map/ppermute | solution.py:260
  5.1 13.6 %collective-permute-start.1 = (bf16[768,128]{1,0:T(8,128)(2,1)S(1)}, bf16[768,128]{1,0:T(8,128)(2,1)S(1)}, u32[]{:S(2)}, u32[]{:S(2)}) collective-permute-start(bf16[768,128]{1,0:T(8,128)(2,1)S(1)} %get-tuple-element.17), channel_id=1, source_target_pairs={{0,127},{1,2},{2,1},{3,4},{4,3},{5,6},{6,5},{7,8},{8,7},{9,10},{10... | collective-permute-start | bytes 589832 | tf_op jit(solution)/shard_map/ppermute | solution.py:264
  14.4 4.2 %copy-start.3 = (bf16[1,4,2,32,256]{4,3,2,1,0:T(8,128)(2,1)S(1)}, bf16[1,4,2,32,256]{4,3,2,1,0:T(8,128)(2,1)}, u32[]{:S(2)}) copy-start(bf16[1,4,2,32,256]{4,3,2,1,0:T(8,128)(2,1)} %param.6) | copy-start | bytes 393220
  14.5 0.7 copy-start.6
  15.3 16.3 %copy-start.1 = (bf16[1,32,1,16,128]{4,3,2,1,0:T(8,128)(2,1)S(1)}, bf16[1,32,1,16,128]{4,3,2,1,0:T(8,128)(2,1)}, u32[]{:S(2)}) copy-start(bf16[1,32,1,16,128]{4,3,2,1,0:T(8,128)(2,1)} %param.11) | copy-start | bytes 393220
  18.7 12.9 %copy-start.4 = (bf16[3,3,3,16,32]{4,3,2,1,0:T(8,128)(2,1)S(1)}, bf16[3,3,3,16,32]{4,3,2,1,0:T(8,128)(2,1)}, u32[]{:S(2)}) copy-start(bf16[3,3,3,16,32]{4,3,2,1,0:T(8,128)(2,1)} %param.9) | copy-start | bytes 82948
  20.6 7.5 %collective-permute-start.2 = (bf16[16,2048]{1,0:T(8,128)(2,1)S(1)}, bf16[16,2048]{1,0:T(8,128)(2,1)S(1)}, u32[]{:S(2)}, u32[]{:S(2)}) collective-permute-start(bf16[16,2048]{1,0:T(8,128)(2,1)S(1)} %get-tuple-element.18.mid_ref), channel_id=1, source_target_pairs={{0,1},{1,0},{2,3},{3,2},{4,5},{5,4},{6,7},{7,6},{8,9},{9,8},{10,11... | collective-permute-start | bytes 196616 | tf_op jit(solution)/shard_map/ppermute | solution.py:260
  20.7 8.6 %collective-permute-start.3 = (bf16[16,2048]{1,0:T(8,128)(2,1)S(1)}, bf16[16,2048]{1,0:T(8,128)(2,1)S(1)}, u32[]{:S(2)}, u32[]{:S(2)}) collective-permute-start(bf16[16,2048]{1,0:T(8,128)(2,1)S(1)} %get-tuple-element.18.mid_ref), channel_id=1, source_target_pairs={{0,127},{1,2},{2,1},{3,4},{4,3},{5,6},{6,5},{7,8},{8,7},{9,10},{10... | collective-permute-start | bytes 196616 | tf_op jit(solution)/shard_map/ppermute | solution.py:264
  27.3 4.3 %collective-permute-start.4 = (bf16[16,2048]{1,0:T(8,128)(2,1)S(1)}, bf16[16,2048]{1,0:T(8,128)(2,1)S(1)}, u32[]{:S(2)}, u32[]{:S(2)}) collective-permute-start(bf16[16,2048]{1,0:T(8,128)(2,1)S(1)} %get-tuple-element.18.mid_ref), channel_id=1, source_target_pairs={{0,2},{1,3},{2,0},{3,1},{4,6},{5,7},{6,4},{7,5},{8,10},{9,11},{10,... | collective-permute-start | bytes 196616 | tf_op jit(solution)/shard_map/ppermute | solution.py:260
  27.3 4.3 %collective-permute-start.5 = (bf16[16,2048]{1,0:T(8,128)(2,1)S(1)}, bf16[16,2048]{1,0:T(8,128)(2,1)S(1)}, u32[]{:S(2)}, u32[]{:S(2)}) collective-permute-start(bf16[16,2048]{1,0:T(8,128)(2,1)S(1)} %get-tuple-element.18.mid_ref), channel_id=1, source_target_pairs={{0,1},{1,0},{2,4},{3,5},{4,2},{5,3},{6,8},{7,9},{8,6},{9,7},{10,12... | collective-permute-start | bytes 196616 | tf_op jit(solution)/shard_map/ppermute | solution.py:264
  27.3 0.7 copy-start.7
  34.5 4.0 %collective-permute-start.6 = (f32[80,128]{1,0:T(8,128)S(1)}, f32[80,128]{1,0:T(8,128)S(1)}, u32[]{:S(2)}, u32[]{:S(2)}) collective-permute-start(f32[80,128]{1,0:T(8,128)S(1)} %slice_select_fusion), channel_id=1, source_target_pairs={{0,128},{128,0},{1,129},{129,1},{2,130},{130,2},{3,131},{131,3},{4... | collective-permute-start | bytes 122888 | tf_op jit(solution)/shard_map/ppermute | solution.py:315
  38.5 3.4 %collective-permute-start.7 = (f32[80,128]{1,0:T(8,128)S(1)}, f32[80,128]{1,0:T(8,128)S(1)}, u32[]{:S(2)}, u32[]{:S(2)}) collective-permute-start(f32[80,128]{1,0:T(8,128)S(1)} %select_add_fusion), channel_id=1, source_target_pairs={{0,32},{1,33},{2,34},{3,35},{4,36},{5,37},{6,38},{7,39},{8,40},{9,... | collective-permute-start | bytes 122888 | tf_op jit(solution)/shard_map/ppermute | solution.py:273
  40.6 2.9 %collective-permute-start.8 = (f32[80,128]{1,0:T(8,128)S(1)}, f32[80,128]{1,0:T(8,128)S(1)}, u32[]{:S(2)}, u32[]{:S(2)}) collective-permute-start(f32[80,128]{1,0:T(8,128)S(1)} %select_add_fusion), channel_id=1, source_target_pairs={{0,1},{1,0},{2,3},{3,2},{4,5},{5,4},{6,7},{7,6},{8,9},{9,8},{10,11... | collective-permute-start | bytes 122888 | tf_op jit(solution)/shard_map/ppermute | solution.py:273
  40.6 3.9 %collective-permute-start.9 = (f32[80,128]{1,0:T(8,128)S(1)}, f32[80,128]{1,0:T(8,128)S(1)}, u32[]{:S(2)}, u32[]{:S(2)}) collective-permute-start(f32[80,128]{1,0:T(8,128)S(1)} %select_add_fusion), channel_id=1, source_target_pairs={{0,33},{1,32},{2,35},{3,34},{4,37},{5,36},{6,39},{7,38},{8,41},{9,... | collective-permute-start | bytes 122888 | tf_op jit(solution)/shard_map/ppermute | solution.py:273
  44.5 4.2 %collective-permute-start.10 = (f32[80,128]{1,0:T(8,128)S(1)}, f32[80,128]{1,0:T(8,128)S(1)}, u32[]{:S(2)}, u32[]{:S(2)}) collective-permute-start(f32[80,128]{1,0:T(8,128)S(1)} %add_add_fusion.2), channel_id=1, source_target_pairs={{0,96},{1,97},{2,98},{3,99},{4,100},{5,101},{6,102},{7,103},{8,104... | collective-permute-start | bytes 122888 | tf_op jit(solution)/shard_map/ppermute | solution.py:273
  46.7 2.9 %collective-permute-start.11 = (f32[80,128]{1,0:T(8,128)S(1)}, f32[80,128]{1,0:T(8,128)S(1)}, u32[]{:S(2)}, u32[]{:S(2)}) collective-permute-start(f32[80,128]{1,0:T(8,128)S(1)} %add_add_fusion.2), channel_id=1, source_target_pairs={{0,8},{1,9},{2,10},{3,11},{4,12},{5,13},{6,14},{7,15},{8,0},{9,1},... | collective-permute-start | bytes 122888 | tf_op jit(solution)/shard_map/ppermute | solution.py:273
  46.7 5.0 %collective-permute-start.12 = (f32[80,128]{1,0:T(8,128)S(1)}, f32[80,128]{1,0:T(8,128)S(1)}, u32[]{:S(2)}, u32[]{:S(2)}) collective-permute-start(f32[80,128]{1,0:T(8,128)S(1)} %add_add_fusion.2), channel_id=1, source_target_pairs={{0,104},{1,105},{2,106},{3,107},{4,108},{5,109},{6,110},{7,111},{8... | collective-permute-start | bytes 122888 | tf_op jit(solution)/shard_map/ppermute | solution.py:273
  51.7 4.8 %collective-permute-start.13 = (f32[80,128]{1,0:T(8,128)S(1)}, f32[80,128]{1,0:T(8,128)S(1)}, u32[]{:S(2)}, u32[]{:S(2)}) collective-permute-start(f32[80,128]{1,0:T(8,128)S(1)} %add_add_fusion.1), channel_id=1, source_target_pairs={{0,2},{1,3},{2,0},{3,1},{4,6},{5,7},{6,4},{7,5},{8,10},{9,11},{10,... | collective-permute-start | bytes 122888 | tf_op jit(solution)/shard_map/ppermute | solution.py:273
  52.5 4.1 %collective-permute-start.14 = (f32[80,128]{1,0:T(8,128)S(1)}, f32[80,128]{1,0:T(8,128)S(1)}, u32[]{:S(2)}, u32[]{:S(2)}) collective-permute-start(f32[80,128]{1,0:T(8,128)S(1)} %add_add_fusion.1), channel_id=1, source_target_pairs={{0,24},{1,25},{2,26},{3,27},{4,28},{5,29},{6,30},{7,31},{8,16},{9,... | collective-permute-start | bytes 122888 | tf_op jit(solution)/shard_map/ppermute | solution.py:273
  52.5 5.9 %collective-permute-start.15 = (f32[80,128]{1,0:T(8,128)S(1)}, f32[80,128]{1,0:T(8,128)S(1)}, u32[]{:S(2)}, u32[]{:S(2)}) collective-permute-start(f32[80,128]{1,0:T(8,128)S(1)} %add_add_fusion.1), channel_id=1, source_target_pairs={{0,26},{1,27},{2,24},{3,25},{4,30},{5,31},{6,28},{7,29},{8,18},{9,... | collective-permute-start | bytes 122888 | tf_op jit(solution)/shard_map/ppermute | solution.py:273
  58.3 4.2 %collective-permute-start.16 = (f32[80,128]{1,0:T(8,128)S(1)}, f32[80,128]{1,0:T(8,128)S(1)}, u32[]{:S(2)}, u32[]{:S(2)}) collective-permute-start(f32[80,128]{1,0:T(8,128)S(1)} %add_add_fusion), channel_id=1, source_target_pairs={{0,7},{1,6},{2,5},{3,4},{4,3},{5,2},{6,1},{7,0},{8,15},{9,14},{10,... | collective-permute-start | bytes 122888 | tf_op jit(solution)/shard_map/ppermute | solution.py:273
  62.5 6.6 %collective-permute-start.17 = (f32[80,128]{1,0:T(8,128)S(1)}, f32[80,128]{1,0:T(8,128)S(1)}, u32[]{:S(2)}, u32[]{:S(2)}) collective-permute-start(f32[80,128]{1,0:T(8,128)S(1)} %add.45.mine_ref), channel_id=1, source_target_pairs={{0,128},{128,0},{1,129},{129,1},{2,130},{130,2},{3,131},{131,3},{4... | collective-permute-start | bytes 122888 | tf_op jit(solution)/shard_map/ppermute | solution.py:323

commit v5 on v4

--- a/solution.py
+++ b/solution.py
@@ -142,7 +142,7 @@
 
 
 def second_kernel(
-    mid_ref, near_even_ref, near_odd_ref, far_even_ref, far_odd_ref, w_ref, b_ref, cot_ref, cot_even_ref, cot_odd_ref,
+    mid_ref, near_even_ref, far_even_ref, near_odd_ref, far_odd_ref, w_ref, b_ref, cot_ref, cot_even_ref, cot_odd_ref,
     slope_ref, patches_ref, act_ref, gw_ref, p_ref, x_ref, g_ref, t_ref, s_ref, cot_lo_ref, cot_hi_ref, u_ref, up_ref, one_ref
 ):
     place(near_even_ref, near_odd_ref, p_ref.at[16:32], p_ref.at[48:64])
@@ -255,14 +255,16 @@
     return jax.ShapeDtypeStruct(dims, kind)
 
 
-def pairs(even, odd, axis, step=1):
+def even_swap(v, axis, step=1):
+    return lax.ppermute(v, axis, [(i, i ^ step) for i in range(lax.axis_size(axis))])
+
+
+def odd_swap(v, axis, step=1):
     n = lax.axis_size(axis)
-    first = lax.ppermute(even, axis, [(i, i ^ step) for i in range(n)])
     to = [(((i + step) ^ step) - step) % n for i in range(n)]
     if step == 2:
         to[0], to[1], to[n - 2], to[n - 1] = 1, 0, n - 1, n - 2
-    second = lax.ppermute(odd, axis, list(enumerate(to)))
-    return first, second
+    return lax.ppermute(v, axis, list(enumerate(to)))
 
 
 def group_sum(v, axis, masks):
@@ -282,7 +284,8 @@
     vol = volumes[0]
     cot = cotangent.reshape(32, ROWS, LANES)
     packed = shape((768, LANES), BF)
-    even_part, odd_part = pairs(*call(pack_kernel, (packed, packed), [], "pack")(vol, cot), depth)
+    even_part, odd_part = call(pack_kernel, (packed, packed), [], "pack")(vol, cot)
+    even_part, odd_part = even_swap(even_part, depth), odd_swap(odd_part, depth)
     base = jnp.pad(conv_one.astype(F32).transpose(4, 0, 2, 1, 3), ((0, 0), (0, 1), (0, 1), (0, 1), (0, 0))).reshape(16, 256)
     plane = pltpu.VMEM((256, LANES), BF)
     patches, slopes, pooled = call(
@@ -291,8 +294,8 @@
         [plane, plane],
         "first",
     )(vol, even_part, odd_part, base, bias_one.reshape(16, 1))
-    near = pairs(pooled, pooled, depth)
-    far = pairs(pooled, pooled, depth, 2)
+    near_even, far_even = even_swap(pooled, depth), even_swap(pooled, depth, 2)
+    near_odd, far_odd = odd_swap(pooled, depth), odd_swap(pooled, depth, 2)
     act, v = call(
         second_kernel,
         (shape((32, ROWS, LANES), BF), shape((160, 128), F32)),
@@ -309,7 +312,7 @@
             pltpu.VMEM((128, CELLS), BF),
         ],
         "second",
-    )(pooled, *near, *far, conv_two.reshape(432, 32), bias_two.reshape(32, 1), cot, even_part, odd_part, slopes, patches)
+    )(pooled, near_even, far_even, near_odd, far_odd, conv_two.reshape(432, 32), bias_two.reshape(32, 1), cot, even_part, odd_part, slopes, patches)
     low = lax.axis_index("core") == 0
     swap = [(0, 1), (1, 0)]
     v = jnp.where(low, v[:80], v[80:]) + lax.ppermute(jnp.where(low, v[80:], v[:80]), "core", swap)

time: 70.5 us -> 71.7 us (1.017)
  waiting for transfers between devices: 17.9 us -> 19.6 us
    ppermute x10, waiting for transfers between devices: 9.18 us -> 11.8 us  [group_sum(): lax.ppermute(v, axis, [(i, i ^ p) for i in range(n)])]
    ppermute x6, waiting for transfers between devices: 6.94 us -> 6.08 us  [the longest x3 6.07 us: odd_swap(): return lax.ppermute(v, axis, list(enumerate(to)))]
where the time goes in v5:
time: 71.7 us; the launch traced here: 71.6 us
  starting transfers between devices  42 us (59%)
  waiting for transfers between devices  19.6 us (27%)
  Pallas kernels  5.7 us (8%)
  local copies, waits for them, and re-layouts  3.4 us (5%)
  between operations  0.74 us (1%)
    ppermute x3, starting transfers between devices, odd_swap(): return lax.ppermute(v, axis, list(enumerate(to)))  16 us
    ppermute x10, starting transfers between devices, group_sum(): lax.ppermute(v, axis, [(i, i ^ p) for i in range(n)])  14.5 us
    ppermute x10, waiting for transfers between devices, group_sum(): lax.ppermute(v, axis, [(i, i ^ p) for i in range(n)])  11.8 us
    ppermute x3, waiting for transfers between devices, odd_swap(): return lax.ppermute(v, axis, list(enumerate(to)))  6.07 us
    ppermute x1, starting transfers between devices, body(): lax.ppermute(v, 'core', swap)  5.76 us
    unnamed x16, local copies, waits for them, and re-layouts  3.14 us
    ppermute x1, starting transfers between devices, body(): lax.ppermute(jnp.where(low, v[80:], v[:80]), 'core', swap)  3.1 us
    pallas_call x1, Pallas kernels, body(): call(second_kernel, (shape((32, ROWS, LANES), BF), shape((160, 128), F32)...  2.87 us
  transfers between devices with their start and end apart: 18, of which 13 were waited for; matrix products, arithmetic and copies ran while one was open for 0% of the time, Pallas kernels for 0%

profile of v5, /device:TPU:1, one launch (start us, length us, event | category | flops | bytes accessed | tf_op | source)
XLA Modules:
  0.0 71.6 jit_solution(13702751477212784983)
XLA Ops:
  0.6 0.0 copy-start
  0.6 0.9 %copy-done = bf16[1,32,1,16,128]{4,3,2,1,0:T(8,128)(2,1)S(1)} copy-done((bf16[1,32,1,16,128]{4,3,2,1,0:T(8,128)(2,1)S(1)}, bf16[1,32,1,16,128]{4,3,2,1,0:T(8,128)(2,1)}, u32[]{:S(2)}) %copy-start) | copy-done | bytes 131096
  1.5 0.0 copy-start.2
  1.5 0.9 %copy-done.2 = bf16[1,4,2,32,256]{4,3,2,1,0:T(8,128)(2,1)S(1)} copy-done((bf16[1,4,2,32,256]{4,3,2,1,0:T(8,128)(2,1)S(1)}, bf16[1,4,2,32,256]{4,3,2,1,0:T(8,128)(2,1)}, u32[]{:S(2)}) %copy-start.2) | copy-done | bytes 131096
  2.4 0.0 copy-start.5
  2.4 0.1 pack.1
  2.5 2.6 %collective-permute-start = (bf16[768,128]{1,0:T(8,128)(2,1)S(1)}, bf16[768,128]{1,0:T(8,128)(2,1)S(1)}, u32[]{:S(2)}, u32[]{:S(2)}) collective-permute-start(bf16[768,128]{1,0:T(8,128)(2,1)S(1)} %get-tuple-element.16), channel_id=1, source_target_pairs={{0,1},{1,0},{2,3},{3,2},{4,5},{5,4},{6,7},{7,6},{8,9},{9,8},{10,11... | collective-permute-start | bytes 589832 | tf_op jit(solution)/shard_map/ppermute | solution.py:259
  5.1 9.3 %collective-permute-start.1 = (bf16[768,128]{1,0:T(8,128)(2,1)S(1)}, bf16[768,128]{1,0:T(8,128)(2,1)S(1)}, u32[]{:S(2)}, u32[]{:S(2)}) collective-permute-start(bf16[768,128]{1,0:T(8,128)(2,1)S(1)} %get-tuple-element.17), channel_id=1, source_target_pairs={{0,127},{1,2},{2,1},{3,4},{4,3},{5,6},{6,5},{7,8},{8,7},{9,10},{10... | collective-permute-start | bytes 589832 | tf_op jit(solution)/shard_map/ppermute | solution.py:267
  14.4 0.0 copy-done.5
  14.4 0.0 copy-start.3
  14.5 0.1 copy.16.w_ref
  14.5 0.0 copy-start.6
  14.5 0.7 copy-done.6
  15.2 0.1 copy.17.b_ref
  15.3 0.0 copy-start.1
  15.3 0.0 collective-permute-done.even_ref.cot_even_ref
  15.3 3.4 %collective-permute-done.1.odd_ref.cot_odd_ref = bf16[768,128]{1,0:T(8,128)(2,1)S(1)} collective-permute-done((bf16[768,128]{1,0:T(8,128)(2,1)S(1)}, bf16[768,128]{1,0:T(8,128)(2,1)S(1)}, u32[]{:S(2)}, u32[]{:S(2)}) %collective-permute-start.1) | collective-permute-done | bytes 196640 | tf_op jit(solution)/shard_map/ppermute | solution.py:267
  18.7 0.0 copy-done.3
  18.7 0.0 copy-start.4
  18.7 1.9 %first.1 = (bf16[256,2048]{1,0:T(8,128)(2,1)S(1)}, f32[128,2048]{1,0:T(8,128)S(1)}, bf16[16,2048]{1,0:T(8,128)(2,1)S(1)}) custom-call(bf16[4,2,32,256]{3,2,1,0:T(8,128)(2,1)S(1)} %bitcast.17, bf16[768,128]{1,0:T(8,128)(2,1)S(1)} %collective-permute-done.even_ref.cot_even_ref, bf16[768,128]{1,0:T(8,128)(2,1)S(1)} %collective-permute-done.1.odd_ref.cot_odd_ref, ...), custom_call_target="tpu_custom_call" | custom-call | tf_op jit(solution)/shard_map/first/pallas_call | solution.py:291
  20.6 0.1 collective-permute-start.2
  20.7 0.1 collective-permute-start.3
  20.8 6.7 %collective-permute-start.4 = (bf16[16,2048]{1,0:T(8,128)(2,1)S(1)}, bf16[16,2048]{1,0:T(8,128)(2,1)S(1)}, u32[]{:S(2)}, u32[]{:S(2)}) collective-permute-start(bf16[16,2048]{1,0:T(8,128)(2,1)S(1)} %get-tuple-element.18.mid_ref), channel_id=1, source_target_pairs={{0,127},{1,2},{2,1},{3,4},{4,3},{5,6},{6,5},{7,8},{8,7},{9,10},{10... | collective-permute-start | bytes 196616 | tf_op jit(solution)/shard_map/ppermute | solution.py:267
  27.4 0.0 collective-permute-start.5
  27.4 0.0 copy-start.7
  27.4 0.7 copy-done.7
  28.1 0.1 copy.18.b_ref
  28.2 0.0 collective-permute-done.2.near_even_ref
  28.2 0.0 collective-permute-done.3.far_even_ref
  28.2 1.2 %collective-permute-done.4.near_odd_ref = bf16[16,2048]{1,0:T(8,128)(2,1)S(1)} collective-permute-done((bf16[16,2048]{1,0:T(8,128)(2,1)S(1)}, bf16[16,2048]{1,0:T(8,128)(2,1)S(1)}, u32[]{:S(2)}, u32[]{:S(2)}) %collective-permute-start.4) | collective-permute-done | bytes 65568 | tf_op jit(solution)/shard_map/ppermute | solution.py:267
  29.4 1.4 %collective-permute-done.5.far_odd_ref = bf16[16,2048]{1,0:T(8,128)(2,1)S(1)} collective-permute-done((bf16[16,2048]{1,0:T(8,128)(2,1)S(1)}, bf16[16,2048]{1,0:T(8,128)(2,1)S(1)}, u32[]{:S(2)}, u32[]{:S(2)}) %collective-permute-start.5) | collective-permute-done | bytes 65568 | tf_op jit(solution)/shard_map/ppermute | solution.py:267
  30.8 0.0 copy-done.1
  30.8 0.0 copy-done.4
  30.8 2.9 %second.1 = (bf16[32,16,128]{2,1,0:T(8,128)(2,1)}, f32[160,128]{1,0:T(8,128)S(1)}) custom-call(bf16[16,2048]{1,0:T(8,128)(2,1)S(1)} %get-tuple-element.18.mid_ref, bf16[16,2048]{1,0:T(8,128)(2,1)S(1)} %collective-permute-done.2.near_even_ref, bf16[16,2048]{1,0:T(8,128)(2,1)S(1)} %collective-permute-done.3.far_even_ref, ...), custom_call_target="tpu_custom_call" | custom-call | tf_op jit(solution)/shard_map/second/pallas_call | solution.py:299
  33.7 3.1 %collective-permute-start.6 = (f32[80,128]{1,0:T(8,128)S(1)}, f32[80,128]{1,0:T(8,128)S(1)}, u32[]{:S(2)}, u32[]{:S(2)}) collective-permute-start(f32[80,128]{1,0:T(8,128)S(1)} %slice_select_fusion), channel_id=1, source_target_pairs={{0,128},{128,0},{1,129},{129,1},{2,130},{130,2},{3,131},{131,3},{4... | collective-permute-start | bytes 122888 | tf_op jit(solution)/shard_map/ppermute | solution.py:318
  36.8 0.9 %collective-permute-done.6 = f32[80,128]{1,0:T(8,128)S(1)} collective-permute-done((f32[80,128]{1,0:T(8,128)S(1)}, f32[80,128]{1,0:T(8,128)S(1)}, u32[]{:S(2)}, u32[]{:S(2)}) %collective-permute-start.6) | collective-permute-done | bytes 40992 | tf_op jit(solution)/shard_map/ppermute | solution.py:318
  37.7 3.0 %collective-permute-start.7 = (f32[80,128]{1,0:T(8,128)S(1)}, f32[80,128]{1,0:T(8,128)S(1)}, u32[]{:S(2)}, u32[]{:S(2)}) collective-permute-start(f32[80,128]{1,0:T(8,128)S(1)} %select_add_fusion), channel_id=1, source_target_pairs={{0,32},{1,33},{2,34},{3,35},{4,36},{5,37},{6,38},{7,39},{8,40},{9,... | collective-permute-start | bytes 122888 | tf_op jit(solution)/shard_map/ppermute | solution.py:275
  40.7 0.0 collective-permute-start.8
  40.7 1.3 %collective-permute-start.9 = (f32[80,128]{1,0:T(8,128)S(1)}, f32[80,128]{1,0:T(8,128)S(1)}, u32[]{:S(2)}, u32[]{:S(2)}) collective-permute-start(f32[80,128]{1,0:T(8,128)S(1)} %select_add_fusion), channel_id=1, source_target_pairs={{0,33},{1,32},{2,35},{3,34},{4,37},{5,36},{6,39},{7,38},{8,41},{9,... | collective-permute-start | bytes 122888 | tf_op jit(solution)/shard_map/ppermute | solution.py:275
  41.9 0.1 collective-permute-done.7
  42.1 1.5 %collective-permute-done.8 = f32[80,128]{1,0:T(8,128)S(1)} collective-permute-done((f32[80,128]{1,0:T(8,128)S(1)}, f32[80,128]{1,0:T(8,128)S(1)}, u32[]{:S(2)}, u32[]{:S(2)}) %collective-permute-start.8) | collective-permute-done | bytes 40992 | tf_op jit(solution)/shard_map/ppermute | solution.py:275
  43.5 1.1 %collective-permute-done.9 = f32[80,128]{1,0:T(8,128)S(1)} collective-permute-done((f32[80,128]{1,0:T(8,128)S(1)}, f32[80,128]{1,0:T(8,128)S(1)}, u32[]{:S(2)}, u32[]{:S(2)}) %collective-permute-start.9) | collective-permute-done | bytes 40992 | tf_op jit(solution)/shard_map/ppermute | solution.py:275
  44.6 2.2 %collective-permute-start.10 = (f32[80,128]{1,0:T(8,128)S(1)}, f32[80,128]{1,0:T(8,128)S(1)}, u32[]{:S(2)}, u32[]{:S(2)}) collective-permute-start(f32[80,128]{1,0:T(8,128)S(1)} %add_add_fusion.2), channel_id=1, source_target_pairs={{0,96},{1,97},{2,98},{3,99},{4,100},{5,101},{6,102},{7,103},{8,104... | collective-permute-start | bytes 122888 | tf_op jit(solution)/shard_map/ppermute | solution.py:275
  46.8 0.0 collective-permute-start.11
  46.8 1.7 %collective-permute-start.12 = (f32[80,128]{1,0:T(8,128)S(1)}, f32[80,128]{1,0:T(8,128)S(1)}, u32[]{:S(2)}, u32[]{:S(2)}) collective-permute-start(f32[80,128]{1,0:T(8,128)S(1)} %add_add_fusion.2), channel_id=1, source_target_pairs={{0,104},{1,105},{2,106},{3,107},{4,108},{5,109},{6,110},{7,111},{8... | collective-permute-start | bytes 122888 | tf_op jit(solution)/shard_map/ppermute | solution.py:275
  48.5 0.2 collective-permute-done.10
  48.7 0.9 %collective-permute-done.11 = f32[80,128]{1,0:T(8,128)S(1)} collective-permute-done((f32[80,128]{1,0:T(8,128)S(1)}, f32[80,128]{1,0:T(8,128)S(1)}, u32[]{:S(2)}, u32[]{:S(2)}) %collective-permute-start.11) | collective-permute-done | bytes 40992 | tf_op jit(solution)/shard_map/ppermute | solution.py:275
  49.6 2.1 %collective-permute-done.12 = f32[80,128]{1,0:T(8,128)S(1)} collective-permute-done((f32[80,128]{1,0:T(8,128)S(1)}, f32[80,128]{1,0:T(8,128)S(1)}, u32[]{:S(2)}, u32[]{:S(2)}) %collective-permute-start.12) | collective-permute-done | bytes 40992 | tf_op jit(solution)/shard_map/ppermute | solution.py:275
  51.8 0.1 collective-permute-start.13
  51.9 1.8 %collective-permute-start.14 = (f32[80,128]{1,0:T(8,128)S(1)}, f32[80,128]{1,0:T(8,128)S(1)}, u32[]{:S(2)}, u32[]{:S(2)}) collective-permute-start(f32[80,128]{1,0:T(8,128)S(1)} %add_add_fusion.1), channel_id=1, source_target_pairs={{0,24},{1,25},{2,26},{3,27},{4,28},{5,29},{6,30},{7,31},{8,16},{9,... | collective-permute-start | bytes 122888 | tf_op jit(solution)/shard_map/ppermute | solution.py:275
  53.7 2.9 %collective-permute-start.15 = (f32[80,128]{1,0:T(8,128)S(1)}, f32[80,128]{1,0:T(8,128)S(1)}, u32[]{:S(2)}, u32[]{:S(2)}) collective-permute-start(f32[80,128]{1,0:T(8,128)S(1)} %add_add_fusion.1), channel_id=1, source_target_pairs={{0,26},{1,27},{2,24},{3,25},{4,30},{5,31},{6,28},{7,29},{8,18},{9,... | collective-permute-start | bytes 122888 | tf_op jit(solution)/shard_map/ppermute | solution.py:275
  56.6 0.0 collective-permute-done.13
  56.6 0.0 collective-permute-done.14
  56.6 2.9 %collective-permute-done.15 = f32[80,128]{1,0:T(8,128)S(1)} collective-permute-done((f32[80,128]{1,0:T(8,128)S(1)}, f32[80,128]{1,0:T(8,128)S(1)}, u32[]{:S(2)}, u32[]{:S(2)}) %collective-permute-start.15) | collective-permute-done | bytes 40992 | tf_op jit(solution)/shard_map/ppermute | solution.py:275
  59.6 1.5 %collective-permute-start.16 = (f32[80,128]{1,0:T(8,128)S(1)}, f32[80,128]{1,0:T(8,128)S(1)}, u32[]{:S(2)}, u32[]{:S(2)}) collective-permute-start(f32[80,128]{1,0:T(8,128)S(1)} %add_add_fusion), channel_id=1, source_target_pairs={{0,7},{1,6},{2,5},{3,4},{4,3},{5,2},{6,1},{7,0},{8,15},{9,14},{10,... | collective-permute-start | bytes 122888 | tf_op jit(solution)/shard_map/ppermute | solution.py:275
  61.0 3.0 %collective-permute-done.16 = f32[80,128]{1,0:T(8,128)S(1)} collective-permute-done((f32[80,128]{1,0:T(8,128)S(1)}, f32[80,128]{1,0:T(8,128)S(1)}, u32[]{:S(2)}, u32[]{:S(2)}) %collective-permute-start.16) | collective-permute-done | bytes 40992 | tf_op jit(solution)/shard_map/ppermute | solution.py:275
  64.0 5.8 %collective-permute-start.17 = (f32[80,128]{1,0:T(8,128)S(1)}, f32[80,128]{1,0:T(8,128)S(1)}, u32[]{:S(2)}, u32[]{:S(2)}) collective-permute-start(f32[80,128]{1,0:T(8,128)S(1)} %add.45.mine_ref), channel_id=1, source_target_pairs={{0,128},{128,0},{1,129},{129,1},{2,130},{130,2},{3,131},{131,3},{4... | collective-permute-start | bytes 122888 | tf_op jit(solution)/shard_map/ppermute | solution.py:326
  69.8 0.9 %collective-permute-done.17.other_ref = f32[80,128]{1,0:T(8,128)S(1)} collective-permute-done((f32[80,128]{1,0:T(8,128)S(1)}, f32[80,128]{1,0:T(8,128)S(1)}, u32[]{:S(2)}, u32[]{:S(2)}) %collective-permute-start.17) | collective-permute-done | bytes 40992 | tf_op jit(solution)/shard_map/ppermute | solution.py:326
  70.7 0.9 %last.1 = (f32[27,4,16]{2,1,0:T(4,128)}, f32[1,16]{1,0:T(1,128)}, f32[27,16,32]{2,1,0:T(8,128)}, f32[1,32]{1,0:T(1,128)}) custom-call(f32[80,128]{1,0:T(8,128)S(1)} %add.45.mine_ref, f32[80,128]{1,0:T(8,128)S(1)} %collective-permute-done.17.other_ref), custom_call_target="tpu_custom_call" | custom-call | tf_op jit(solution)/shard_map/last/pallas_call | solution.py:321
  (8 shorter events, 0.1 us)
Async XLA Ops:
  0.6 0.9 %copy-start = (bf16[1,32,1,16,128]{4,3,2,1,0:T(8,128)(2,1)S(1)}, bf16[1,32,1,16,128]{4,3,2,1,0:T(8,128)(2,1)}, u32[]{:S(2)}) copy-start(bf16[1,32,1,16,128]{4,3,2,1,0:T(8,128)(2,1)} %param.11) | copy-start | bytes 393220
  1.5 0.9 %copy-start.2 = (bf16[1,4,2,32,256]{4,3,2,1,0:T(8,128)(2,1)S(1)}, bf16[1,4,2,32,256]{4,3,2,1,0:T(8,128)(2,1)}, u32[]{:S(2)}) copy-start(bf16[1,4,2,32,256]{4,3,2,1,0:T(8,128)(2,1)} %param.6) | copy-start | bytes 393220
  2.4 11.9 %copy-start.5 = (bf16[3,3,3,4,16]{4,3,2,1,0:T(4,128)(2,1)S(1)}, bf16[3,3,3,4,16]{4,3,2,1,0:T(4,128)(2,1)}, u32[]{:S(2)}) copy-start(bf16[3,3,3,4,16]{4,3,2,1,0:T(4,128)(2,1)} %param.7) | copy-start | bytes 10372
  2.5 12.8 %collective-permute-start = (bf16[768,128]{1,0:T(8,128)(2,1)S(1)}, bf16[768,128]{1,0:T(8,128)(2,1)S(1)}, u32[]{:S(2)}, u32[]{:S(2)}) collective-permute-start(bf16[768,128]{1,0:T(8,128)(2,1)S(1)} %get-tuple-element.16), channel_id=1, source_target_pairs={{0,1},{1,0},{2,3},{3,2},{4,5},{5,4},{6,7},{7,6},{8,9},{9,8},{10,11... | collective-permute-start | bytes 589832 | tf_op jit(solution)/shard_map/ppermute | solution.py:259
  5.1 13.6 %collective-permute-start.1 = (bf16[768,128]{1,0:T(8,128)(2,1)S(1)}, bf16[768,128]{1,0:T(8,128)(2,1)S(1)}, u32[]{:S(2)}, u32[]{:S(2)}) collective-permute-start(bf16[768,128]{1,0:T(8,128)(2,1)S(1)} %get-tuple-element.17), channel_id=1, source_target_pairs={{0,127},{1,2},{2,1},{3,4},{4,3},{5,6},{6,5},{7,8},{8,7},{9,10},{10... | collective-permute-start | bytes 589832 | tf_op jit(solution)/shard_map/ppermute | solution.py:267
  14.4 4.2 %copy-start.3 = (bf16[1,4,2,32,256]{4,3,2,1,0:T(8,128)(2,1)S(1)}, bf16[1,4,2,32,256]{4,3,2,1,0:T(8,128)(2,1)}, u32[]{:S(2)}) copy-start(bf16[1,4,2,32,256]{4,3,2,1,0:T(8,128)(2,1)} %param.6) | copy-start | bytes 393220
  14.5 0.7 copy-start.6
  15.3 15.6 %copy-start.1 = (bf16[1,32,1,16,128]{4,3,2,1,0:T(8,128)(2,1)S(1)}, bf16[1,32,1,16,128]{4,3,2,1,0:T(8,128)(2,1)}, u32[]{:S(2)}) copy-start(bf16[1,32,1,16,128]{4,3,2,1,0:T(8,128)(2,1)} %param.11) | copy-start | bytes 393220
  18.7 12.1 %copy-start.4 = (bf16[3,3,3,16,32]{4,3,2,1,0:T(8,128)(2,1)S(1)}, bf16[3,3,3,16,32]{4,3,2,1,0:T(8,128)(2,1)}, u32[]{:S(2)}) copy-start(bf16[3,3,3,16,32]{4,3,2,1,0:T(8,128)(2,1)} %param.9) | copy-start | bytes 82948
  20.6 7.6 %collective-permute-start.2 = (bf16[16,2048]{1,0:T(8,128)(2,1)S(1)}, bf16[16,2048]{1,0:T(8,128)(2,1)S(1)}, u32[]{:S(2)}, u32[]{:S(2)}) collective-permute-start(bf16[16,2048]{1,0:T(8,128)(2,1)S(1)} %get-tuple-element.18.mid_ref), channel_id=1, source_target_pairs={{0,1},{1,0},{2,3},{3,2},{4,5},{5,4},{6,7},{7,6},{8,9},{9,8},{10,11... | collective-permute-start | bytes 196616 | tf_op jit(solution)/shard_map/ppermute | solution.py:259
  20.7 7.5 %collective-permute-start.3 = (bf16[16,2048]{1,0:T(8,128)(2,1)S(1)}, bf16[16,2048]{1,0:T(8,128)(2,1)S(1)}, u32[]{:S(2)}, u32[]{:S(2)}) collective-permute-start(bf16[16,2048]{1,0:T(8,128)(2,1)S(1)} %get-tuple-element.18.mid_ref), channel_id=1, source_target_pairs={{0,2},{1,3},{2,0},{3,1},{4,6},{5,7},{6,4},{7,5},{8,10},{9,11},{10,... | collective-permute-start | bytes 196616 | tf_op jit(solution)/shard_map/ppermute | solution.py:259
  20.8 8.6 %collective-permute-start.4 = (bf16[16,2048]{1,0:T(8,128)(2,1)S(1)}, bf16[16,2048]{1,0:T(8,128)(2,1)S(1)}, u32[]{:S(2)}, u32[]{:S(2)}) collective-permute-start(bf16[16,2048]{1,0:T(8,128)(2,1)S(1)} %get-tuple-element.18.mid_ref), channel_id=1, source_target_pairs={{0,127},{1,2},{2,1},{3,4},{4,3},{5,6},{6,5},{7,8},{8,7},{9,10},{10... | collective-permute-start | bytes 196616 | tf_op jit(solution)/shard_map/ppermute | solution.py:267
  27.4 3.4 %collective-permute-start.5 = (bf16[16,2048]{1,0:T(8,128)(2,1)S(1)}, bf16[16,2048]{1,0:T(8,128)(2,1)S(1)}, u32[]{:S(2)}, u32[]{:S(2)}) collective-permute-start(bf16[16,2048]{1,0:T(8,128)(2,1)S(1)} %get-tuple-element.18.mid_ref), channel_id=1, source_target_pairs={{0,1},{1,0},{2,4},{3,5},{4,2},{5,3},{6,8},{7,9},{8,6},{9,7},{10,12... | collective-permute-start | bytes 196616 | tf_op jit(solution)/shard_map/ppermute | solution.py:267
  27.4 0.7 copy-start.7
  33.7 4.0 %collective-permute-start.6 = (f32[80,128]{1,0:T(8,128)S(1)}, f32[80,128]{1,0:T(8,128)S(1)}, u32[]{:S(2)}, u32[]{:S(2)}) collective-permute-start(f32[80,128]{1,0:T(8,128)S(1)} %slice_select_fusion), channel_id=1, source_target_pairs={{0,128},{128,0},{1,129},{129,1},{2,130},{130,2},{3,131},{131,3},{4... | collective-permute-start | bytes 122888 | tf_op jit(solution)/shard_map/ppermute | solution.py:318
  37.7 4.3 %collective-permute-start.7 = (f32[80,128]{1,0:T(8,128)S(1)}, f32[80,128]{1,0:T(8,128)S(1)}, u32[]{:S(2)}, u32[]{:S(2)}) collective-permute-start(f32[80,128]{1,0:T(8,128)S(1)} %select_add_fusion), channel_id=1, source_target_pairs={{0,32},{1,33},{2,34},{3,35},{4,36},{5,37},{6,38},{7,39},{8,40},{9,... | collective-permute-start | bytes 122888 | tf_op jit(solution)/shard_map/ppermute | solution.py:275
  40.7 2.9 %collective-permute-start.8 = (f32[80,128]{1,0:T(8,128)S(1)}, f32[80,128]{1,0:T(8,128)S(1)}, u32[]{:S(2)}, u32[]{:S(2)}) collective-permute-start(f32[80,128]{1,0:T(8,128)S(1)} %select_add_fusion), channel_id=1, source_target_pairs={{0,1},{1,0},{2,3},{3,2},{4,5},{5,4},{6,7},{7,6},{8,9},{9,8},{10,11... | collective-permute-start | bytes 122888 | tf_op jit(solution)/shard_map/ppermute | solution.py:275
  40.7 3.9 %collective-permute-start.9 = (f32[80,128]{1,0:T(8,128)S(1)}, f32[80,128]{1,0:T(8,128)S(1)}, u32[]{:S(2)}, u32[]{:S(2)}) collective-permute-start(f32[80,128]{1,0:T(8,128)S(1)} %select_add_fusion), channel_id=1, source_target_pairs={{0,33},{1,32},{2,35},{3,34},{4,37},{5,36},{6,39},{7,38},{8,41},{9,... | collective-permute-start | bytes 122888 | tf_op jit(solution)/shard_map/ppermute | solution.py:275
  44.6 4.2 %collective-permute-start.10 = (f32[80,128]{1,0:T(8,128)S(1)}, f32[80,128]{1,0:T(8,128)S(1)}, u32[]{:S(2)}, u32[]{:S(2)}) collective-permute-start(f32[80,128]{1,0:T(8,128)S(1)} %add_add_fusion.2), channel_id=1, source_target_pairs={{0,96},{1,97},{2,98},{3,99},{4,100},{5,101},{6,102},{7,103},{8,104... | collective-permute-start | bytes 122888 | tf_op jit(solution)/shard_map/ppermute | solution.py:275
  46.8 2.9 %collective-permute-start.11 = (f32[80,128]{1,0:T(8,128)S(1)}, f32[80,128]{1,0:T(8,128)S(1)}, u32[]{:S(2)}, u32[]{:S(2)}) collective-permute-start(f32[80,128]{1,0:T(8,128)S(1)} %add_add_fusion.2), channel_id=1, source_target_pairs={{0,8},{1,9},{2,10},{3,11},{4,12},{5,13},{6,14},{7,15},{8,0},{9,1},... | collective-permute-start | bytes 122888 | tf_op jit(solution)/shard_map/ppermute | solution.py:275
  46.8 5.0 %collective-permute-start.12 = (f32[80,128]{1,0:T(8,128)S(1)}, f32[80,128]{1,0:T(8,128)S(1)}, u32[]{:S(2)}, u32[]{:S(2)}) collective-permute-start(f32[80,128]{1,0:T(8,128)S(1)} %add_add_fusion.2), channel_id=1, source_target_pairs={{0,104},{1,105},{2,106},{3,107},{4,108},{5,109},{6,110},{7,111},{8... | collective-permute-start | bytes 122888 | tf_op jit(solution)/shard_map/ppermute | solution.py:275
  51.8 4.8 %collective-permute-start.13 = (f32[80,128]{1,0:T(8,128)S(1)}, f32[80,128]{1,0:T(8,128)S(1)}, u32[]{:S(2)}, u32[]{:S(2)}) collective-permute-start(f32[80,128]{1,0:T(8,128)S(1)} %add_add_fusion.1), channel_id=1, source_target_pairs={{0,2},{1,3},{2,0},{3,1},{4,6},{5,7},{6,4},{7,5},{8,10},{9,11},{10,... | collective-permute-start | bytes 122888 | tf_op jit(solution)/shard_map/ppermute | solution.py:275
  51.9 4.8 %collective-permute-start.14 = (f32[80,128]{1,0:T(8,128)S(1)}, f32[80,128]{1,0:T(8,128)S(1)}, u32[]{:S(2)}, u32[]{:S(2)}) collective-permute-start(f32[80,128]{1,0:T(8,128)S(1)} %add_add_fusion.1), channel_id=1, source_target_pairs={{0,24},{1,25},{2,26},{3,27},{4,28},{5,29},{6,30},{7,31},{8,16},{9,... | collective-permute-start | bytes 122888 | tf_op jit(solution)/shard_map/ppermute | solution.py:275
  53.7 5.9 %collective-permute-start.15 = (f32[80,128]{1,0:T(8,128)S(1)}, f32[80,128]{1,0:T(8,128)S(1)}, u32[]{:S(2)}, u32[]{:S(2)}) collective-permute-start(f32[80,128]{1,0:T(8,128)S(1)} %add_add_fusion.1), channel_id=1, source_target_pairs={{0,26},{1,27},{2,24},{3,25},{4,30},{5,31},{6,28},{7,29},{8,18},{9,... | collective-permute-start | bytes 122888 | tf_op jit(solution)/shard_map/ppermute | solution.py:275
  59.6 4.4 %collective-permute-start.16 = (f32[80,128]{1,0:T(8,128)S(1)}, f32[80,128]{1,0:T(8,128)S(1)}, u32[]{:S(2)}, u32[]{:S(2)}) collective-permute-start(f32[80,128]{1,0:T(8,128)S(1)} %add_add_fusion), channel_id=1, source_target_pairs={{0,7},{1,6},{2,5},{3,4},{4,3},{5,2},{6,1},{7,0},{8,15},{9,14},{10,... | collective-permute-start | bytes 122888 | tf_op jit(solution)/shard_map/ppermute | solution.py:275
  64.0 6.6 %collective-permute-start.17 = (f32[80,128]{1,0:T(8,128)S(1)}, f32[80,128]{1,0:T(8,128)S(1)}, u32[]{:S(2)}, u32[]{:S(2)}) collective-permute-start(f32[80,128]{1,0:T(8,128)S(1)} %add.45.mine_ref), channel_id=1, source_target_pairs={{0,128},{128,0},{1,129},{129,1},{2,130},{130,2},{3,131},{131,3},{4... | collective-permute-start | bytes 122888 | tf_op jit(solution)/shard_map/ppermute | solution.py:326

commit v6 on v5

--- a/solution.py
+++ b/solution.py
@@ -99,7 +99,7 @@
 
 
 def first_kernel(
-    vol_ref, even_ref, odd_ref, w_ref, b_ref, patches_ref, slope_ref, pooled_ref, lo_ref, hi_ref
+    vol_ref, odd_ref, even_ref, w_ref, b_ref, patches_ref, slope_ref, pooled_ref, lo_ref, hi_ref
 ):
     place(even_ref.at[512:768], odd_ref.at[512:768], lo_ref, hi_ref)
     cols = iota((256, 512), 1)
@@ -142,7 +142,7 @@
 
 
 def second_kernel(
-    mid_ref, near_even_ref, far_even_ref, near_odd_ref, far_odd_ref, w_ref, b_ref, cot_ref, cot_even_ref, cot_odd_ref,
+    mid_ref, near_odd_ref, far_odd_ref, near_even_ref, far_even_ref, w_ref, b_ref, cot_ref, cot_even_ref, cot_odd_ref,
     slope_ref, patches_ref, act_ref, gw_ref, p_ref, x_ref, g_ref, t_ref, s_ref, cot_lo_ref, cot_hi_ref, u_ref, up_ref, one_ref
 ):
     place(near_even_ref, near_odd_ref, p_ref.at[16:32], p_ref.at[48:64])
@@ -285,7 +285,7 @@
     cot = cotangent.reshape(32, ROWS, LANES)
     packed = shape((768, LANES), BF)
     even_part, odd_part = call(pack_kernel, (packed, packed), [], "pack")(vol, cot)
-    even_part, odd_part = even_swap(even_part, depth), odd_swap(odd_part, depth)
+    odd_part, even_part = odd_swap(odd_part, depth), even_swap(even_part, depth)
     base = jnp.pad(conv_one.astype(F32).transpose(4, 0, 2, 1, 3), ((0, 0), (0, 1), (0, 1), (0, 1), (0, 0))).reshape(16, 256)
     plane = pltpu.VMEM((256, LANES), BF)
     patches, slopes, pooled = call(
@@ -293,9 +293,9 @@
         (shape((256, CELLS), BF), shape((128, CELLS), F32), shape((16, CELLS), BF)),
         [plane, plane],
         "first",
-    )(vol, even_part, odd_part, base, bias_one.reshape(16, 1))
+    )(vol, odd_part, even_part, base, bias_one.reshape(16, 1))
+    near_odd, far_odd = odd_swap(pooled, depth), odd_swap(pooled, depth, 2)
     near_even, far_even = even_swap(pooled, depth), even_swap(pooled, depth, 2)
-    near_odd, far_odd = odd_swap(pooled, depth), odd_swap(pooled, depth, 2)
     act, v = call(
         second_kernel,
         (shape((32, ROWS, LANES), BF), shape((160, 128), F32)),
@@ -312,7 +312,7 @@
             pltpu.VMEM((128, CELLS), BF),
         ],
         "second",
-    )(pooled, near_even, far_even, near_odd, far_odd, conv_two.reshape(432, 32), bias_two.reshape(32, 1), cot, even_part, odd_part, slopes, patches)
+    )(pooled, near_odd, far_odd, near_even, far_even, conv_two.reshape(432, 32), bias_two.reshape(32, 1), cot, even_part, odd_part, slopes, patches)
     low = lax.axis_index("core") == 0
     swap = [(0, 1), (1, 0)]
     v = jnp.where(low, v[:80], v[80:]) + lax.ppermute(jnp.where(low, v[80:], v[:80]), "core", swap)

time: 71.7 us -> 70.3 us (0.980)
  waiting for transfers between devices: 19.6 us -> 18.1 us
    ppermute x10, waiting for transfers between devices: 11.8 us -> 7.93 us  [group_sum(): lax.ppermute(v, axis, [(i, i ^ p) for i in range(n)])]
    ppermute x3, waiting for transfers between devices: 0.01 us -> 3.45 us  [even_swap(): lax.ppermute(v, axis, [(i, i ^ step) for i in range(lax.axis_size(axis))])]
    ppermute x3, starting transfers between devices: 2.74 us -> 1.47 us  [even_swap(): lax.ppermute(v, axis, [(i, i ^ step) for i in range(lax.axis_size(axis))])]
    ppermute x3, waiting for transfers between devices: 6.07 us -> 4.93 us  [odd_swap(): return lax.ppermute(v, axis, list(enumerate(to)))]
    ppermute x3, starting transfers between devices: 16 us -> 17 us  [odd_swap(): return lax.ppermute(v, axis, list(enumerate(to)))]
  transfers between devices with their start and end apart: 18 -> 18, of which waited for: 13 -> 16; matrix products, arithmetic and copies ran while one was open for 0% -> 0% of each run, Pallas kernels for 0% -> 0%
where the time goes in v6:
time: 70.3 us; the launch traced here: 69.6 us
  starting transfers between devices  41.6 us (59%)
  waiting for transfers between devices  18.1 us (26%)
  Pallas kernels  5.69 us (8%)
  local copies, waits for them, and re-layouts  3.4 us (5%)
  between operations  0.74 us (1%)
    ppermute x3, starting transfers between devices, odd_swap(): return lax.ppermute(v, axis, list(enumerate(to)))  17 us
    ppermute x10, starting transfers between devices, group_sum(): lax.ppermute(v, axis, [(i, i ^ p) for i in range(n)])  14.2 us
    ppermute x10, waiting for transfers between devices, group_sum(): lax.ppermute(v, axis, [(i, i ^ p) for i in range(n)])  7.93 us
    ppermute x1, starting transfers between devices, body(): lax.ppermute(v, 'core', swap)  5.71 us
    ppermute x3, waiting for transfers between devices, odd_swap(): return lax.ppermute(v, axis, list(enumerate(to)))  4.93 us
    ppermute x3, waiting for transfers between devices, even_swap(): lax.ppermute(v, axis, [(i, i ^ step) for i in range(lax.axis_size(axis))])  3.45 us
    ppermute x1, starting transfers between devices, body(): lax.ppermute(jnp.where(low, v[80:], v[:80]), 'core', swap)  3.23 us
    unnamed x16, local copies, waits for them, and re-layouts  3.14 us
  transfers between devices with their start and end apart: 18, of which 16 were waited for; matrix products, arithmetic and copies ran while one was open for 0% of the time, Pallas kernels for 0%

profile of v6, /device:TPU:1, one launch (start us, length us, event | category | flops | bytes accessed | tf_op | source)
XLA Modules:
  0.0 69.6 jit_solution(12858884347980871984)
XLA Ops:
  0.6 0.0 copy-start
  0.6 0.9 %copy-done = bf16[1,32,1,16,128]{4,3,2,1,0:T(8,128)(2,1)S(1)} copy-done((bf16[1,32,1,16,128]{4,3,2,1,0:T(8,128)(2,1)S(1)}, bf16[1,32,1,16,128]{4,3,2,1,0:T(8,128)(2,1)}, u32[]{:S(2)}) %copy-start) | copy-done | bytes 131096
  1.5 0.0 copy-start.2
  1.5 0.9 %copy-done.2 = bf16[1,4,2,32,256]{4,3,2,1,0:T(8,128)(2,1)S(1)} copy-done((bf16[1,4,2,32,256]{4,3,2,1,0:T(8,128)(2,1)S(1)}, bf16[1,4,2,32,256]{4,3,2,1,0:T(8,128)(2,1)}, u32[]{:S(2)}) %copy-start.2) | copy-done | bytes 131096
  2.4 0.0 copy-start.5
  2.4 0.1 pack.1
  2.5 11.1 %collective-permute-start = (bf16[768,128]{1,0:T(8,128)(2,1)S(1)}, bf16[768,128]{1,0:T(8,128)(2,1)S(1)}, u32[]{:S(2)}, u32[]{:S(2)}) collective-permute-start(bf16[768,128]{1,0:T(8,128)(2,1)S(1)} %get-tuple-element.16), channel_id=1, source_target_pairs={{0,127},{1,2},{2,1},{3,4},{4,3},{5,6},{6,5},{7,8},{8,7},{9,10},{10... | collective-permute-start | bytes 589832 | tf_op jit(solution)/shard_map/ppermute | solution.py:267
  13.7 0.0 collective-permute-start.1
  13.7 0.0 copy-done.5
  13.7 0.0 copy-start.3
  13.7 0.1 copy.16.w_ref
  13.8 0.0 copy-start.6
  13.8 0.7 copy-done.6
  14.5 0.1 copy.17.b_ref
  14.5 0.0 copy-start.1
  14.5 3.7 %collective-permute-done.odd_ref.cot_odd_ref = bf16[768,128]{1,0:T(8,128)(2,1)S(1)} collective-permute-done((bf16[768,128]{1,0:T(8,128)(2,1)S(1)}, bf16[768,128]{1,0:T(8,128)(2,1)S(1)}, u32[]{:S(2)}, u32[]{:S(2)}) %collective-permute-start) | collective-permute-done | bytes 196640 | tf_op jit(solution)/shard_map/ppermute | solution.py:267
  18.3 0.8 %collective-permute-done.1.even_ref.cot_even_ref = bf16[768,128]{1,0:T(8,128)(2,1)S(1)} collective-permute-done((bf16[768,128]{1,0:T(8,128)(2,1)S(1)}, bf16[768,128]{1,0:T(8,128)(2,1)S(1)}, u32[]{:S(2)}, u32[]{:S(2)}) %collective-permute-start.1) | collective-permute-done | bytes 196640 | tf_op jit(solution)/shard_map/ppermute | solution.py:259
  19.1 0.0 copy-done.3
  19.1 0.0 copy-start.4
  19.1 1.8 %first.1 = (bf16[256,2048]{1,0:T(8,128)(2,1)S(1)}, f32[128,2048]{1,0:T(8,128)S(1)}, bf16[16,2048]{1,0:T(8,128)(2,1)S(1)}) custom-call(bf16[4,2,32,256]{3,2,1,0:T(8,128)(2,1)S(1)} %bitcast.17, bf16[768,128]{1,0:T(8,128)(2,1)S(1)} %collective-permute-done.odd_ref.cot_odd_ref, bf16[768,128]{1,0:T(8,128)(2,1)S(1)} %collective-permute-done.1.even_ref.cot_even_ref, ...), custom_call_target="tpu_custom_call" | custom-call | tf_op jit(solution)/shard_map/first/pallas_call | solution.py:291
  21.0 5.9 %collective-permute-start.2 = (bf16[16,2048]{1,0:T(8,128)(2,1)S(1)}, bf16[16,2048]{1,0:T(8,128)(2,1)S(1)}, u32[]{:S(2)}, u32[]{:S(2)}) collective-permute-start(bf16[16,2048]{1,0:T(8,128)(2,1)S(1)} %get-tuple-element.18.mid_ref), channel_id=1, source_target_pairs={{0,127},{1,2},{2,1},{3,4},{4,3},{5,6},{6,5},{7,8},{8,7},{9,10},{10... | collective-permute-start | bytes 196616 | tf_op jit(solution)/shard_map/ppermute | solution.py:267
  26.8 0.0 collective-permute-start.3
  26.8 1.5 %collective-permute-start.4 = (bf16[16,2048]{1,0:T(8,128)(2,1)S(1)}, bf16[16,2048]{1,0:T(8,128)(2,1)S(1)}, u32[]{:S(2)}, u32[]{:S(2)}) collective-permute-start(bf16[16,2048]{1,0:T(8,128)(2,1)S(1)} %get-tuple-element.18.mid_ref), channel_id=1, source_target_pairs={{0,1},{1,0},{2,3},{3,2},{4,5},{5,4},{6,7},{7,6},{8,9},{9,8},{10,11... | collective-permute-start | bytes 196616 | tf_op jit(solution)/shard_map/ppermute | solution.py:259
  28.3 0.0 collective-permute-start.5
  28.3 0.0 copy-start.7
  28.3 0.7 copy-done.7
  29.0 0.1 copy.18.b_ref
  29.0 0.5 collective-permute-done.2.near_odd_ref
  29.6 0.6 collective-permute-done.3.far_odd_ref
  30.2 0.7 %collective-permute-done.4.near_even_ref = bf16[16,2048]{1,0:T(8,128)(2,1)S(1)} collective-permute-done((bf16[16,2048]{1,0:T(8,128)(2,1)S(1)}, bf16[16,2048]{1,0:T(8,128)(2,1)S(1)}, u32[]{:S(2)}, u32[]{:S(2)}) %collective-permute-start.4) | collective-permute-done | bytes 65568 | tf_op jit(solution)/shard_map/ppermute | solution.py:259
  30.9 1.9 %collective-permute-done.5.far_even_ref = bf16[16,2048]{1,0:T(8,128)(2,1)S(1)} collective-permute-done((bf16[16,2048]{1,0:T(8,128)(2,1)S(1)}, bf16[16,2048]{1,0:T(8,128)(2,1)S(1)}, u32[]{:S(2)}, u32[]{:S(2)}) %collective-permute-start.5) | collective-permute-done | bytes 65568 | tf_op jit(solution)/shard_map/ppermute | solution.py:259
  32.9 0.0 copy-done.1
  32.9 0.0 copy-done.4
  32.9 2.9 %second.1 = (bf16[32,16,128]{2,1,0:T(8,128)(2,1)}, f32[160,128]{1,0:T(8,128)S(1)}) custom-call(bf16[16,2048]{1,0:T(8,128)(2,1)S(1)} %get-tuple-element.18.mid_ref, bf16[16,2048]{1,0:T(8,128)(2,1)S(1)} %collective-permute-done.2.near_odd_ref, bf16[16,2048]{1,0:T(8,128)(2,1)S(1)} %collective-permute-done.3.far_odd_ref, ...), custom_call_target="tpu_custom_call" | custom-call | tf_op jit(solution)/shard_map/second/pallas_call | solution.py:299
  35.8 3.2 %collective-permute-start.6 = (f32[80,128]{1,0:T(8,128)S(1)}, f32[80,128]{1,0:T(8,128)S(1)}, u32[]{:S(2)}, u32[]{:S(2)}) collective-permute-start(f32[80,128]{1,0:T(8,128)S(1)} %slice_select_fusion), channel_id=1, source_target_pairs={{0,128},{128,0},{1,129},{129,1},{2,130},{130,2},{3,131},{131,3},{4... | collective-permute-start | bytes 122888 | tf_op jit(solution)/shard_map/ppermute | solution.py:318
  39.0 0.9 %collective-permute-done.6 = f32[80,128]{1,0:T(8,128)S(1)} collective-permute-done((f32[80,128]{1,0:T(8,128)S(1)}, f32[80,128]{1,0:T(8,128)S(1)}, u32[]{:S(2)}, u32[]{:S(2)}) %collective-permute-start.6) | collective-permute-done | bytes 40992 | tf_op jit(solution)/shard_map/ppermute | solution.py:318
  39.9 0.6 collective-permute-start.7
  40.5 0.0 collective-permute-start.8
  40.5 2.1 %collective-permute-start.9 = (f32[80,128]{1,0:T(8,128)S(1)}, f32[80,128]{1,0:T(8,128)S(1)}, u32[]{:S(2)}, u32[]{:S(2)}) collective-permute-start(f32[80,128]{1,0:T(8,128)S(1)} %select_add_fusion), channel_id=1, source_target_pairs={{0,33},{1,32},{2,35},{3,34},{4,37},{5,36},{6,39},{7,38},{8,41},{9,... | collective-permute-start | bytes 122888 | tf_op jit(solution)/shard_map/ppermute | solution.py:275
  42.6 0.2 collective-permute-done.7
  42.8 0.8 %collective-permute-done.8 = f32[80,128]{1,0:T(8,128)S(1)} collective-permute-done((f32[80,128]{1,0:T(8,128)S(1)}, f32[80,128]{1,0:T(8,128)S(1)}, u32[]{:S(2)}, u32[]{:S(2)}) %collective-permute-start.8) | collective-permute-done | bytes 40992 | tf_op jit(solution)/shard_map/ppermute | solution.py:275
  43.7 0.8 %collective-permute-done.9 = f32[80,128]{1,0:T(8,128)S(1)} collective-permute-done((f32[80,128]{1,0:T(8,128)S(1)}, f32[80,128]{1,0:T(8,128)S(1)}, u32[]{:S(2)}, u32[]{:S(2)}) %collective-permute-start.9) | collective-permute-done | bytes 40992 | tf_op jit(solution)/shard_map/ppermute | solution.py:275
  44.5 2.2 %collective-permute-start.10 = (f32[80,128]{1,0:T(8,128)S(1)}, f32[80,128]{1,0:T(8,128)S(1)}, u32[]{:S(2)}, u32[]{:S(2)}) collective-permute-start(f32[80,128]{1,0:T(8,128)S(1)} %add_add_fusion.2), channel_id=1, source_target_pairs={{0,96},{1,97},{2,98},{3,99},{4,100},{5,101},{6,102},{7,103},{8,104... | collective-permute-start | bytes 122888 | tf_op jit(solution)/shard_map/ppermute | solution.py:275
  46.6 0.0 collective-permute-start.11
  46.6 1.8 %collective-permute-start.12 = (f32[80,128]{1,0:T(8,128)S(1)}, f32[80,128]{1,0:T(8,128)S(1)}, u32[]{:S(2)}, u32[]{:S(2)}) collective-permute-start(f32[80,128]{1,0:T(8,128)S(1)} %add_add_fusion.2), channel_id=1, source_target_pairs={{0,104},{1,105},{2,106},{3,107},{4,108},{5,109},{6,110},{7,111},{8... | collective-permute-start | bytes 122888 | tf_op jit(solution)/shard_map/ppermute | solution.py:275
  48.4 0.2 collective-permute-done.10
  48.6 0.9 %collective-permute-done.11 = f32[80,128]{1,0:T(8,128)S(1)} collective-permute-done((f32[80,128]{1,0:T(8,128)S(1)}, f32[80,128]{1,0:T(8,128)S(1)}, u32[]{:S(2)}, u32[]{:S(2)}) %collective-permute-start.11) | collective-permute-done | bytes 40992 | tf_op jit(solution)/shard_map/ppermute | solution.py:275
  49.5 2.1 %collective-permute-done.12 = f32[80,128]{1,0:T(8,128)S(1)} collective-permute-done((f32[80,128]{1,0:T(8,128)S(1)}, f32[80,128]{1,0:T(8,128)S(1)}, u32[]{:S(2)}, u32[]{:S(2)}) %collective-permute-start.12) | collective-permute-done | bytes 40992 | tf_op jit(solution)/shard_map/ppermute | solution.py:275
  51.6 0.1 collective-permute-start.13
  51.7 0.1 collective-permute-start.14
  51.8 4.6 %collective-permute-start.15 = (f32[80,128]{1,0:T(8,128)S(1)}, f32[80,128]{1,0:T(8,128)S(1)}, u32[]{:S(2)}, u32[]{:S(2)}) collective-permute-start(f32[80,128]{1,0:T(8,128)S(1)} %add_add_fusion.1), channel_id=1, source_target_pairs={{0,26},{1,27},{2,24},{3,25},{4,30},{5,31},{6,28},{7,29},{8,18},{9,... | collective-permute-start | bytes 122888 | tf_op jit(solution)/shard_map/ppermute | solution.py:275
  56.5 0.0 collective-permute-done.13
  56.5 0.0 collective-permute-done.14
  56.5 1.4 %collective-permute-done.15 = f32[80,128]{1,0:T(8,128)S(1)} collective-permute-done((f32[80,128]{1,0:T(8,128)S(1)}, f32[80,128]{1,0:T(8,128)S(1)}, u32[]{:S(2)}, u32[]{:S(2)}) %collective-permute-start.15) | collective-permute-done | bytes 40992 | tf_op jit(solution)/shard_map/ppermute | solution.py:275
  57.9 2.7 %collective-permute-start.16 = (f32[80,128]{1,0:T(8,128)S(1)}, f32[80,128]{1,0:T(8,128)S(1)}, u32[]{:S(2)}, u32[]{:S(2)}) collective-permute-start(f32[80,128]{1,0:T(8,128)S(1)} %add_add_fusion), channel_id=1, source_target_pairs={{0,7},{1,6},{2,5},{3,4},{4,3},{5,2},{6,1},{7,0},{8,15},{9,14},{10,... | collective-permute-start | bytes 122888 | tf_op jit(solution)/shard_map/ppermute | solution.py:275
  60.6 1.5 %collective-permute-done.16 = f32[80,128]{1,0:T(8,128)S(1)} collective-permute-done((f32[80,128]{1,0:T(8,128)S(1)}, f32[80,128]{1,0:T(8,128)S(1)}, u32[]{:S(2)}, u32[]{:S(2)}) %collective-permute-start.16) | collective-permute-done | bytes 40992 | tf_op jit(solution)/shard_map/ppermute | solution.py:275
  62.1 5.7 %collective-permute-start.17 = (f32[80,128]{1,0:T(8,128)S(1)}, f32[80,128]{1,0:T(8,128)S(1)}, u32[]{:S(2)}, u32[]{:S(2)}) collective-permute-start(f32[80,128]{1,0:T(8,128)S(1)} %add.45.mine_ref), channel_id=1, source_target_pairs={{0,128},{128,0},{1,129},{129,1},{2,130},{130,2},{3,131},{131,3},{4... | collective-permute-start | bytes 122888 | tf_op jit(solution)/shard_map/ppermute | solution.py:326
  67.8 0.9 %collective-permute-done.17.other_ref = f32[80,128]{1,0:T(8,128)S(1)} collective-permute-done((f32[80,128]{1,0:T(8,128)S(1)}, f32[80,128]{1,0:T(8,128)S(1)}, u32[]{:S(2)}, u32[]{:S(2)}) %collective-permute-start.17) | collective-permute-done | bytes 40992 | tf_op jit(solution)/shard_map/ppermute | solution.py:326
  68.7 0.9 %last.1 = (f32[27,4,16]{2,1,0:T(4,128)}, f32[1,16]{1,0:T(1,128)}, f32[27,16,32]{2,1,0:T(8,128)}, f32[1,32]{1,0:T(1,128)}) custom-call(f32[80,128]{1,0:T(8,128)S(1)} %add.45.mine_ref, f32[80,128]{1,0:T(8,128)S(1)} %collective-permute-done.17.other_ref), custom_call_target="tpu_custom_call" | custom-call | tf_op jit(solution)/shard_map/last/pallas_call | solution.py:321
  (8 shorter events, 0.1 us)
Async XLA Ops:
  0.6 0.9 %copy-start = (bf16[1,32,1,16,128]{4,3,2,1,0:T(8,128)(2,1)S(1)}, bf16[1,32,1,16,128]{4,3,2,1,0:T(8,128)(2,1)}, u32[]{:S(2)}) copy-start(bf16[1,32,1,16,128]{4,3,2,1,0:T(8,128)(2,1)} %param.11) | copy-start | bytes 393220
  1.5 0.9 %copy-start.2 = (bf16[1,4,2,32,256]{4,3,2,1,0:T(8,128)(2,1)S(1)}, bf16[1,4,2,32,256]{4,3,2,1,0:T(8,128)(2,1)}, u32[]{:S(2)}) copy-start(bf16[1,4,2,32,256]{4,3,2,1,0:T(8,128)(2,1)} %param.6) | copy-start | bytes 393220
  2.4 11.2 %copy-start.5 = (bf16[3,3,3,4,16]{4,3,2,1,0:T(4,128)(2,1)S(1)}, bf16[3,3,3,4,16]{4,3,2,1,0:T(4,128)(2,1)}, u32[]{:S(2)}) copy-start(bf16[3,3,3,4,16]{4,3,2,1,0:T(4,128)(2,1)} %param.7) | copy-start | bytes 10372
  2.5 15.8 %collective-permute-start = (bf16[768,128]{1,0:T(8,128)(2,1)S(1)}, bf16[768,128]{1,0:T(8,128)(2,1)S(1)}, u32[]{:S(2)}, u32[]{:S(2)}) collective-permute-start(bf16[768,128]{1,0:T(8,128)(2,1)S(1)} %get-tuple-element.16), channel_id=1, source_target_pairs={{0,127},{1,2},{2,1},{3,4},{4,3},{5,6},{6,5},{7,8},{8,7},{9,10},{10... | collective-permute-start | bytes 589832 | tf_op jit(solution)/shard_map/ppermute | solution.py:267
  13.7 5.5 %collective-permute-start.1 = (bf16[768,128]{1,0:T(8,128)(2,1)S(1)}, bf16[768,128]{1,0:T(8,128)(2,1)S(1)}, u32[]{:S(2)}, u32[]{:S(2)}) collective-permute-start(bf16[768,128]{1,0:T(8,128)(2,1)S(1)} %get-tuple-element.17), channel_id=1, source_target_pairs={{0,1},{1,0},{2,3},{3,2},{4,5},{5,4},{6,7},{7,6},{8,9},{9,8},{10,11... | collective-permute-start | bytes 589832 | tf_op jit(solution)/shard_map/ppermute | solution.py:259
  13.7 5.4 %copy-start.3 = (bf16[1,4,2,32,256]{4,3,2,1,0:T(8,128)(2,1)S(1)}, bf16[1,4,2,32,256]{4,3,2,1,0:T(8,128)(2,1)}, u32[]{:S(2)}) copy-start(bf16[1,4,2,32,256]{4,3,2,1,0:T(8,128)(2,1)} %param.6) | copy-start | bytes 393220
  13.8 0.7 copy-start.6
  14.5 18.3 %copy-start.1 = (bf16[1,32,1,16,128]{4,3,2,1,0:T(8,128)(2,1)S(1)}, bf16[1,32,1,16,128]{4,3,2,1,0:T(8,128)(2,1)}, u32[]{:S(2)}) copy-start(bf16[1,32,1,16,128]{4,3,2,1,0:T(8,128)(2,1)} %param.11) | copy-start | bytes 393220
  19.1 13.8 %copy-start.4 = (bf16[3,3,3,16,32]{4,3,2,1,0:T(8,128)(2,1)S(1)}, bf16[3,3,3,16,32]{4,3,2,1,0:T(8,128)(2,1)}, u32[]{:S(2)}) copy-start(bf16[3,3,3,16,32]{4,3,2,1,0:T(8,128)(2,1)} %param.9) | copy-start | bytes 82948
  21.0 8.6 %collective-permute-start.2 = (bf16[16,2048]{1,0:T(8,128)(2,1)S(1)}, bf16[16,2048]{1,0:T(8,128)(2,1)S(1)}, u32[]{:S(2)}, u32[]{:S(2)}) collective-permute-start(bf16[16,2048]{1,0:T(8,128)(2,1)S(1)} %get-tuple-element.18.mid_ref), channel_id=1, source_target_pairs={{0,127},{1,2},{2,1},{3,4},{4,3},{5,6},{6,5},{7,8},{8,7},{9,10},{10... | collective-permute-start | bytes 196616 | tf_op jit(solution)/shard_map/ppermute | solution.py:267
  26.8 3.4 %collective-permute-start.3 = (bf16[16,2048]{1,0:T(8,128)(2,1)S(1)}, bf16[16,2048]{1,0:T(8,128)(2,1)S(1)}, u32[]{:S(2)}, u32[]{:S(2)}) collective-permute-start(bf16[16,2048]{1,0:T(8,128)(2,1)S(1)} %get-tuple-element.18.mid_ref), channel_id=1, source_target_pairs={{0,1},{1,0},{2,4},{3,5},{4,2},{5,3},{6,8},{7,9},{8,6},{9,7},{10,12... | collective-permute-start | bytes 196616 | tf_op jit(solution)/shard_map/ppermute | solution.py:267
  26.8 4.1 %collective-permute-start.4 = (bf16[16,2048]{1,0:T(8,128)(2,1)S(1)}, bf16[16,2048]{1,0:T(8,128)(2,1)S(1)}, u32[]{:S(2)}, u32[]{:S(2)}) collective-permute-start(bf16[16,2048]{1,0:T(8,128)(2,1)S(1)} %get-tuple-element.18.mid_ref), channel_id=1, source_target_pairs={{0,1},{1,0},{2,3},{3,2},{4,5},{5,4},{6,7},{7,6},{8,9},{9,8},{10,11... | collective-permute-start | bytes 196616 | tf_op jit(solution)/shard_map/ppermute | solution.py:259
  28.3 4.6 %collective-permute-start.5 = (bf16[16,2048]{1,0:T(8,128)(2,1)S(1)}, bf16[16,2048]{1,0:T(8,128)(2,1)S(1)}, u32[]{:S(2)}, u32[]{:S(2)}) collective-permute-start(bf16[16,2048]{1,0:T(8,128)(2,1)S(1)} %get-tuple-element.18.mid_ref), channel_id=1, source_target_pairs={{0,2},{1,3},{2,0},{3,1},{4,6},{5,7},{6,4},{7,5},{8,10},{9,11},{10,... | collective-permute-start | bytes 196616 | tf_op jit(solution)/shard_map/ppermute | solution.py:259
  28.3 0.7 copy-start.7
  35.8 4.1 %collective-permute-start.6 = (f32[80,128]{1,0:T(8,128)S(1)}, f32[80,128]{1,0:T(8,128)S(1)}, u32[]{:S(2)}, u32[]{:S(2)}) collective-permute-start(f32[80,128]{1,0:T(8,128)S(1)} %slice_select_fusion), channel_id=1, source_target_pairs={{0,128},{128,0},{1,129},{129,1},{2,130},{130,2},{3,131},{131,3},{4... | collective-permute-start | bytes 122888 | tf_op jit(solution)/shard_map/ppermute | solution.py:318
  39.9 2.9 %collective-permute-start.7 = (f32[80,128]{1,0:T(8,128)S(1)}, f32[80,128]{1,0:T(8,128)S(1)}, u32[]{:S(2)}, u32[]{:S(2)}) collective-permute-start(f32[80,128]{1,0:T(8,128)S(1)} %select_add_fusion), channel_id=1, source_target_pairs={{0,32},{1,33},{2,34},{3,35},{4,36},{5,37},{6,38},{7,39},{8,40},{9,... | collective-permute-start | bytes 122888 | tf_op jit(solution)/shard_map/ppermute | solution.py:275
  40.5 3.1 %collective-permute-start.8 = (f32[80,128]{1,0:T(8,128)S(1)}, f32[80,128]{1,0:T(8,128)S(1)}, u32[]{:S(2)}, u32[]{:S(2)}) collective-permute-start(f32[80,128]{1,0:T(8,128)S(1)} %select_add_fusion), channel_id=1, source_target_pairs={{0,1},{1,0},{2,3},{3,2},{4,5},{5,4},{6,7},{7,6},{8,9},{9,8},{10,11... | collective-permute-start | bytes 122888 | tf_op jit(solution)/shard_map/ppermute | solution.py:275
  40.5 3.9 %collective-permute-start.9 = (f32[80,128]{1,0:T(8,128)S(1)}, f32[80,128]{1,0:T(8,128)S(1)}, u32[]{:S(2)}, u32[]{:S(2)}) collective-permute-start(f32[80,128]{1,0:T(8,128)S(1)} %select_add_fusion), channel_id=1, source_target_pairs={{0,33},{1,32},{2,35},{3,34},{4,37},{5,36},{6,39},{7,38},{8,41},{9,... | collective-permute-start | bytes 122888 | tf_op jit(solution)/shard_map/ppermute | solution.py:275
  44.5 4.2 %collective-permute-start.10 = (f32[80,128]{1,0:T(8,128)S(1)}, f32[80,128]{1,0:T(8,128)S(1)}, u32[]{:S(2)}, u32[]{:S(2)}) collective-permute-start(f32[80,128]{1,0:T(8,128)S(1)} %add_add_fusion.2), channel_id=1, source_target_pairs={{0,96},{1,97},{2,98},{3,99},{4,100},{5,101},{6,102},{7,103},{8,104... | collective-permute-start | bytes 122888 | tf_op jit(solution)/shard_map/ppermute | solution.py:275
  46.6 2.9 %collective-permute-start.11 = (f32[80,128]{1,0:T(8,128)S(1)}, f32[80,128]{1,0:T(8,128)S(1)}, u32[]{:S(2)}, u32[]{:S(2)}) collective-permute-start(f32[80,128]{1,0:T(8,128)S(1)} %add_add_fusion.2), channel_id=1, source_target_pairs={{0,8},{1,9},{2,10},{3,11},{4,12},{5,13},{6,14},{7,15},{8,0},{9,1},... | collective-permute-start | bytes 122888 | tf_op jit(solution)/shard_map/ppermute | solution.py:275
  46.6 5.0 %collective-permute-start.12 = (f32[80,128]{1,0:T(8,128)S(1)}, f32[80,128]{1,0:T(8,128)S(1)}, u32[]{:S(2)}, u32[]{:S(2)}) collective-permute-start(f32[80,128]{1,0:T(8,128)S(1)} %add_add_fusion.2), channel_id=1, source_target_pairs={{0,104},{1,105},{2,106},{3,107},{4,108},{5,109},{6,110},{7,111},{8... | collective-permute-start | bytes 122888 | tf_op jit(solution)/shard_map/ppermute | solution.py:275
  51.6 4.8 %collective-permute-start.13 = (f32[80,128]{1,0:T(8,128)S(1)}, f32[80,128]{1,0:T(8,128)S(1)}, u32[]{:S(2)}, u32[]{:S(2)}) collective-permute-start(f32[80,128]{1,0:T(8,128)S(1)} %add_add_fusion.1), channel_id=1, source_target_pairs={{0,2},{1,3},{2,0},{3,1},{4,6},{5,7},{6,4},{7,5},{8,10},{9,11},{10,... | collective-permute-start | bytes 122888 | tf_op jit(solution)/shard_map/ppermute | solution.py:275
  51.7 4.8 %collective-permute-start.14 = (f32[80,128]{1,0:T(8,128)S(1)}, f32[80,128]{1,0:T(8,128)S(1)}, u32[]{:S(2)}, u32[]{:S(2)}) collective-permute-start(f32[80,128]{1,0:T(8,128)S(1)} %add_add_fusion.1), channel_id=1, source_target_pairs={{0,24},{1,25},{2,26},{3,27},{4,28},{5,29},{6,30},{7,31},{8,16},{9,... | collective-permute-start | bytes 122888 | tf_op jit(solution)/shard_map/ppermute | solution.py:275
  51.8 6.0 %collective-permute-start.15 = (f32[80,128]{1,0:T(8,128)S(1)}, f32[80,128]{1,0:T(8,128)S(1)}, u32[]{:S(2)}, u32[]{:S(2)}) collective-permute-start(f32[80,128]{1,0:T(8,128)S(1)} %add_add_fusion.1), channel_id=1, source_target_pairs={{0,26},{1,27},{2,24},{3,25},{4,30},{5,31},{6,28},{7,29},{8,18},{9,... | collective-permute-start | bytes 122888 | tf_op jit(solution)/shard_map/ppermute | solution.py:275
  57.9 4.2 %collective-permute-start.16 = (f32[80,128]{1,0:T(8,128)S(1)}, f32[80,128]{1,0:T(8,128)S(1)}, u32[]{:S(2)}, u32[]{:S(2)}) collective-permute-start(f32[80,128]{1,0:T(8,128)S(1)} %add_add_fusion), channel_id=1, source_target_pairs={{0,7},{1,6},{2,5},{3,4},{4,3},{5,2},{6,1},{7,0},{8,15},{9,14},{10,... | collective-permute-start | bytes 122888 | tf_op jit(solution)/shard_map/ppermute | solution.py:275
  62.1 6.6 %collective-permute-start.17 = (f32[80,128]{1,0:T(8,128)S(1)}, f32[80,128]{1,0:T(8,128)S(1)}, u32[]{:S(2)}, u32[]{:S(2)}) collective-permute-start(f32[80,128]{1,0:T(8,128)S(1)} %add.45.mine_ref), channel_id=1, source_target_pairs={{0,128},{128,0},{1,129},{129,1},{2,130},{130,2},{3,131},{131,3},{4... | collective-permute-start | bytes 122888 | tf_op jit(solution)/shard_map/ppermute | solution.py:326
